TPU v7x, 128 devices: a whole 4x4x4 slice. The times are simulated.
128 devices in a mesh: fsdp: 16 (over y, z), ctx: 8 (over x, core).
Axes of the slice: x: 4, y: 4, z: 4, core: 2. Of those that a mesh axis runs over, the one named last changes fastest.
Arguments:
- tokens: bfloat16 [16, 1024, 1152], P('fsdp', 'ctx'), may hold values from -6 to 6
- norm_gains: bfloat16 [4, 1152], P(None, 'fsdp'), may hold values from 0.099609375 to 1.8984375
- qk_gains: bfloat16 [2, 256], P(None, 'fsdp'), may hold values from 0.099609375 to 1.8984375
- qkv_weight: bfloat16 [1152, 1536], P('fsdp'), may hold values from -0.1875 to 0.1875
- out_weight: bfloat16 [1024, 1152], P('fsdp'), may hold values from -0.1875 to 0.1875
- gate_weight: bfloat16 [6912, 1152], P('fsdp'), may hold values from -0.1875 to 0.1875
- up_weight: bfloat16 [6912, 1152], P('fsdp'), may hold values from -0.1875 to 0.1875
- down_weight: bfloat16 [6912, 1152], P('fsdp'), may hold values from -0.078125 to 0.078125
- segments: int32 [16, 1024], P('fsdp', 'ctx'), may hold values from 0 to 8, as said below
- cotangent: bfloat16 [16, 1024, 1152], P('fsdp', 'ctx'), may hold values from -6 to 6
Outputs:
- out: bfloat16 [16, 1024, 1152], P('fsdp', 'ctx')
- grad_tokens: float32 [16, 1024, 1152], P('fsdp', 'ctx')
- grad_norm_gains: float32 [4, 1152], P(None, 'fsdp')
- grad_qk_gains: float32 [2, 256], P(None, 'fsdp')
- grad_qkv_weight: float32 [1152, 1536], P('fsdp')
- grad_out_weight: float32 [1024, 1152], P('fsdp')
- grad_gate_weight: float32 [6912, 1152], P('fsdp')
- grad_up_weight: float32 [6912, 1152], P('fsdp')
- grad_down_weight: float32 [6912, 1152], P('fsdp')
Inputs may be any that keep to these rules, and one draw needn't show every extreme that they name: `segments`: along each sequence the segment numbers never fall.
All inputs are finite; a program needn't handle non-finite values.
Results may differ from a plain program's by a relative error of at most 0.024.
Values may be sent and summed in bfloat16 or wider, within the bound.
A program may use at most 320 MiB of HBM per device.

v0:
```python
from functools import partial

import jax
import jax.numpy as jnp
from jax import lax
from jax.sharding import PartitionSpec as P

D = 1152
NH = 4
HD = 256
WINDOW = 512


EPS = 1e-06
ROPE_BASE = 10000.0
NEG_FILL = -1e30
CONTRACT_LAST = (((1,), (1,)), ((), ()))
CONTRACT_FIRST = (((0,), (0,)), ((), ()))


def carried_in(part, axis, combine, identity):
    place = lax.axis_index(axis)
    gathered = jax.tree.map(lambda a: lax.all_gather(a, axis), part)
    state = jax.tree.map(lambda a, e: jnp.zeros_like(a) + jnp.asarray(e, a.dtype), part, identity)

    def one(lap, state):
        return combine(
            state, jax.tree.map(lambda a: lax.dynamic_index_in_dim(a, lap, 0, False), gathered)
        )

    return lax.fori_loop(0, place, one, state)


def from_behind(array, axis, by):
    devices = lax.axis_size(axis)
    pairs = [(i, i + by) for i in range(devices) if 0 <= i + by < devices]
    return lax.ppermute(array, axis, pairs)


def rms_norm(values, gain_vec):
    return values * lax.rsqrt(jnp.mean(values * values, axis=-1, keepdims=True) + EPS) * gain_vec


def rotate(values, cos_table, sin_table):
    half_size = values.shape[-1] // 2
    first_half = values[..., :half_size]
    second_half = values[..., half_size:]
    return jnp.concatenate(
        [
            first_half * cos_table - second_half * sin_table,
            second_half * cos_table + first_half * sin_table,
        ],
        axis=-1,
    )


def rope_tables(positions):
    frequency = ROPE_BASE ** (-(2.0 * jnp.arange(HD // 2).astype(jnp.float32)) / HD)
    angles = positions.astype(jnp.float32)[..., None] * frequency
    return (jnp.cos(angles), jnp.sin(angles))


def head_prep(q_raw, k_raw, q_gain, k_gain, cos_table, sin_table):
    queries = rotate(rms_norm(q_raw, q_gain), cos_table[:, :, None, :], sin_table[:, :, None, :])
    key_rows = rotate(rms_norm(k_raw, k_gain), cos_table, sin_table)
    return (queries, key_rows)


def gelu_product(gate_pre, up_pre):
    return jax.nn.gelu(gate_pre, approximate=True) * up_pre


def join_runs(first_part, second_part):
    count_one, head_seg_one, tail_seg_one, run_one = first_part
    count_two, head_seg_two, tail_seg_two, run_two = second_part
    carried = (count_one > 0) & (head_seg_two == tail_seg_two) & (tail_seg_one == tail_seg_two)
    run_begin = jnp.where(count_two > 0, jnp.where(carried, run_one, run_two), run_one)
    return (
        count_one + count_two,
        jnp.where(count_one > 0, head_seg_one, head_seg_two),
        jnp.where(count_two > 0, tail_seg_two, tail_seg_one),
        run_begin,
    )


def on_device(
    tokens,
    norm_gains,
    qk_gains,
    qkv_weight,
    out_weight,
    gate_weight,
    up_weight,
    down_weight,
    segments,
    cotangent,
):
    seq_count, local_len = (tokens.shape[0], tokens.shape[1])
    tok_rows = seq_count * local_len
    scale = HD ** (-0.5)
    gains_got, qk_got, qkv_full, out_full = (
        lax.all_gather(norm_gains, "fsdp", axis=1, tiled=True),
        lax.all_gather(qk_gains, "fsdp", axis=1, tiled=True),
        lax.all_gather(qkv_weight, "fsdp", axis=0, tiled=True),
        lax.all_gather(out_weight, "fsdp", axis=0, tiled=True),
    )
    gains_all = gains_got.astype(jnp.float32)
    qk_all = qk_got.astype(jnp.float32)
    ctx_index = lax.axis_index("ctx")
    local_idx = jnp.arange(local_len, dtype=jnp.int32)
    change = jnp.concatenate(
        [jnp.ones((seq_count, 1), jnp.bool_), segments[:, 1:] != segments[:, :-1]], axis=1
    )
    run_start = lax.cummax(jnp.where(change, local_idx[None, :], 0), axis=1)
    offset = ctx_index * local_len
    summary = (
        jnp.full((seq_count,), local_len, jnp.int32),
        segments[:, 0],
        segments[:, -1],
        offset + run_start[:, -1],
    )
    zero_runs = jnp.zeros((seq_count,), jnp.int32)
    count_before, head_before, tail_before, begin_before = carried_in(
        summary, "ctx", join_runs, (zero_runs, zero_runs, zero_runs, zero_runs)
    )
    carried = (run_start == 0) & (count_before > 0)[:, None] & (tail_before[:, None] == segments)
    starts = jnp.where(carried, begin_before[:, None], offset + run_start)
    positions = offset + local_idx[None, :] - starts
    cos_table, sin_table = rope_tables(positions)
    stream = tokens.astype(jnp.float32).reshape(tok_rows, D)
    flat_normed = rms_norm(stream, gains_all[0]).astype(jnp.bfloat16)
    projected = jnp.dot(flat_normed, qkv_full, preferred_element_type=jnp.float32)
    q_raw = projected[:, : NH * HD].reshape(seq_count, local_len, NH, HD)
    k_raw = projected[:, NH * HD : NH * HD + HD].reshape(seq_count, local_len, HD)
    values = projected[:, NH * HD + HD :].reshape(seq_count, local_len, HD).astype(jnp.bfloat16)
    q_rot, k_rot = head_prep(q_raw, k_raw, qk_all[0], qk_all[1], cos_table, sin_table)
    queries = q_rot.astype(jnp.bfloat16)
    key_rows = k_rot.astype(jnp.bfloat16)
    own_pair = jnp.concatenate([key_rows, values], axis=-1)
    reach = min(-(-(WINDOW - 1) // local_len), lax.axis_size("ctx") - 1)
    pieces = [own_pair]
    for distance in range(1, reach + 1):
        pieces.insert(0, from_behind(own_pair, "ctx", distance))
    pair_all = jnp.concatenate(pieces, axis=1)
    key_all = pair_all[..., :HD]
    value_all = pair_all[..., HD:]
    key_index = (ctx_index - reach) * local_len + jnp.arange(
        (reach + 1) * local_len, dtype=jnp.int32
    )
    query_index = offset + local_idx
    spacing = query_index[:, None] - key_index[None, :]
    allowed = ((spacing >= 0) & (spacing < WINDOW))[None] & (spacing[None] <= positions[:, :, None])
    raw_scores = (
        jnp.einsum("sqhd,skd->shqk", queries, key_all, preferred_element_type=jnp.float32) * scale
    )
    scores = jnp.where(allowed[:, None], raw_scores, NEG_FILL)
    top_score = jnp.max(scores, axis=-1, keepdims=True)
    expo = jnp.exp(scores - top_score)
    probs = expo / jnp.sum(expo, axis=-1, keepdims=True)
    probs_low = probs.astype(jnp.bfloat16)
    attended = (
        jnp.einsum("shqk,skd->sqhd", probs_low, value_all, preferred_element_type=jnp.float32)
        .astype(jnp.bfloat16)
        .reshape(tok_rows, NH * HD)
    )
    attn = jnp.dot(attended, out_full, preferred_element_type=jnp.float32)
    mid_stream = stream + rms_norm(attn, gains_all[1])
    normed_two = rms_norm(mid_stream, gains_all[2]).astype(jnp.bfloat16)
    gate_pre = lax.dot_general(
        normed_two,
        lax.all_gather(gate_weight, "fsdp", axis=0, tiled=True),
        CONTRACT_LAST,
        preferred_element_type=jnp.float32,
    )
    up_pre = lax.dot_general(
        normed_two,
        lax.all_gather(up_weight, "fsdp", axis=0, tiled=True),
        CONTRACT_LAST,
        preferred_element_type=jnp.float32,
    )
    hidden_part = gelu_product(gate_pre, up_pre).astype(jnp.bfloat16)
    mlp_out = jnp.dot(
        hidden_part,
        lax.all_gather(down_weight, "fsdp", axis=0, tiled=True),
        preferred_element_type=jnp.float32,
    )
    final = mid_stream + rms_norm(mlp_out, gains_all[3])
    output = final.reshape(seq_count, local_len, D).astype(jnp.bfloat16)
    grad_final = cotangent.astype(jnp.float32).reshape(tok_rows, D)
    grad_mlp, grad_gain_three = jax.vjp(rms_norm, mlp_out, gains_all[3])[1](grad_final)
    grad_mlp_low = grad_mlp.astype(jnp.bfloat16)
    full_gate, full_up, full_down = (
        lax.all_gather(gate_weight, "fsdp", axis=0, tiled=True),
        lax.all_gather(up_weight, "fsdp", axis=0, tiled=True),
        lax.all_gather(down_weight, "fsdp", axis=0, tiled=True),
    )
    gate_pre = lax.dot_general(
        normed_two, full_gate, CONTRACT_LAST, preferred_element_type=jnp.float32
    )
    up_pre = lax.dot_general(normed_two, full_up, CONTRACT_LAST, preferred_element_type=jnp.float32)
    hidden_value, hidden_back = jax.vjp(gelu_product, gate_pre, up_pre)
    hidden_low = hidden_value.astype(jnp.bfloat16)
    grad_hidden = lax.dot_general(
        grad_mlp_low, full_down, CONTRACT_LAST, preferred_element_type=jnp.float32
    )
    grad_gate, grad_up = hidden_back(grad_hidden)
    grad_gate_low = grad_gate.astype(jnp.bfloat16)
    grad_up_low = grad_up.astype(jnp.bfloat16)
    grad_normed_two = jnp.dot(
        grad_gate_low, full_gate, preferred_element_type=jnp.float32
    ) + jnp.dot(grad_up_low, full_up, preferred_element_type=jnp.float32)
    mlp_grads = lax.psum_scatter(
        jnp.concatenate(
            [
                lax.dot_general(
                    grad_gate_low, normed_two, CONTRACT_FIRST, preferred_element_type=jnp.float32
                ),
                lax.dot_general(
                    grad_up_low, normed_two, CONTRACT_FIRST, preferred_element_type=jnp.float32
                ),
                lax.dot_general(
                    hidden_low, grad_mlp_low, CONTRACT_FIRST, preferred_element_type=jnp.float32
                ),
            ],
            axis=1,
        ).astype(jnp.bfloat16),
        "fsdp",
        scatter_dimension=0,
        tiled=True,
    )
    grad_mid_part, grad_gain_two = jax.vjp(rms_norm, mid_stream, gains_all[2])[1](grad_normed_two)
    grad_mid = grad_final + grad_mid_part
    grad_attn, grad_gain_one = jax.vjp(rms_norm, attn, gains_all[1])[1](grad_mid)
    grad_attn_low = grad_attn.astype(jnp.bfloat16)
    qkv_back, out_back = (
        lax.all_gather(qkv_weight, "fsdp", axis=0, tiled=True),
        lax.all_gather(out_weight, "fsdp", axis=0, tiled=True),
    )
    grad_attended = lax.dot_general(
        grad_attn_low, out_back, CONTRACT_LAST, preferred_element_type=jnp.float32
    ).astype(jnp.bfloat16)
    grad_out_weight = lax.dot_general(
        attended, grad_attn_low, CONTRACT_FIRST, preferred_element_type=jnp.float32
    )
    grad_heads = grad_attended.reshape(seq_count, local_len, NH, HD)
    grad_probs = jnp.einsum(
        "sqhd,skd->shqk", grad_heads, value_all, preferred_element_type=jnp.float32
    )
    row_total = jnp.sum(probs * grad_probs, axis=-1, keepdims=True)
    grad_scores = (probs * (grad_probs - row_total)).astype(jnp.bfloat16)
    grad_queries = (
        jnp.einsum("shqk,skd->sqhd", grad_scores, key_all, preferred_element_type=jnp.float32)
        * scale
    )
    grad_keys = (
        jnp.einsum("shqk,sqhd->skd", grad_scores, queries, preferred_element_type=jnp.float32)
        * scale
    )
    grad_values = jnp.einsum(
        "shqk,sqhd->skd", probs_low, grad_heads, preferred_element_type=jnp.float32
    )
    grad_pairs = jnp.concatenate([grad_keys, grad_values], axis=-1)
    own_grad = grad_pairs[:, reach * local_len :]
    for distance in range(1, reach + 1):
        block_grad = grad_pairs[
            :, (reach - distance) * local_len : (reach - distance + 1) * local_len
        ]
        own_grad = own_grad + from_behind(block_grad.astype(jnp.bfloat16), "ctx", -distance).astype(
            block_grad.dtype
        )
    prep_fixed = partial(head_prep, cos_table=cos_table, sin_table=sin_table)
    prep_back = jax.vjp(prep_fixed, q_raw, k_raw, qk_all[0], qk_all[1])[1]
    grad_q_raw, grad_k_raw, grad_q_gain, grad_k_gain = prep_back((grad_queries, own_grad[..., :HD]))
    grad_projected = jnp.concatenate(
        [
            grad_q_raw.reshape(tok_rows, NH * HD),
            grad_k_raw.reshape(tok_rows, HD),
            own_grad[..., HD:].reshape(tok_rows, HD),
        ],
        axis=1,
    ).astype(jnp.bfloat16)
    grad_normed = lax.dot_general(
        grad_projected, qkv_back, CONTRACT_LAST, preferred_element_type=jnp.float32
    )
    grad_qkv_weight = lax.dot_general(
        flat_normed, grad_projected, CONTRACT_FIRST, preferred_element_type=jnp.float32
    )
    grad_input_part, grad_gain_zero = jax.vjp(rms_norm, stream, gains_all[0])[1](grad_normed)
    grad_tokens = (grad_mid + grad_input_part).reshape(seq_count, local_len, D)
    gain_grads = jnp.stack([grad_gain_zero, grad_gain_one, grad_gain_two, grad_gain_three])
    qk_grads = jnp.stack([grad_q_gain, grad_k_gain])
    share_qkv, share_out, share_gains, share_qk = (
        lax.psum_scatter(
            grad_qkv_weight.astype(jnp.bfloat16), "fsdp", scatter_dimension=0, tiled=True
        ).astype(jnp.float32),
        lax.psum_scatter(
            grad_out_weight.astype(jnp.bfloat16), "fsdp", scatter_dimension=0, tiled=True
        ).astype(jnp.float32),
        lax.psum_scatter(
            gain_grads.astype(jnp.bfloat16), "fsdp", scatter_dimension=1, tiled=True
        ).astype(jnp.float32),
        lax.psum_scatter(
            qk_grads.astype(jnp.bfloat16), "fsdp", scatter_dimension=1, tiled=True
        ).astype(jnp.float32),
    )
    total_qkv, total_out, total_gains, total_qk, total_mlp = (
        lax.psum(share_qkv.astype(jnp.bfloat16), "ctx").astype(jnp.float32),
        lax.psum(share_out.astype(jnp.bfloat16), "ctx").astype(jnp.float32),
        lax.psum(share_gains.astype(jnp.bfloat16), "ctx").astype(jnp.float32),
        lax.psum(share_qk.astype(jnp.bfloat16), "ctx").astype(jnp.float32),
        lax.psum(mlp_grads, "ctx").astype(jnp.float32),
    )
    return (
        output,
        grad_tokens,
        total_gains,
        total_qk,
        total_qkv,
        total_out,
        total_mlp[:, :D],
        total_mlp[:, D : 2 * D],
        total_mlp[:, 2 * D :],
    )


def solution(mesh):
    in_specs = (
        P("fsdp", "ctx", None),
        P(None, "fsdp"),
        P(None, "fsdp"),
        P("fsdp", None),
        P("fsdp", None),
        P("fsdp", None),
        P("fsdp", None),
        P("fsdp", None),
        P("fsdp", "ctx"),
        P("fsdp", "ctx", None),
    )
    out_specs = (
        P("fsdp", "ctx", None),
        P("fsdp", "ctx", None),
        P(None, "fsdp"),
        P(None, "fsdp"),
        P("fsdp", None),
        P("fsdp", None),
        P("fsdp", None),
        P("fsdp", None),
        P("fsdp", None),
    )
    return jax.shard_map(
        on_device, mesh=mesh, in_specs=in_specs, out_specs=out_specs, check_vma=False
    )
```

profile of v0, /device:TPU:73, one launch (start us, length us, event | category | flops | bytes accessed | tf_op | source)
XLA Modules:
  0.0 1310.5 jit_solution(13904732102404482032)
XLA Ops:
  19.8 7.7 all-reduce.12
  33.3 17.0 %all-gather.2 = bf16[16,16,2]{1,2,0:T(2,128)(2,1)S(1)} all-gather(bf16[1,16,2]{1,2,0:T(2,128)(2,1)S(1)} %bitcast.206), channel_id=1, replica_groups=mesh['fsdp'=16,'ctx'=8] {'fsdp'}, dimensions={0}, use_global_device_ids=true | all-gather | bytes 1088 | tf_op jit(solution)/shard_map/all_gather | solution.py:103
  50.4 15.7 %all-gather.1 = bf16[16,72,4]{1,2,0:T(4,128)(2,1)S(1)} all-gather(bf16[1,72,4]{1,2,0:T(4,128)(2,1)S(1)} %bitcast.205), channel_id=1, replica_groups=mesh['fsdp'=16,'ctx'=8] {'fsdp'}, dimensions={0}, use_global_device_ids=true | all-gather | bytes 9792 | tf_op jit(solution)/shard_map/all_gather | solution.py:102
  71.5 17.5 %collective-permute-start.3 = (bf16[1,128,512]{2,1,0:T(8,128)(2,1)S(1)}, bf16[1,128,512]{2,1,0:T(8,128)(2,1)S(1)}, u32[]{:S(2)}, u32[]{:S(2)}) collective-permute-start(bf16[1,128,512]{2,1,0:T(8,128)(2,1)S(1)} %pad_maximum_fusion.8), channel_id=1, source_target_pairs={{0,1},{1,2},{2,3},{3,4},{4,5},{5,6},{6,7},{8,9},{9,10},{10,11},{11... | collective-permute-start | bytes 393224 | tf_op jit(solution)/shard_map/ppermute | solution.py:37
  89.0 13.8 %collective-permute-start.2 = (bf16[1,128,512]{2,1,0:T(8,128)(2,1)S(1)}, bf16[1,128,512]{2,1,0:T(8,128)(2,1)S(1)}, u32[]{:S(2)}, u32[]{:S(2)}) collective-permute-start(bf16[1,128,512]{2,1,0:T(8,128)(2,1)S(1)} %pad_maximum_fusion.8), channel_id=1, source_target_pairs={{0,2},{1,3},{2,4},{3,5},{4,6},{5,7},{8,10},{9,11},{10,12},{11,13},... | collective-permute-start | bytes 393224 | tf_op jit(solution)/shard_map/ppermute | solution.py:37
  102.8 15.4 %collective-permute-start.1 = (bf16[1,128,512]{2,1,0:T(8,128)(2,1)S(1)}, bf16[1,128,512]{2,1,0:T(8,128)(2,1)S(1)}, u32[]{:S(2)}, u32[]{:S(2)}) collective-permute-start(bf16[1,128,512]{2,1,0:T(8,128)(2,1)S(1)} %pad_maximum_fusion.8), channel_id=1, source_target_pairs={{0,3},{1,4},{2,5},{3,6},{4,7},{8,11},{9,12},{10,13},{11,14},{12,15... | collective-permute-start | bytes 393224 | tf_op jit(solution)/shard_map/ppermute | solution.py:37
  129.9 85.4 %all-gather.13.cloned.1.call-done = bf16[6912,1152]{1,0:T(8,128)(2,1)} async-done(((bf16[432,1152]{1,0:T(8,128)(2,1)}), bf16[6912,1152]{1,0:T(8,128)(2,1)}) %all-gather.13.cloned.1.call-update) | async-done | bytes 15925264 | tf_op jit(solution)/shard_map/all_gather | solution.py:171
  215.3 11.6 fusion.87
  226.9 97.2 %all-gather.15.cloned.1.call-done = bf16[6912,1152]{1,0:T(8,128)(2,1)} async-done(((bf16[432,1152]{1,0:T(8,128)(2,1)}), bf16[6912,1152]{1,0:T(8,128)(2,1)}) %all-gather.15.cloned.1.call-update) | async-done | bytes 15925264 | tf_op jit(solution)/shard_map/all_gather | solution.py:177
  324.1 12.7 multiply_convert_fusion.1
  336.8 96.1 %all-gather.17.cloned.1.call-done = bf16[6912,1152]{1,0:T(8,128)(2,1)} async-done(((bf16[432,1152]{1,0:T(8,128)(2,1)}), bf16[6912,1152]{1,0:T(8,128)(2,1)}) %all-gather.17.cloned.1.call-update) | async-done | bytes 15925264 | tf_op jit(solution)/shard_map/all_gather | solution.py:184
  432.9 8.1 multiply_reduce_fusion.5
  442.8 8.0 convolution_convert_fusion
  450.8 11.2 multiply_convert_fusion
  462.0 9.3 convolution_convert_fusion.1
  471.3 7.9 convolution_convert_fusion.2
  479.1 32.6 %pad_maximum_fusion = bf16[6912,3456]{0,1:T(8,128)(2,1)} fusion(bf16[6912,1152]{0,1:T(8,128)(2,1)} %convolution_convert_fusion, bf16[6912,1152]{0,1:T(8,128)(2,1)} %convolution_convert_fusion.1, bf16[6912,1152]{0,1:T(8,128)(2,1)} %convolution_convert_fusion.2), kind=kLoop, calls=%fused_computation.4 | loop fusion | flops 143327232 | bytes 95551488 | tf_op jit(solution)/shard_map/concatenate | solution.py:213
  512.1 8.1 fusion.88
  520.3 10.3 multiply_reduce_fusion.1
  562.9 482.6 %all-reduce.19.cloned.1.call-done = bf16[6912,3456]{0,1:T(8,128)(2,1)} async-done(((bf16[6912,3456]{0,1:T(8,128)(2,1)}), bf16[6912,3456]{0,1:T(8,128)(2,1)}) %all-reduce.19.cloned.1.call-update) | async-done | bytes 47775760
  1051.7 71.6 %reduce-scatter.8.cloned.1.call-done = bf16[64,1152]{1,0:T(8,128)(2,1)} async-done(((bf16[1024,1152]{1,0:T(8,128)(2,1)}), bf16[64,1152]{1,0:T(8,128)(2,1)}) %reduce-scatter.8.cloned.1.call-update) | async-done | bytes 147472 | tf_op jit(solution)/shard_map/reduce_scatter | solution.py:296
  1123.3 79.3 %reduce-scatter.10.cloned.1.call-done = bf16[72,1536]{1,0:T(8,128)(2,1)} async-done(((bf16[1152,1536]{1,0:T(8,128)(2,1)}), bf16[72,1536]{1,0:T(8,128)(2,1)}) %reduce-scatter.10.cloned.1.call-update) | async-done | bytes 221200
  1207.5 49.7 %all-reduce.13 = (bf16[4,1152]{1,0:T(4,128)(2,1)S(1)}, bf16[2,256]{1,0:T(2,128)(2,1)S(1)}) all-reduce(bf16[4,1152]{1,0:T(4,128)(2,1)S(1)} %pad_maximum_fusion.9, bf16[2,256]{1,0:T(2,128)(2,1)S(1)} %pad_maximum_fusion.10), channel_id=3, replica_groups=mesh['fsdp'=16,'ctx'=8] {'fsdp'}, use_global_device_ids=true, to_apply=%region_22.23.clone | all-reduce | flops 5120 | bytes 20480
  1257.4 27.9 %all-reduce.14 = (bf16[4,72]{1,0:T(4,128)(2,1)S(1)}, bf16[2,16]{1,0:T(2,128)(2,1)S(1)}) all-reduce(bf16[4,72]{1,0:T(4,128)(2,1)S(1)} %constant_dynamic-slice_fusion.6, bf16[2,16]{1,0:T(2,128)(2,1)S(1)} %constant_dynamic-slice_fusion.5), channel_id=1, replica_groups=mesh['fsdp'=16,'ctx'=8] {'ctx'}, use_global_device_ids=true, to_apply=%region_23.24 | all-reduce | flops 320 | bytes 1280 | tf_op jit(solution)/shard_map/psum | solution.py:309
  (275 shorter events, 97.6 us)
Async XLA Ops:
  7.2 60.9 %all-gather.9.cloned.1.call-start = ((), (), s32[]{:S(2)}) async-start(), calls=%async_computation.2 | async-start | bytes 3760128 | tf_op jit(solution)/shard_map/all_gather | solution.py:104
  8.0 118.5 %all-gather.11.cloned.1.call-start = ((), (), s32[]{:S(2)}) async-start(), calls=%async_computation.3 | async-start | bytes 2506752 | tf_op jit(solution)/shard_map/all_gather | solution.py:105
  8.7 206.6 %all-gather.13.cloned.1.call-start = ((), (), s32[]{:S(2)}) async-start(), calls=%async_computation.4 | async-start | bytes 16920576 | tf_op jit(solution)/shard_map/all_gather | solution.py:171
  9.4 314.7 %all-gather.15.cloned.1.call-start = ((), (), s32[]{:S(2)}) async-start(), calls=%async_computation.5 | async-start | bytes 16920576 | tf_op jit(solution)/shard_map/all_gather | solution.py:177
  10.0 422.9 %all-gather.17.cloned.1.call-start = ((), (), s32[]{:S(2)}) async-start(), calls=%async_computation.6 | async-start | bytes 16920576 | tf_op jit(solution)/shard_map/all_gather | solution.py:184
  10.6 1034.9 %all-reduce.19.cloned.1.call-start = ((), (), s32[]{:S(2)}) async-start(), calls=%async_computation.8 | async-start | bytes 95551488
  66.9 62.9 %copy-start.22 = (f32[1152]{0:T(1024)}, f32[1152]{0:T(1024)S(1)}, u32[]{:S(2)}) copy-start(f32[1152]{0:T(1024)S(1)} %get-tuple-element.144) | copy-start | bytes 13828
  71.5 53.0 %collective-permute-start.3 = (bf16[1,128,512]{2,1,0:T(8,128)(2,1)S(1)}, bf16[1,128,512]{2,1,0:T(8,128)(2,1)S(1)}, u32[]{:S(2)}, u32[]{:S(2)}) collective-permute-start(bf16[1,128,512]{2,1,0:T(8,128)(2,1)S(1)} %pad_maximum_fusion.8), channel_id=1, source_target_pairs={{0,1},{1,2},{2,3},{3,4},{4,5},{5,6},{6,7},{8,9},{9,10},{10,11},{11... | collective-permute-start | bytes 393224 | tf_op jit(solution)/shard_map/ppermute | solution.py:37
  89.0 35.4 %collective-permute-start.2 = (bf16[1,128,512]{2,1,0:T(8,128)(2,1)S(1)}, bf16[1,128,512]{2,1,0:T(8,128)(2,1)S(1)}, u32[]{:S(2)}, u32[]{:S(2)}) collective-permute-start(bf16[1,128,512]{2,1,0:T(8,128)(2,1)S(1)} %pad_maximum_fusion.8), channel_id=1, source_target_pairs={{0,2},{1,3},{2,4},{3,5},{4,6},{5,7},{8,10},{9,11},{10,12},{11,13},... | collective-permute-start | bytes 393224 | tf_op jit(solution)/shard_map/ppermute | solution.py:37
  102.8 21.6 %collective-permute-start.1 = (bf16[1,128,512]{2,1,0:T(8,128)(2,1)S(1)}, bf16[1,128,512]{2,1,0:T(8,128)(2,1)S(1)}, u32[]{:S(2)}, u32[]{:S(2)}) collective-permute-start(bf16[1,128,512]{2,1,0:T(8,128)(2,1)S(1)} %pad_maximum_fusion.8), channel_id=1, source_target_pairs={{0,3},{1,4},{2,5},{3,6},{4,7},{8,11},{9,12},{10,13},{11,14},{12,15... | collective-permute-start | bytes 393224 | tf_op jit(solution)/shard_map/ppermute | solution.py:37
  118.3 6.1 collective-permute-start
  129.2 97.8 %copy-start.50 = (f32[128]{0:T(128)}, f32[128]{0:T(128)S(1)}, u32[]{:S(2)}) copy-start(f32[128]{0:T(128)S(1)} %fusion.74) | copy-start | bytes 1540
  511.8 611.5 %reduce-scatter.8.cloned.1.call-start = ((), (), s32[]{:S(2)}) async-start(), calls=%async_computation.7 | async-start | bytes 2506752 | tf_op jit(solution)/shard_map/reduce_scatter | solution.py:296
  534.8 667.9 %reduce-scatter.10.cloned.1.call-start = ((), (), s32[]{:S(2)}) async-start(), calls=%async_computation.9 | async-start | bytes 3760128
  541.6 7.7 collective-permute-start.4
  544.1 8.9 collective-permute-start.7
  545.4 8.9 collective-permute-start.6
  546.7 7.7 collective-permute-start.5
  561.3 726.1 %all-reduce.21.cloned.1.call-start = ((), (), s32[]{:S(2)}) async-start(), calls=%async_computation.10 | async-start | bytes 7815168 | tf_op jit(solution)/shard_map/psum | solution.py:311
  1051.7 152.3 %copy-start.32 = (bf16[1152]{0:T(1024)(128)(2,1)S(1)}, bf16[1152]{0:T(1024)(128)(2,1)}, u32[]{:S(2)}) copy-start(bf16[1152]{0:T(1024)(128)(2,1)} %get-tuple-element.131) | copy-start | bytes 6916
  1051.7 152.4 %copy-start.35 = (bf16[1152]{0:T(1024)(128)(2,1)S(1)}, bf16[1152]{0:T(1024)(128)(2,1)}, u32[]{:S(2)}) copy-start(bf16[1152]{0:T(1024)(128)(2,1)} %get-tuple-element.133) | copy-start | bytes 6916
  1051.7 152.4 %copy-start.31 = (bf16[1152]{0:T(1024)(128)(2,1)S(1)}, bf16[1152]{0:T(1024)(128)(2,1)}, u32[]{:S(2)}) copy-start(bf16[1152]{0:T(1024)(128)(2,1)} %get-tuple-element.141) | copy-start | bytes 6916
  1202.6 83.8 %copy-start.57 = (f32[128]{0:T(128)S(1)}, f32[128]{0:T(128)}, u32[]{:S(2)}) copy-start(f32[128]{0:T(128)} %copy-done.56) | copy-start | bytes 1540
  1202.7 83.8 %copy-start.6 = (f32[128,1152]{1,0:T(8,128)S(1)}, f32[128,1152]{1,0:T(8,128)}, u32[]{:S(2)}) copy-start(f32[128,1152]{1,0:T(8,128)} %copy-done.5) | copy-start | bytes 1769476
  (57 other events, 882.1 us)
Sparse Core Ops, SparseCore 0:
  10.2 48.8 all-gather.8
  61.3 43.8 all-gather.10
  107.4 107.8 all-gather.12
  217.4 106.6 all-gather.14
  326.2 106.6 all-gather.16
  511.9 533.5 all-reduce.18
  1049.1 74.1 reduce-scatter.7
  1127.1 75.5 reduce-scatter.9
  1205.4 72.5 all-reduce.20
where the time goes:
time: 1330 us; the launch traced here: 1310 us
  waiting for transfers between devices  924 us (69%)
  blocking collectives  118 us (9%)
  matrix products  106 us (8%)
  starting transfers between devices  55.8 us (4%)
  other arithmetic  50.5 us (4%)
  local copies, waits for them, and re-layouts  34.5 us (3%)
  between operations  17.5 us (1%)
    unnamed x11, waiting for transfers between devices  565 us
    all_gather x1, waiting for transfers between devices, on_device(): lax.all_gather(up_weight, 'fsdp', axis=0, tiled=True)  97.2 us
    all_gather x1, waiting for transfers between devices, on_device(): lax.all_gather(down_weight, 'fsdp', axis=0, tiled=True)  96.1 us
    all_gather x1, waiting for transfers between devices, on_device(): lax.all_gather(gate_weight, 'fsdp', axis=0, tiled=True)  85.4 us
    reduce_scatter x1, waiting for transfers between devices, on_device(): lax.psum_scatter(grad_out_weight.astype(jnp.bfloat16), 'fsdp', scatter_di...  71.6 us
    unnamed x2, blocking collectives  57.4 us
    ppermute x8, starting transfers between devices, from_behind(): return lax.ppermute(array, axis, pairs)  55 us
    concatenate x1, other arithmetic, on_device(): jnp.concatenate([lax.dot_general(grad_gate_low, normed_two, CONTRACT_FIRS...  32.6 us
  transfers between devices with their start and end apart: 17, of which 10 were waited for; matrix products, arithmetic and copies ran while one was open for 7% of the time, Pallas kernels for 0%

commit v1 on v0

v1 whole, which is shorter than its diff:
```python
from functools import partial

import jax
import jax.numpy as jnp
from jax import lax
from jax.sharding import PartitionSpec as P

D = 1152
NH = 4
HD = 256
WINDOW = 512


EPS = 1e-06
ROPE_BASE = 10000.0
NEG_FILL = -1e30
CONTRACT_LAST = (((1,), (1,)), ((), ()))
CONTRACT_FIRST = (((0,), (0,)), ((), ()))


def from_behind(array, axis, by):
    devices = lax.axis_size(axis)
    pairs = [(i, i + by) for i in range(devices) if 0 <= i + by < devices]
    return lax.ppermute(array, axis, pairs)


def rms_norm(values, gain_vec):
    return values * lax.rsqrt(jnp.mean(values * values, axis=-1, keepdims=True) + EPS) * gain_vec


def rotate(values, cos_table, sin_table):
    half_size = values.shape[-1] // 2
    first_half = values[..., :half_size]
    second_half = values[..., half_size:]
    return jnp.concatenate(
        [
            first_half * cos_table - second_half * sin_table,
            second_half * cos_table + first_half * sin_table,
        ],
        axis=-1,
    )


def rope_tables(positions):
    frequency = ROPE_BASE ** (-(2.0 * jnp.arange(HD // 2).astype(jnp.float32)) / HD)
    angles = positions.astype(jnp.float32)[..., None] * frequency
    return (jnp.cos(angles), jnp.sin(angles))


def head_prep(q_raw, k_raw, q_gain, k_gain, cos_table, sin_table):
    queries = rotate(rms_norm(q_raw, q_gain), cos_table[:, None, :], sin_table[:, None, :])
    key_rows = rotate(rms_norm(k_raw, k_gain), cos_table, sin_table)
    return (queries, key_rows)


def gelu_product(gate_pre, up_pre):
    return jax.nn.gelu(gate_pre, approximate=True) * up_pre


def on_device(
    tokens,
    norm_gains,
    qk_gains,
    qkv_weight,
    out_weight,
    gate_weight,
    up_weight,
    down_weight,
    segments,
    cotangent,
):
    local_len = tokens.shape[1]
    scale = HD ** (-0.5)
    ctx_index = lax.axis_index("ctx")
    ctx_size = lax.axis_size("ctx")
    own_rows = gate_weight.shape[0]
    slice_rows = own_rows // ctx_size
    padded = -(-slice_rows // 16) * 16
    gains_flat = jnp.concatenate([norm_gains.reshape(-1), qk_gains.reshape(-1)])
    gains_got = lax.all_gather(gains_flat, "fsdp")
    n_gain = norm_gains.size
    gains_all = (
        gains_got[:, :n_gain]
        .reshape(-1, 4, norm_gains.shape[1])
        .transpose(1, 0, 2)
        .reshape(4, D)
        .astype(jnp.float32)
    )
    qk_all = (
        gains_got[:, n_gain:]
        .reshape(-1, 2, qk_gains.shape[1])
        .transpose(1, 0, 2)
        .reshape(2, HD)
        .astype(jnp.float32)
    )
    seg_all = lax.all_gather(segments[0], "ctx", axis=0, tiled=True)
    qkv_full = lax.all_gather(qkv_weight, "fsdp", axis=0, tiled=True)
    out_full = lax.all_gather(out_weight, "fsdp", axis=0, tiled=True)

    def my_slice(weight):
        part = lax.dynamic_index_in_dim(
            weight.reshape(ctx_size, slice_rows, D), ctx_index, 0, False
        )
        return jnp.pad(part, ((0, padded - slice_rows), (0, 0)))

    gate_full = lax.all_gather(my_slice(gate_weight), "fsdp", axis=0, tiled=True)
    up_full = lax.all_gather(my_slice(up_weight), "fsdp", axis=0, tiled=True)
    down_full = lax.all_gather(my_slice(down_weight), "fsdp", axis=0, tiled=True)

    offset = ctx_index * local_len
    positions = offset + jnp.arange(local_len, dtype=jnp.int32)
    cos_table, sin_table = rope_tables(positions)
    stream = tokens.astype(jnp.float32).reshape(local_len, D)
    flat_normed = rms_norm(stream, gains_all[0]).astype(jnp.bfloat16)
    projected = jnp.dot(flat_normed, qkv_full, preferred_element_type=jnp.float32)
    q_raw = projected[:, : NH * HD].reshape(local_len, NH, HD)
    k_raw = projected[:, NH * HD : NH * HD + HD]
    values = projected[:, NH * HD + HD :].astype(jnp.bfloat16)
    prep_fixed = partial(head_prep, cos_table=cos_table, sin_table=sin_table)
    (q_rot, k_rot), prep_back = jax.vjp(prep_fixed, q_raw, k_raw, qk_all[0], qk_all[1])
    queries = q_rot.astype(jnp.bfloat16)
    own_pair = jnp.concatenate([k_rot.astype(jnp.bfloat16), values], axis=-1)
    reach = min(-(-(WINDOW - 1) // local_len), ctx_size - 1)
    pieces = [own_pair]
    for distance in range(1, reach + 1):
        pieces.insert(0, from_behind(own_pair, "ctx", distance))
    pair_all = jnp.concatenate(pieces, axis=0)
    key_all = pair_all[:, :HD]
    value_all = pair_all[:, HD:]
    key_index = offset - reach * local_len + jnp.arange((reach + 1) * local_len, dtype=jnp.int32)
    seg_padded = jnp.concatenate([jnp.full((reach * local_len,), -1, jnp.int32), seg_all])
    key_seg = lax.dynamic_slice_in_dim(seg_padded, offset, (reach + 1) * local_len, 0)
    spacing = positions[:, None] - key_index[None, :]
    allowed = (
        (spacing >= 0) & (spacing < WINDOW) & (segments[0][:, None] == key_seg[None, :])
    )
    raw_scores = (
        jnp.einsum("qhd,kd->hqk", queries, key_all, preferred_element_type=jnp.float32) * scale
    )
    scores = jnp.where(allowed[None], raw_scores, NEG_FILL)
    top_score = jnp.max(scores, axis=-1, keepdims=True)
    expo = jnp.exp(scores - top_score)
    probs = expo / jnp.sum(expo, axis=-1, keepdims=True)
    probs_low = probs.astype(jnp.bfloat16)
    attended = (
        jnp.einsum("hqk,kd->qhd", probs_low, value_all, preferred_element_type=jnp.float32)
        .astype(jnp.bfloat16)
        .reshape(local_len, NH * HD)
    )
    attn = jnp.dot(attended, out_full, preferred_element_type=jnp.float32)
    mid_stream = stream + rms_norm(attn, gains_all[1])
    normed_two = rms_norm(mid_stream, gains_all[2]).astype(jnp.bfloat16)

    normed_seq = lax.all_gather(normed_two, "ctx", axis=0, tiled=True)
    gate_pre = lax.dot_general(
        normed_seq, gate_full, CONTRACT_LAST, preferred_element_type=jnp.float32
    )
    up_pre = lax.dot_general(normed_seq, up_full, CONTRACT_LAST, preferred_element_type=jnp.float32)
    hidden_value, hidden_back = jax.vjp(gelu_product, gate_pre, up_pre)
    hidden_low = hidden_value.astype(jnp.bfloat16)
    mlp_part = jnp.dot(hidden_low, down_full, preferred_element_type=jnp.float32)
    mlp_out = lax.psum_scatter(
        mlp_part.astype(jnp.bfloat16), "ctx", scatter_dimension=0, tiled=True
    ).astype(jnp.float32)
    final = mid_stream + rms_norm(mlp_out, gains_all[3])
    output = final.reshape(1, local_len, D).astype(jnp.bfloat16)
    grad_final = cotangent.astype(jnp.float32).reshape(local_len, D)
    grad_mlp, grad_gain_three = jax.vjp(rms_norm, mlp_out, gains_all[3])[1](grad_final)
    grad_mlp_seq = lax.all_gather(grad_mlp.astype(jnp.bfloat16), "ctx", axis=0, tiled=True)
    grad_hidden = lax.dot_general(
        grad_mlp_seq, down_full, CONTRACT_LAST, preferred_element_type=jnp.float32
    )
    grad_gate, grad_up = hidden_back(grad_hidden)
    grad_gate_low = grad_gate.astype(jnp.bfloat16)
    grad_up_low = grad_up.astype(jnp.bfloat16)
    grad_normed_part = jnp.dot(
        grad_gate_low, gate_full, preferred_element_type=jnp.float32
    ) + jnp.dot(grad_up_low, up_full, preferred_element_type=jnp.float32)
    grad_normed_two = lax.psum_scatter(
        grad_normed_part.astype(jnp.bfloat16), "ctx", scatter_dimension=0, tiled=True
    ).astype(jnp.float32)
    mlp_grads = jnp.concatenate(
        [
            lax.dot_general(
                grad_gate_low, normed_seq, CONTRACT_FIRST, preferred_element_type=jnp.float32
            ),
            lax.dot_general(
                grad_up_low, normed_seq, CONTRACT_FIRST, preferred_element_type=jnp.float32
            ),
            lax.dot_general(
                hidden_low, grad_mlp_seq, CONTRACT_FIRST, preferred_element_type=jnp.float32
            ),
        ],
        axis=1,
    ).astype(jnp.bfloat16)
    mlp_share = lax.psum_scatter(mlp_grads, "fsdp", scatter_dimension=0, tiled=True)
    mlp_total = lax.all_gather(mlp_share[:slice_rows], "ctx", axis=0, tiled=True).astype(
        jnp.float32
    )

    grad_mid_part, grad_gain_two = jax.vjp(rms_norm, mid_stream, gains_all[2])[1](grad_normed_two)
    grad_mid = grad_final + grad_mid_part
    grad_attn, grad_gain_one = jax.vjp(rms_norm, attn, gains_all[1])[1](grad_mid)
    grad_attn_low = grad_attn.astype(jnp.bfloat16)
    grad_attended = lax.dot_general(
        grad_attn_low, out_full, CONTRACT_LAST, preferred_element_type=jnp.float32
    ).astype(jnp.bfloat16)
    grad_out_weight = lax.dot_general(
        attended, grad_attn_low, CONTRACT_FIRST, preferred_element_type=jnp.float32
    )
    grad_heads = grad_attended.reshape(local_len, NH, HD)
    grad_probs = jnp.einsum(
        "qhd,kd->hqk", grad_heads, value_all, preferred_element_type=jnp.float32
    )
    row_total = jnp.sum(probs * grad_probs, axis=-1, keepdims=True)
    grad_scores = (probs * (grad_probs - row_total)).astype(jnp.bfloat16)
    grad_queries = (
        jnp.einsum("hqk,kd->qhd", grad_scores, key_all, preferred_element_type=jnp.float32) * scale
    )
    grad_keys = (
        jnp.einsum("hqk,qhd->kd", grad_scores, queries, preferred_element_type=jnp.float32) * scale
    )
    grad_values = jnp.einsum(
        "hqk,qhd->kd", probs_low, grad_heads, preferred_element_type=jnp.float32
    )
    grad_pairs = jnp.concatenate([grad_keys, grad_values], axis=-1)
    own_grad = grad_pairs[reach * local_len :]
    for distance in range(1, reach + 1):
        block_grad = grad_pairs[(reach - distance) * local_len : (reach - distance + 1) * local_len]
        own_grad = own_grad + from_behind(block_grad.astype(jnp.bfloat16), "ctx", -distance).astype(
            jnp.float32
        )
    grad_q_raw, grad_k_raw, grad_q_gain, grad_k_gain = prep_back((grad_queries, own_grad[:, :HD]))
    grad_projected = jnp.concatenate(
        [grad_q_raw.reshape(local_len, NH * HD), grad_k_raw, own_grad[:, HD:]], axis=1
    ).astype(jnp.bfloat16)
    grad_normed = lax.dot_general(
        grad_projected, qkv_full, CONTRACT_LAST, preferred_element_type=jnp.float32
    )
    grad_qkv_weight = lax.dot_general(
        flat_normed, grad_projected, CONTRACT_FIRST, preferred_element_type=jnp.float32
    )
    grad_input_part, grad_gain_zero = jax.vjp(rms_norm, stream, gains_all[0])[1](grad_normed)
    grad_tokens = (grad_mid + grad_input_part).reshape(1, local_len, D)
    gain_grads = jnp.stack([grad_gain_zero, grad_gain_one, grad_gain_two, grad_gain_three])
    qk_grads = jnp.stack([grad_q_gain, grad_k_gain])
    fsdp_size = lax.axis_size("fsdp")
    small = jnp.concatenate(
        [
            gain_grads.reshape(4, fsdp_size, -1).transpose(1, 0, 2).reshape(fsdp_size, -1),
            qk_grads.reshape(2, fsdp_size, -1).transpose(1, 0, 2).reshape(fsdp_size, -1),
        ],
        axis=1,
    )
    small_total = lax.psum(small, ("fsdp", "ctx"))
    small_own = lax.dynamic_index_in_dim(small_total, lax.axis_index("fsdp"), 0, False)
    total_gains = small_own[:n_gain].reshape(norm_gains.shape)
    total_qk = small_own[n_gain:].reshape(qk_gains.shape)
    share_qkv = lax.psum_scatter(
        grad_qkv_weight.astype(jnp.bfloat16), "fsdp", scatter_dimension=0, tiled=True
    )
    share_out = lax.psum_scatter(
        grad_out_weight.astype(jnp.bfloat16), "fsdp", scatter_dimension=0, tiled=True
    )
    total_qkv = lax.psum(share_qkv, "ctx").astype(jnp.float32)
    total_out = lax.psum(share_out, "ctx").astype(jnp.float32)
    return (
        output,
        grad_tokens,
        total_gains,
        total_qk,
        total_qkv,
        total_out,
        mlp_total[:, :D],
        mlp_total[:, D : 2 * D],
        mlp_total[:, 2 * D :],
    )


def solution(mesh):
    in_specs = (
        P("fsdp", "ctx", None),
        P(None, "fsdp"),
        P(None, "fsdp"),
        P("fsdp", None),
        P("fsdp", None),
        P("fsdp", None),
        P("fsdp", None),
        P("fsdp", None),
        P("fsdp", "ctx"),
        P("fsdp", "ctx", None),
    )
    out_specs = (
        P("fsdp", "ctx", None),
        P("fsdp", "ctx", None),
        P(None, "fsdp"),
        P(None, "fsdp"),
        P("fsdp", None),
        P("fsdp", None),
        P("fsdp", None),
        P("fsdp", None),
        P("fsdp", None),
    )
    return jax.shard_map(
        on_device, mesh=mesh, in_specs=in_specs, out_specs=out_specs, check_vma=False
    )
```

time: 1330 us -> 764 us (0.57)
  waiting for transfers between devices: 924 us -> 455 us
  starting transfers between devices: 55.8 us -> 18.2 us
  matrix products: 106 us -> 74.4 us
  other arithmetic: 50.5 us -> 23.9 us
  blocking collectives: 118 us -> 140 us
    unnamed x11 -> x15, waiting for transfers between devices: 565 us -> 80.7 us
    reduce_scatter x0 -> x3, waiting for transfers between devices: none -> 151 us  [the longest x1 85.8 us: on_device(): lax.psum_scatter(mlp_grads, 'fsdp', scatter_dimension=0, tiled=True)]
    all_gather x5 -> x8, waiting for transfers between devices: 279 us -> 188 us  [the longest x1 38.4 us: on_device(): up_full = lax.all_gather(my_slice(up_weight), 'fsdp', axis=0, tiled=True)]
    reduce_scatter x1, waiting for transfers between devices: 71.6 us -> 27.5 us  [on_device(): lax.psum_scatter(grad_out_weight.astype(jnp.bfloat16), 'fsdp', scatter_di...]
    ppermute x8, starting transfers between devices: 55 us -> 17.3 us  [from_behind(): return lax.ppermute(array, axis, pairs)]
    psum x1, blocking collectives: 27.9 us -> 64.7 us  [on_device(): small_total = lax.psum(small, ('fsdp', 'ctx'))]
    dot_general x17 -> x16, matrix products: 96 us -> 62.5 us  [the longest x1 9.85 us: on_device(): lax.dot_general(grad_mlp_seq, down_full, CONTRACT_LAST, preferred_element...]
    concatenate x4 -> x5, other arithmetic: 32.7 us -> 3.52 us  [the longest x1 3.33 us: on_device(): jnp.concatenate([lax.dot_general(grad_gate_low, normed_seq, CONTRACT_FIRS...]
  transfers between devices with their start and end apart: 17 -> 22, of which waited for: 10 -> 16; matrix products, arithmetic and copies ran while one was open for 7% -> 10% of each run, Pallas kernels for 0% -> 0%
where the time goes in v1:
time: 764 us; the launch traced here: 756 us
  waiting for transfers between devices  455 us (60%)
  blocking collectives  140 us (18%)
  matrix products  74.4 us (10%)
  local copies, waits for them, and re-layouts  27.5 us (4%)
  other arithmetic  23.9 us (3%)
  starting transfers between devices  18.2 us (2%)
  between operations  16.2 us (2%)
    reduce_scatter x1, waiting for transfers between devices, on_device(): lax.psum_scatter(mlp_grads, 'fsdp', scatter_dimension=0, tiled=True)  85.8 us
    unnamed x15, waiting for transfers between devices  80.7 us
    psum x1, blocking collectives, on_device(): small_total = lax.psum(small, ('fsdp', 'ctx'))  64.7 us
    unnamed x1, blocking collectives  52.4 us
    all_gather x1, waiting for transfers between devices, on_device(): up_full = lax.all_gather(my_slice(up_weight), 'fsdp', axis=0, tiled=True)  38.4 us
    all_gather x1, waiting for transfers between devices, on_device(): lax.all_gather(my_slice(down_weight), 'fsdp', axis=0, tiled=True)  37.4 us
    all_gather x1, waiting for transfers between devices, on_device(): lax.all_gather(my_slice(gate_weight), 'fsdp', axis=0, tiled=True)  36.1 us
    reduce_scatter x1, waiting for transfers between devices, on_device(): lax.psum_scatter(mlp_part.astype(jnp.bfloat16), 'ctx', scatter_dimension=...  33.6 us
  transfers between devices with their start and end apart: 22, of which 16 were waited for; matrix products, arithmetic and copies ran while one was open for 10% of the time, Pallas kernels for 0%

profile of v1, /device:TPU:73, one launch (start us, length us, event | category | flops | bytes accessed | tf_op | source)
XLA Modules:
  0.0 756.2 jit_solution(4124299335552264497)
XLA Ops:
  12.8 52.4 %all-reduce.8 = bf16[5120]{0:T(1024)(128)(2,1)S(1)} all-reduce(bf16[5120]{0:T(1024)(128)(2,1)S(1)} %dynamic-update-slice), channel_id=2, replica_groups=mesh['fsdp'=16,'ctx'=8] {'fsdp'}, use_global_device_ids=true, to_apply=%add.8 | all-reduce | flops 5120 | bytes 20480
  66.1 23.3 %all-gather.1 = s32[1,1024]{1,0:T(1,128)S(1)} all-gather(s32[1,128]{1,0:T(1,128)S(1)} %copy-done.38), channel_id=3, replica_groups=mesh['fsdp'=16,'ctx'=8] {'ctx'}, dimensions={1}, use_global_device_ids=true | all-gather | bytes 4608 | tf_op jit(solution)/shard_map/all_gather | solution.py:96
  117.3 36.1 %all-gather.18.cloned.1.call-done = bf16[1024,1152]{1,0:T(8,128)(2,1)} async-done(((bf16[64,1152]{1,0:T(8,128)(2,1)}), bf16[1024,1152]{1,0:T(8,128)(2,1)}) %all-gather.18.cloned.1.call-update) | async-done | bytes 2359312 | tf_op jit(solution)/shard_map/all_gather | solution.py:106
  153.4 30.4 %all-gather.16.cloned.1.call-done = bf16[1024,1152]{1,0:T(8,128)(2,1)} async-done(((bf16[128,1152]{1,0:T(8,128)(2,1)}), bf16[1024,1152]{1,0:T(8,128)(2,1)}) %all-gather.16.cloned.1.call-update) | async-done | bytes 2359312 | tf_op jit(solution)/shard_map/all_gather | solution.py:154
  183.8 7.2 fusion.87
  191.0 38.4 %all-gather.20.cloned.1.call-done = bf16[1024,1152]{1,0:T(8,128)(2,1)} async-done(((bf16[64,1152]{1,0:T(8,128)(2,1)}), bf16[1024,1152]{1,0:T(8,128)(2,1)}) %all-gather.20.cloned.1.call-update) | async-done | bytes 2359312 | tf_op jit(solution)/shard_map/all_gather | solution.py:107
  229.4 9.7 %multiply_convert_fusion.1 = (bf16[1024,1024]{1,0:T(8,128)(2,1)}, f32[1024,1024]{1,0:T(8,128)}) fusion(f32[1024,1024]{1,0:T(8,128)} %fusion.87, bf16[1024,1152]{1,0:T(8,128)(2,1)} %all-gather.16.cloned.1.call-done, bf16[1024,1152]{1,0:T(8,128)(2,1)} %all-gather.20.cloned.1.call-done), kind=kOutput, calls=%fused_computation.14 | convolution fusion | flops 2426404864 | bytes 15204352 | tf_op jit(solution)/shard_map/dot_general | solution.py:158
  239.1 37.4 %all-gather.22.cloned.1.call-done = bf16[1024,1152]{1,0:T(8,128)(2,1)} async-done(((bf16[64,1152]{1,0:T(8,128)(2,1)}), bf16[1024,1152]{1,0:T(8,128)(2,1)}) %all-gather.22.cloned.1.call-update) | async-done | bytes 2359312 | tf_op jit(solution)/shard_map/all_gather | solution.py:108
  276.5 6.6 convolution_convert_fusion.5
  283.2 33.6 %reduce-scatter.8.cloned.1.call-done = bf16[128,1152]{1,0:T(8,128)(2,1)} async-done(((bf16[1024,1152]{1,0:T(8,128)(2,1)}), bf16[128,1152]{1,0:T(8,128)(2,1)}) %reduce-scatter.8.cloned.1.call-update) | async-done | bytes 294928 | tf_op jit(solution)/shard_map/reduce_scatter | solution.py:162
  321.9 27.5 %all-gather.24.cloned.1.call-done = bf16[1024,1152]{1,0:T(8,128)(2,1)} async-done(((bf16[128,1152]{1,0:T(8,128)(2,1)}), bf16[1024,1152]{1,0:T(8,128)(2,1)}) %all-gather.24.cloned.1.call-update) | async-done | bytes 2359312 | tf_op jit(solution)/shard_map/all_gather | solution.py:169
  349.5 9.9 %multiply_convert_fusion = (bf16[1024,1024]{1,0:T(8,128)(2,1)S(1)}, bf16[1024,1024]{1,0:T(8,128)(2,1)S(1)}) fusion(f32[1024,1024]{1,0:T(8,128)} %fusion.87, f32[1024,1024]{1,0:T(8,128)} %get-tuple-element.59, bf16[1024,1152]{1,0:T(8,128)(2,1)} %all-gather.24.cloned.1.call-done, bf16[1024,1152]{1,0:T(8,128)(2,1)} %all-gather.22.cloned.1.call-done), kind=kOutput, calls=%fused_computation.13 | convolution fusion | flops 2441084928 | bytes 17301504 | tf_op jit(solution)/shard_map/dot_general | solution.py:170
  362.5 4.1 add_convert_fusion
  366.8 31.6 %reduce-scatter.10.cloned.1.call-done = bf16[128,1152]{1,0:T(8,128)(2,1)} async-done(((bf16[1024,1152]{1,0:T(8,128)(2,1)}), bf16[128,1152]{1,0:T(8,128)(2,1)}) %reduce-scatter.10.cloned.1.call-update) | async-done | bytes 294928 | tf_op jit(solution)/shard_map/reduce_scatter | solution.py:179
  419.8 5.6 collective-permute-start.4
  437.3 5.4 convolution_convert_fusion.1
  452.6 27.5 %reduce-scatter.12.cloned.1.call-done = bf16[64,1152]{1,0:T(8,128)(2,1)} async-done(((bf16[1024,1152]{1,0:T(8,128)(2,1)}), bf16[64,1152]{1,0:T(8,128)(2,1)}) %reduce-scatter.12.cloned.1.call-update) | async-done | bytes 147472 | tf_op jit(solution)/shard_map/reduce_scatter | solution.py:262
  480.1 79.1 %reduce-scatter.16.cloned.1.call-done = bf16[72,1536]{1,0:T(8,128)(2,1)} async-done(((bf16[1152,1536]{1,0:T(8,128)(2,1)}), bf16[72,1536]{1,0:T(8,128)(2,1)}) %reduce-scatter.16.cloned.1.call-update) | async-done | bytes 221200
  559.3 85.8 %reduce-scatter.14.cloned.1.call-done = bf16[64,3456]{1,0:T(8,128)(2,1)} async-done(((bf16[1024,3456]{1,0:T(8,128)(2,1)}), bf16[64,3456]{1,0:T(8,128)(2,1)}) %reduce-scatter.14.cloned.1.call-update) | async-done | bytes 442384 | tf_op jit(solution)/shard_map/reduce_scatter | solution.py:196
  647.6 3.4 fusion.22
  651.3 64.7 %psum.21 = f32[16,320]{1,0:T(8,128)S(1)} all-reduce(f32[16,320]{1,0:T(8,128)S(1)} %pad_maximum_fusion.11), channel_id=1, replica_groups=mesh['fsdp'=16,'ctx'=8] {'fsdp','ctx'}, use_global_device_ids=true, to_apply=%region_23.24 | all-reduce | flops 5120 | bytes 40960 | tf_op jit(solution)/shard_map/psum | solution.py:255
  721.8 17.7 %all-gather.26.cloned.1.call-done = bf16[8,54,3456]{2,1,0:T(8,128)(2,1)} async-done(((bf16[1,54,3456]{2,1,0:T(8,128)(2,1)}), bf16[8,54,3456]{2,1,0:T(8,128)(2,1)}) %all-gather.26.cloned.1.call-update) | async-done | bytes 2986000 | tf_op jit(solution)/shard_map/all_gather | solution.py:197
  739.5 4.3 reshape.391
  743.8 5.5 fusion.84
  (272 shorter events, 92.7 us)
Async XLA Ops:
  7.2 82.9 %all-gather.12.cloned.1.call-start = ((), (), s32[]{:S(2)}) async-start(), calls=%async_computation.5 | async-start | bytes 3760128 | tf_op jit(solution)/shard_map/all_gather | solution.py:97
  8.0 101.1 %all-gather.14.cloned.1.call-start = ((), (), s32[]{:S(2)}) async-start(), calls=%async_computation.6 | async-start | bytes 2506752 | tf_op jit(solution)/shard_map/all_gather | solution.py:98
  8.7 144.7 %all-gather.18.cloned.1.call-start = ((), (), s32[]{:S(2)}) async-start(), calls=%async_computation.8 | async-start | bytes 2506752 | tf_op jit(solution)/shard_map/all_gather | solution.py:106
  11.0 172.8 %all-gather.16.cloned.1.call-start = ((), (), s32[]{:S(2)}) async-start(), calls=%async_computation.7 | async-start | bytes 2654208 | tf_op jit(solution)/shard_map/all_gather | solution.py:154
  93.5 8.7 %collective-permute-start = (bf16[128,512]{1,0:T(8,128)(2,1)S(1)}, bf16[128,512]{1,0:T(8,128)(2,1)S(1)}, u32[]{:S(2)}, u32[]{:S(2)}) collective-permute-start(bf16[128,512]{1,0:T(8,128)(2,1)S(1)} %pad_maximum_fusion.8), channel_id=1, source_target_pairs={{0,4},{1,5},{2,6},{3,7},{8,12},{9,13},{10,14},{11,15},{16,20},{17,... | collective-permute-start | bytes 393224 | tf_op jit(solution)/shard_map/ppermute | solution.py:24
  96.0 6.3 collective-permute-start.1
  97.4 6.9 collective-permute-start.2
  99.2 7.1 collective-permute-start.3
  111.4 288.6 %copy-start.31 = (f32[128]{0:T(128)}, f32[128]{0:T(128)S(1)}, u32[]{:S(2)}) copy-start(f32[128]{0:T(128)S(1)} %fusion.71) | copy-start | bytes 1540
  112.6 116.8 %all-gather.20.cloned.1.call-start = ((), (), s32[]{:S(2)}) async-start(), calls=%async_computation.9 | async-start | bytes 2506752 | tf_op jit(solution)/shard_map/all_gather | solution.py:107
  114.8 161.7 %all-gather.22.cloned.1.call-start = ((), (), s32[]{:S(2)}) async-start(), calls=%async_computation.10 | async-start | bytes 2506752 | tf_op jit(solution)/shard_map/all_gather | solution.py:108
  117.1 199.8 %reduce-scatter.8.cloned.1.call-start = ((), (), s32[]{:S(2)}) async-start(), calls=%async_computation.11 | async-start | bytes 2654208 | tf_op jit(solution)/shard_map/reduce_scatter | solution.py:162
  283.1 66.4 %all-gather.24.cloned.1.call-start = ((), (), s32[]{:S(2)}) async-start(), calls=%async_computation.12 | async-start | bytes 2654208 | tf_op jit(solution)/shard_map/all_gather | solution.py:169
  321.7 76.6 %reduce-scatter.10.cloned.1.call-start = ((), (), s32[]{:S(2)}) async-start(), calls=%async_computation.13 | async-start | bytes 2654208 | tf_op jit(solution)/shard_map/reduce_scatter | solution.py:179
  366.7 113.4 %reduce-scatter.12.cloned.1.call-start = ((), (), s32[]{:S(2)}) async-start(), calls=%async_computation.14 | async-start | bytes 2506752 | tf_op jit(solution)/shard_map/reduce_scatter | solution.py:262
  406.7 152.5 %reduce-scatter.16.cloned.1.call-start = ((), (), s32[]{:S(2)}) async-start(), calls=%async_computation.17 | async-start | bytes 3760128
  415.9 10.8 %collective-permute-start.7 = (bf16[128,512]{1,0:T(8,128)(2,1)}, bf16[128,512]{1,0:T(8,128)(2,1)S(1)}, u32[]{:S(2)}, u32[]{:S(2)}) collective-permute-start(bf16[128,512]{1,0:T(8,128)(2,1)} %get-tuple-element.40), channel_id=1, source_target_pairs={{4,0},{5,1},{6,2},{7,3},{12,8},{13,9},{14,10},{15,11},{20,16},{21,... | collective-permute-start | bytes 393224 | tf_op jit(solution)/shard_map/ppermute | solution.py:24
  417.2 12.0 %collective-permute-start.6 = (bf16[128,512]{1,0:T(8,128)(2,1)}, bf16[128,512]{1,0:T(8,128)(2,1)S(1)}, u32[]{:S(2)}, u32[]{:S(2)}) collective-permute-start(bf16[128,512]{1,0:T(8,128)(2,1)} %get-tuple-element.41), channel_id=1, source_target_pairs={{3,0},{4,1},{5,2},{6,3},{7,4},{11,8},{12,9},{13,10},{14,11},{15,12... | collective-permute-start | bytes 393224 | tf_op jit(solution)/shard_map/ppermute | solution.py:24
  418.5 11.5 %collective-permute-start.5 = (bf16[128,512]{1,0:T(8,128)(2,1)S(1)}, bf16[128,512]{1,0:T(8,128)(2,1)S(1)}, u32[]{:S(2)}, u32[]{:S(2)}) collective-permute-start(bf16[128,512]{1,0:T(8,128)(2,1)S(1)} %get-tuple-element.42), channel_id=1, source_target_pairs={{2,0},{3,1},{4,2},{5,3},{6,4},{7,5},{10,8},{11,9},{12,10},{13,11},... | collective-permute-start | bytes 393224 | tf_op jit(solution)/shard_map/ppermute | solution.py:24
  419.8 11.5 %collective-permute-start.4 = (bf16[128,512]{1,0:T(8,128)(2,1)S(1)}, bf16[128,512]{1,0:T(8,128)(2,1)S(1)}, u32[]{:S(2)}, u32[]{:S(2)}) collective-permute-start(bf16[128,512]{1,0:T(8,128)(2,1)S(1)} %get-tuple-element.39), channel_id=1, source_target_pairs={{1,0},{2,1},{3,2},{4,3},{5,4},{6,5},{7,6},{9,8},{10,9},{11,10},{12... | collective-permute-start | bytes 393224 | tf_op jit(solution)/shard_map/ppermute | solution.py:24
  437.2 208.0 %reduce-scatter.14.cloned.1.call-start = ((), (), s32[]{:S(2)}) async-start(), calls=%async_computation.15 | async-start | bytes 7520256 | tf_op jit(solution)/shard_map/reduce_scatter | solution.py:196
  452.5 194.7 %copy-start.22 = (f32[1152]{0:T(1024)S(1)}, f32[1152]{0:T(1024)}, u32[]{:S(2)}) copy-start(f32[1152]{0:T(1024)} %get-tuple-element.9) | copy-start | bytes 13828
  452.5 265.9 %all-reduce.13.cloned.1.call-start = ((), (), s32[]{:S(2)}) async-start(), calls=%async_computation.18 | async-start | bytes 737280 | tf_op jit(solution)/shard_map/psum | solution.py:265
  559.3 180.2 %all-gather.26.cloned.1.call-start = ((), (), s32[]{:S(2)}) async-start(), calls=%async_computation.16 | async-start | bytes 3483648 | tf_op jit(solution)/shard_map/all_gather | solution.py:197
  (51 other events, 1118.9 us)
Sparse Core Ops, SparseCore 0:
  10.2 49.0 all-gather.11
  61.5 43.9 all-gather.13
  108.3 45.0 all-gather.17
  155.5 28.2 all-gather.15
  186.4 42.9 all-gather.19
  231.4 45.0 all-gather.21
  283.2 33.6 reduce-scatter.7
  321.8 27.6 all-gather.23
  366.8 31.4 reduce-scatter.9
  406.8 73.2 reduce-scatter.11
  483.5 75.7 reduce-scatter.15
  562.6 82.5 reduce-scatter.13
  647.7 60.3 all-reduce.12
  710.2 29.2 all-gather.25

commit v2 on v1

--- a/solution.py
+++ b/solution.py
@@ -3,6 +3,8 @@
 import jax
 import jax.numpy as jnp
 from jax import lax
+from jax.experimental import pallas as pl
+from jax.experimental.pallas import tpu as pltpu
 from jax.sharding import PartitionSpec as P
 
 D = 1152
@@ -55,6 +57,236 @@
 
 def gelu_product(gate_pre, up_pre):
     return jax.nn.gelu(gate_pre, approximate=True) * up_pre
+
+
+MESH = pl.DeviceIdType.MESH
+NT = (((1,), (1,)), ((), ()))
+NN = (((1,), (0,)), ((), ()))
+TN = (((0,), (0,)), ((), ()))
+GELU_C = 0.7978845608028654
+GELU_A = 0.044715
+
+
+def dot32(left, right, dims):
+    return lax.dot_general(left, right, dims, preferred_element_type=jnp.float32)
+
+
+def ffn_kernel(
+    normed_ref, mid_ref, cot_ref, gain_ref, wg_hbm, wu_hbm, wd_hbm,
+    out_ref, gn_ref, ggain_ref, dg_hbm, du_hbm, dd_hbm,
+    wg, wu, wd, seq, gseq, act_a, act_b, hid, dgate, dup, part,
+    d2d_snd, d2d_in, ici_snd, ici_in, dw,
+    w_sem, o_sem, ag_s, ag_r, rd_s, rd_r, ri_s, ri_r,
+):
+    rows = normed_ref.shape[0]
+    units = wg.shape[0]
+    tile = 256
+    me = lax.axis_index("ctx")
+    chip, core = me // 2, lax.rem(me, 2)
+    partner = {"ctx": chip * 2 + 1 - core}
+    chips = {k: {"ctx": lax.rem(chip + k, 4) * 2 + core} for k in (1, 2, 3)}
+    order = (0, 1, 3, 2)
+
+    loads = [
+        pltpu.make_async_copy(src, dst, w_sem.at[i])
+        for i, (src, dst) in enumerate(((wg_hbm, wg), (wu_hbm, wu), (wd_hbm, wd)))
+    ]
+    for load in loads:
+        load.start()
+
+    barrier = pltpu.get_barrier_semaphore()
+    for peer in (partner, chips[1], chips[2], chips[3]):
+        pl.semaphore_signal(barrier, inc=1, device_id=peer, device_id_type=MESH)
+    pl.semaphore_wait(barrier, 4)
+
+    started = []
+
+    def send(src, dst, s_sem, r_sem, peer):
+        copy = pltpu.make_async_remote_copy(
+            src_ref=src, dst_ref=dst, send_sem=s_sem, recv_sem=r_sem,
+            device_id=peer, device_id_type=MESH,
+        )
+        copy.start()
+        started.append(copy)
+        return copy
+
+    def mine(k):
+        return pl.ds(k * 2 * rows, rows)
+
+    def other(k):
+        return pl.ds(k * 2 * rows + rows, rows)
+
+    def pair(k):
+        return pl.ds(k * 2 * rows, 2 * rows)
+
+    def spread(buf, ph):
+        own = buf.at[mine(0)]
+        got = {}
+        for k in (1, 3, 2):
+            back = 4 - k
+            got[back] = send(own, buf.at[mine(back)], ag_s.at[ph, k], ag_r.at[ph, back], chips[k])
+        got[0] = send(own, buf.at[other(0)], ag_s.at[ph, 0], ag_r.at[ph, 0], partner)
+        return got
+
+    def relay(buf, ph, got, k):
+        got[k].wait_recv()
+        got[k] = send(
+            buf.at[mine(k)], buf.at[other(k)], ag_s.at[ph, 4 + k], ag_r.at[ph, 4 + k], partner
+        )
+
+    def sum_out(ph, k):
+        d2d_snd[ph, k] = part[pl.ds(rows, rows), :].astype(jnp.bfloat16)
+        copy = send(
+            d2d_snd.at[ph, k], d2d_in.at[ph, k], rd_s.at[ph, k], rd_r.at[ph, k], partner
+        )
+        copy.wait_recv()
+        total = part[pl.ds(0, rows), :] + d2d_in[ph, k].astype(jnp.float32)
+        if k == 0:
+            return total
+        ici_snd[ph, k - 1] = total.astype(jnp.bfloat16)
+        back = 4 - k
+        return send(
+            ici_snd.at[ph, k - 1], ici_in.at[ph, back - 1], ri_s.at[ph, k], ri_r.at[ph, back],
+            chips[k],
+        )
+
+    def phase(buf, ph, work):
+        got = spread(buf, ph)
+        if ph == 0:
+            for load in loads:
+                load.wait()
+        sums = {}
+        for k in order:
+            if k == 1:
+                relay(buf, ph, got, 1)
+                relay(buf, ph, got, 3)
+            if k == 2:
+                relay(buf, ph, got, 2)
+            got[k].wait_recv()
+            work(k)
+            sums[k] = sum_out(ph, k)
+        return sums
+
+    def collect(ph, sums):
+        total = sums[0]
+        for k in (1, 3, 2):
+            sums[k].wait_recv()
+        for k in (1, 2, 3):
+            total = total + ici_in[ph, k - 1].astype(jnp.float32)
+        return total
+
+    def forward(k):
+        def one(t, carry):
+            cols = pl.ds(pl.multiple_of(t * tile, tile), tile)
+            block = seq[pair(k), :]
+            gate = dot32(block, wg[cols, :], NT)
+            up = dot32(block, wu[cols, :], NT)
+            square = gate * gate
+            th = jnp.tanh(GELU_C * gate * (1.0 + GELU_A * square))
+            half = 0.5 * (1.0 + th)
+            gelu = gate * half
+            slope = half + (0.5 * GELU_C) * gate * (1.0 - th * th) * (1.0 + 3.0 * GELU_A * square)
+            hid[pair(k), cols] = (gelu * up).astype(jnp.bfloat16)
+            act_a[pair(k), cols] = up * slope
+            act_b[pair(k), cols] = gelu
+            return carry
+
+        lax.fori_loop(0, units // tile, one, 0)
+        part[...] = dot32(hid[pair(k), :], wd[...], NN)
+
+    seq[mine(0), :] = normed_ref[...]
+    sums = phase(seq, 0, forward)
+    mlp = collect(0, sums)
+    r = lax.rsqrt(jnp.mean(mlp * mlp, axis=-1, keepdims=True) + EPS)
+    n = mlp * r
+    gain = gain_ref[...]
+    out_ref[...] = (mid_ref[...] + n * gain).astype(jnp.bfloat16)
+    dy = cot_ref[...].astype(jnp.float32)
+    ggain_ref[...] = jnp.sum(dy * n, axis=0, keepdims=True)
+    dyg = dy * gain
+    dv = r * (dyg - n * jnp.mean(dyg * n, axis=-1, keepdims=True))
+    gseq[mine(0), :] = dv.astype(jnp.bfloat16)
+
+    def backward(k):
+        def one(t, carry):
+            cols = pl.ds(pl.multiple_of(t * tile, tile), tile)
+            gh = dot32(gseq[pair(k), :], wd[cols, :], NT)
+            dgate[pair(k), cols] = (gh * act_a[pair(k), cols]).astype(jnp.bfloat16)
+            dup[pair(k), cols] = (gh * act_b[pair(k), cols]).astype(jnp.bfloat16)
+            return carry
+
+        lax.fori_loop(0, units // tile, one, 0)
+        part[...] = dot32(dgate[pair(k), :], wg[...], NN) + dot32(dup[pair(k), :], wu[...], NN)
+
+    sums = phase(gseq, 1, backward)
+    stores = []
+    for i, (left, right, dst) in enumerate(
+        ((hid, gseq, dd_hbm), (dgate, seq, dg_hbm), (dup, seq, du_hbm))
+    ):
+        def one(t, carry, i=i, left=left, right=right):
+            cols = pl.ds(pl.multiple_of(t * tile, tile), tile)
+            dw[i, cols, :] = dot32(left[:, cols], right[...], TN).astype(jnp.bfloat16)
+            return carry
+
+        lax.fori_loop(0, units // tile, one, 0)
+        store = pltpu.make_async_copy(dw.at[i], dst, o_sem.at[i])
+        store.start()
+        stores.append(store)
+    gn_ref[...] = collect(1, sums)
+    for copy in started:
+        copy.wait_send()
+    for store in stores:
+        store.wait()
+
+
+def ffn(normed_two, mid, cot, gain, wg, wu, wd):
+    rows = normed_two.shape[0]
+    units = wg.shape[0]
+    seq_rows = rows * 8
+    bf, f32 = jnp.bfloat16, jnp.float32
+    vm = pl.BlockSpec(memory_space=pltpu.VMEM)
+    hbm = pl.BlockSpec(memory_space=pl.ANY)
+    dma = pltpu.SemaphoreType.DMA
+    weight = jax.ShapeDtypeStruct((units, D), bf)
+    return pl.pallas_call(
+        ffn_kernel,
+        out_shape=(
+            jax.ShapeDtypeStruct((rows, D), bf),
+            jax.ShapeDtypeStruct((rows, D), f32),
+            jax.ShapeDtypeStruct((1, D), f32),
+            weight, weight, weight,
+        ),
+        in_specs=[vm] * 4 + [hbm] * 3,
+        out_specs=(vm, vm, vm, hbm, hbm, hbm),
+        scratch_shapes=[
+            pltpu.VMEM((units, D), bf),
+            pltpu.VMEM((units, D), bf),
+            pltpu.VMEM((units, D), bf),
+            pltpu.VMEM((seq_rows, D), bf),
+            pltpu.VMEM((seq_rows, D), bf),
+            pltpu.VMEM((seq_rows, units), f32),
+            pltpu.VMEM((seq_rows, units), f32),
+            pltpu.VMEM((seq_rows, units), bf),
+            pltpu.VMEM((seq_rows, units), bf),
+            pltpu.VMEM((seq_rows, units), bf),
+            pltpu.VMEM((2 * rows, D), f32),
+            pltpu.VMEM((2, 4, rows, D), bf),
+            pltpu.VMEM((2, 4, rows, D), bf),
+            pltpu.VMEM((2, 3, rows, D), bf),
+            pltpu.VMEM((2, 3, rows, D), bf),
+            pltpu.VMEM((3, units, D), bf),
+            dma((3,)), dma((3,)),
+            dma((2, 8)), dma((2, 8)),
+            dma((2, 4)), dma((2, 4)),
+            dma((2, 4)), dma((2, 4)),
+        ],
+        compiler_params=pltpu.CompilerParams(
+            collective_id=1, has_side_effects=True, vmem_limit_bytes=58 * 1024 * 1024
+        ),
+        cost_estimate=pl.CostEstimate(
+            flops=18 * seq_rows * units * D, bytes_accessed=14 * units * D, transcendentals=0
+        ),
+    )(normed_two, mid, cot, gain, wg, wu, wd)
 
 
 def on_device(
@@ -151,48 +383,19 @@
     mid_stream = stream + rms_norm(attn, gains_all[1])
     normed_two = rms_norm(mid_stream, gains_all[2]).astype(jnp.bfloat16)
 
-    normed_seq = lax.all_gather(normed_two, "ctx", axis=0, tiled=True)
-    gate_pre = lax.dot_general(
-        normed_seq, gate_full, CONTRACT_LAST, preferred_element_type=jnp.float32
-    )
-    up_pre = lax.dot_general(normed_seq, up_full, CONTRACT_LAST, preferred_element_type=jnp.float32)
-    hidden_value, hidden_back = jax.vjp(gelu_product, gate_pre, up_pre)
-    hidden_low = hidden_value.astype(jnp.bfloat16)
-    mlp_part = jnp.dot(hidden_low, down_full, preferred_element_type=jnp.float32)
-    mlp_out = lax.psum_scatter(
-        mlp_part.astype(jnp.bfloat16), "ctx", scatter_dimension=0, tiled=True
-    ).astype(jnp.float32)
-    final = mid_stream + rms_norm(mlp_out, gains_all[3])
-    output = final.reshape(1, local_len, D).astype(jnp.bfloat16)
     grad_final = cotangent.astype(jnp.float32).reshape(local_len, D)
-    grad_mlp, grad_gain_three = jax.vjp(rms_norm, mlp_out, gains_all[3])[1](grad_final)
-    grad_mlp_seq = lax.all_gather(grad_mlp.astype(jnp.bfloat16), "ctx", axis=0, tiled=True)
-    grad_hidden = lax.dot_general(
-        grad_mlp_seq, down_full, CONTRACT_LAST, preferred_element_type=jnp.float32
-    )
-    grad_gate, grad_up = hidden_back(grad_hidden)
-    grad_gate_low = grad_gate.astype(jnp.bfloat16)
-    grad_up_low = grad_up.astype(jnp.bfloat16)
-    grad_normed_part = jnp.dot(
-        grad_gate_low, gate_full, preferred_element_type=jnp.float32
-    ) + jnp.dot(grad_up_low, up_full, preferred_element_type=jnp.float32)
-    grad_normed_two = lax.psum_scatter(
-        grad_normed_part.astype(jnp.bfloat16), "ctx", scatter_dimension=0, tiled=True
-    ).astype(jnp.float32)
-    mlp_grads = jnp.concatenate(
-        [
-            lax.dot_general(
-                grad_gate_low, normed_seq, CONTRACT_FIRST, preferred_element_type=jnp.float32
-            ),
-            lax.dot_general(
-                grad_up_low, normed_seq, CONTRACT_FIRST, preferred_element_type=jnp.float32
-            ),
-            lax.dot_general(
-                hidden_low, grad_mlp_seq, CONTRACT_FIRST, preferred_element_type=jnp.float32
-            ),
-        ],
-        axis=1,
-    ).astype(jnp.bfloat16)
+    output, grad_normed_two, grad_gain_three, d_gate, d_up, d_down = ffn(
+        normed_two,
+        mid_stream,
+        cotangent.reshape(local_len, D),
+        gains_all[3:4],
+        gate_full,
+        up_full,
+        down_full,
+    )
+    output = output.reshape(1, local_len, D)
+    grad_gain_three = grad_gain_three[0]
+    mlp_grads = jnp.concatenate([d_gate, d_up, d_down], axis=1)
     mlp_share = lax.psum_scatter(mlp_grads, "fsdp", scatter_dimension=0, tiled=True)
     mlp_total = lax.all_gather(mlp_share[:slice_rows], "ctx", axis=0, tiled=True).astype(
         jnp.float32

time: 764 us -> 688 us (0.901)
  waiting for transfers between devices: 455 us -> 359 us
  Pallas kernels: 0 us -> 83.1 us
  matrix products: 74.4 us -> 22.1 us
    pallas_call x0 -> x1, Pallas kernels: none -> 83.1 us  [ffn(): pl.pallas_call(ffn_kernel, out_shape=(jax.ShapeDtypeStruct((rows, D), bf)...]
    reduce_scatter x2 -> x0, waiting for transfers between devices: 65.2 us -> none  [the longest x1 33.6 us: on_device(): lax.psum_scatter(mlp_part.astype(jnp.bfloat16), 'ctx', scatter_dimension=...]
    all_gather x2 -> x0, waiting for transfers between devices: 57.9 us -> none  [the longest x1 30.4 us: on_device(): normed_seq = lax.all_gather(normed_two, 'ctx', axis=0, tiled=True)]
    dot_general x9 -> x0, matrix products: 52.2 us -> none  [the longest x1 9.85 us: on_device(): lax.dot_general(grad_mlp_seq, down_full, CONTRACT_LAST, preferred_element...]
    all_gather x1, waiting for transfers between devices: 37.4 us -> 47.1 us  [on_device(): lax.all_gather(my_slice(down_weight), 'fsdp', axis=0, tiled=True)]
    all_gather x1, waiting for transfers between devices: 38.4 us -> 47.7 us  [on_device(): up_full = lax.all_gather(my_slice(up_weight), 'fsdp', axis=0, tiled=True)]
    unnamed x15 -> x11, waiting for transfers between devices: 80.7 us -> 80.6 us
  transfers between devices with their start and end apart: 22 -> 18, of which waited for: 16 -> 12; matrix products, arithmetic and copies ran while one was open for 10% -> 7% of each run, Pallas kernels for 0% -> 0%
where the time goes in v2:
time: 688 us; the launch traced here: 685 us
  waiting for transfers between devices  359 us (52%)
  blocking collectives  141 us (20%)
  Pallas kernels  83.1 us (12%)
  local copies, waits for them, and re-layouts  29.3 us (4%)
  matrix products  22.1 us (3%)
  other arithmetic  19.5 us (3%)
  between operations  15.9 us (2%)
  starting transfers between devices  15.2 us (2%)
    reduce_scatter x1, waiting for transfers between devices, on_device(): lax.psum_scatter(mlp_grads, 'fsdp', scatter_dimension=0, tiled=True)  85.9 us
    pallas_call x1, Pallas kernels, ffn(): pl.pallas_call(ffn_kernel, out_shape=(jax.ShapeDtypeStruct((rows, D), bf)...  83.1 us
    unnamed x11, waiting for transfers between devices  80.6 us
    psum x1, blocking collectives, on_device(): small_total = lax.psum(small, ('fsdp', 'ctx'))  65.1 us
    unnamed x1, blocking collectives  52 us
    all_gather x1, waiting for transfers between devices, on_device(): up_full = lax.all_gather(my_slice(up_weight), 'fsdp', axis=0, tiled=True)  47.7 us
    all_gather x1, waiting for transfers between devices, on_device(): lax.all_gather(my_slice(down_weight), 'fsdp', axis=0, tiled=True)  47.1 us
    all_gather x1, waiting for transfers between devices, on_device(): lax.all_gather(my_slice(gate_weight), 'fsdp', axis=0, tiled=True)  37.8 us
  transfers between devices with their start and end apart: 18, of which 12 were waited for; matrix products, arithmetic and copies ran while one was open for 7% of the time, Pallas kernels for 0%

profile of v2, /device:TPU:73, one launch (start us, length us, event | category | flops | bytes accessed | tf_op | source)
XLA Modules:
  0.0 685.5 jit_solution(7965549095739397622)
XLA Ops:
  15.0 52.0 %all-reduce.8 = bf16[5120]{0:T(1024)(128)(2,1)S(1)} all-reduce(bf16[5120]{0:T(1024)(128)(2,1)S(1)} %dynamic-update-slice), channel_id=2, replica_groups=mesh['fsdp'=16,'ctx'=8] {'fsdp'}, use_global_device_ids=true, to_apply=%add.8 | all-reduce | flops 5120 | bytes 20480
  67.9 24.0 %all-gather.1 = s32[1,1024]{1,0:T(1,128)S(1)} all-gather(s32[1,128]{1,0:T(1,128)S(1)} %copy-done.41), channel_id=3, replica_groups=mesh['fsdp'=16,'ctx'=8] {'ctx'}, dimensions={1}, use_global_device_ids=true | all-gather | bytes 4608 | tf_op jit(solution)/shard_map/all_gather | solution.py:328
  93.1 2.7 fusion.41
  96.5 2.5 collective-permute-start
  112.1 2.3 multiply_reduce_fusion.6
  115.5 37.8 %all-gather.14.cloned.1.call-done.wg_hbm = bf16[1024,1152]{1,0:T(8,128)(2,1)} async-done(((bf16[64,1152]{1,0:T(8,128)(2,1)}), bf16[1024,1152]{1,0:T(8,128)(2,1)}) %all-gather.14.cloned.1.call-update) | async-done | bytes 2359312 | tf_op jit(solution)/shard_map/all_gather | solution.py:338
  153.4 47.7 %all-gather.16.cloned.1.call-done.wu_hbm = bf16[1024,1152]{1,0:T(8,128)(2,1)} async-done(((bf16[64,1152]{1,0:T(8,128)(2,1)}), bf16[1024,1152]{1,0:T(8,128)(2,1)}) %all-gather.16.cloned.1.call-update) | async-done | bytes 2359312 | tf_op jit(solution)/shard_map/all_gather | solution.py:339
  201.1 47.1 %all-gather.18.cloned.1.call-done.wd_hbm = bf16[1024,1152]{1,0:T(8,128)(2,1)} async-done(((bf16[64,1152]{1,0:T(8,128)(2,1)}), bf16[1024,1152]{1,0:T(8,128)(2,1)}) %all-gather.18.cloned.1.call-update) | async-done | bytes 2359312 | tf_op jit(solution)/shard_map/all_gather | solution.py:340
  248.2 83.1 %shard_map.169 = (bf16[128,1152]{1,0:T(8,128)(2,1)}, f32[128,1152]{1,0:T(8,128)}, f32[1,1152]{1,0:T(1,128)}, bf16[1024,1152]{1,0:T(8,128)(2,1)}, bf16[1024,1152]{1,0:T(8,128)(2,1)}, /*index=5*/bf16[1024,1152]{1,0:T(8,128)(2,1)}) custom-call(bf16[128,1152]{1,0:T(8,128)(2,1)} %multiply_convert_fusion.1.normed_ref, f32[128,1152]{1,0:T(8,128)} %copy-done.1, ...), custom_call_target="tpu_custom_call" | custom-call | flops 21743271936 | bytes 16515072 | tf_op jit(solution)/shard_map/pallas_call | solution.py:251
  335.3 2.2 convolution_convert_fusion.1
  342.5 2.3 convolution_bitcast_fusion.1
  348.3 3.1 collective-permute-start.4
  356.6 2.4 collective-permute-done.5
  361.0 2.7 collective-permute-done.7
  366.5 3.1 convolution_convert_fusion
  371.2 5.7 pad_maximum_fusion
  377.1 31.5 %reduce-scatter.6.cloned.1.call-done = bf16[64,1152]{1,0:T(8,128)(2,1)} async-done(((bf16[1024,1152]{1,0:T(8,128)(2,1)}), bf16[64,1152]{1,0:T(8,128)(2,1)}) %reduce-scatter.6.cloned.1.call-update) | async-done | bytes 147472 | tf_op jit(solution)/shard_map/reduce_scatter | solution.py:465
  408.6 79.1 %reduce-scatter.10.cloned.1.call-done = bf16[72,1536]{1,0:T(8,128)(2,1)} async-done(((bf16[1152,1536]{1,0:T(8,128)(2,1)}), bf16[72,1536]{1,0:T(8,128)(2,1)}) %reduce-scatter.10.cloned.1.call-update) | async-done | bytes 221200
  487.8 85.9 %reduce-scatter.8.cloned.1.call-done = bf16[64,3456]{1,0:T(8,128)(2,1)} async-done(((bf16[1024,3456]{1,0:T(8,128)(2,1)}), bf16[64,3456]{1,0:T(8,128)(2,1)}) %reduce-scatter.8.cloned.1.call-update) | async-done | bytes 442384 | tf_op jit(solution)/shard_map/reduce_scatter | solution.py:399
  575.8 3.4 fusion.11
  579.8 65.1 %psum.21 = f32[16,320]{1,0:T(8,128)S(1)} all-reduce(f32[16,320]{1,0:T(8,128)S(1)} %pad_maximum_fusion.11), channel_id=1, replica_groups=mesh['fsdp'=16,'ctx'=8] {'fsdp','ctx'}, use_global_device_ids=true, to_apply=%region_18.19 | all-reduce | flops 5120 | bytes 40960 | tf_op jit(solution)/shard_map/psum | solution.py:458
  650.7 17.4 %all-gather.20.cloned.1.call-done = bf16[8,54,3456]{2,1,0:T(8,128)(2,1)} async-done(((bf16[1,54,3456]{2,1,0:T(8,128)(2,1)}), bf16[8,54,3456]{2,1,0:T(8,128)(2,1)}) %all-gather.20.cloned.1.call-update) | async-done | bytes 2986000 | tf_op jit(solution)/shard_map/all_gather | solution.py:400
  668.1 4.3 reshape.371
  672.4 5.5 fusion.65
  (242 shorter events, 56.5 us)
Async XLA Ops:
  7.2 85.9 %all-gather.10.cloned.1.call-start = ((), (), s32[]{:S(2)}) async-start(), calls=%async_computation.3 | async-start | bytes 3760128 | tf_op jit(solution)/shard_map/all_gather | solution.py:329
  7.9 104.2 %all-gather.12.cloned.1.call-start = ((), (), s32[]{:S(2)}) async-start(), calls=%async_computation.4 | async-start | bytes 2506752 | tf_op jit(solution)/shard_map/all_gather | solution.py:330
  8.7 144.7 %all-gather.14.cloned.1.call-start = ((), (), s32[]{:S(2)}) async-start(), calls=%async_computation.5 | async-start | bytes 2506752 | tf_op jit(solution)/shard_map/all_gather | solution.py:338
  11.0 190.1 %all-gather.16.cloned.1.call-start = ((), (), s32[]{:S(2)}) async-start(), calls=%async_computation.6 | async-start | bytes 2506752 | tf_op jit(solution)/shard_map/all_gather | solution.py:339
  12.1 236.1 %all-gather.18.cloned.1.call-start = ((), (), s32[]{:S(2)}) async-start(), calls=%async_computation.7 | async-start | bytes 2506752 | tf_op jit(solution)/shard_map/all_gather | solution.py:340
  13.2 395.4 %reduce-scatter.6.cloned.1.call-start = ((), (), s32[]{:S(2)}) async-start(), calls=%async_computation.8 | async-start | bytes 2506752 | tf_op jit(solution)/shard_map/reduce_scatter | solution.py:465
  96.5 8.7 %collective-permute-start = (bf16[128,512]{1,0:T(8,128)(2,1)S(1)}, bf16[128,512]{1,0:T(8,128)(2,1)S(1)}, u32[]{:S(2)}, u32[]{:S(2)}) collective-permute-start(bf16[128,512]{1,0:T(8,128)(2,1)S(1)} %pad_maximum_fusion.8), channel_id=1, source_target_pairs={{0,4},{1,5},{2,6},{3,7},{8,12},{9,13},{10,14},{11,15},{16,20},{17,... | collective-permute-start | bytes 393224 | tf_op jit(solution)/shard_map/ppermute | solution.py:26
  99.0 6.3 collective-permute-start.1
  100.4 6.9 %collective-permute-start.2 = (bf16[128,512]{1,0:T(8,128)(2,1)S(1)}, bf16[128,512]{1,0:T(8,128)(2,1)S(1)}, u32[]{:S(2)}, u32[]{:S(2)}) collective-permute-start(bf16[128,512]{1,0:T(8,128)(2,1)S(1)} %pad_maximum_fusion.8), channel_id=1, source_target_pairs={{0,2},{1,3},{2,4},{3,5},{4,6},{5,7},{8,10},{9,11},{10,12},{11,13},... | collective-permute-start | bytes 393224 | tf_op jit(solution)/shard_map/ppermute | solution.py:26
  102.3 7.1 %collective-permute-start.3 = (bf16[128,512]{1,0:T(8,128)(2,1)S(1)}, bf16[128,512]{1,0:T(8,128)(2,1)S(1)}, u32[]{:S(2)}, u32[]{:S(2)}) collective-permute-start(bf16[128,512]{1,0:T(8,128)(2,1)S(1)} %pad_maximum_fusion.8), channel_id=1, source_target_pairs={{0,1},{1,2},{2,3},{3,4},{4,5},{5,6},{6,7},{8,9},{9,10},{10,11},{11... | collective-permute-start | bytes 393224 | tf_op jit(solution)/shard_map/ppermute | solution.py:26
  114.6 133.6 %copy-start.1 = (f32[128,1152]{1,0:T(8,128)}, f32[128,1152]{1,0:T(8,128)S(1)}, u32[]{:S(2)}) copy-start(f32[128,1152]{1,0:T(8,128)S(1)} %get-tuple-element.41.mid_ref) | copy-start | bytes 1769476
  248.2 85.3 %copy-start.21 = (bf16[1,128,1152]{2,1,0:T(8,128)(2,1)S(1)}, bf16[1,128,1152]{2,1,0:T(8,128)(2,1)}, u32[]{:S(2)}) copy-start(bf16[1,128,1152]{2,1,0:T(8,128)(2,1)} %param.19) | copy-start | bytes 884740
  337.4 150.3 %reduce-scatter.10.cloned.1.call-start = ((), (), s32[]{:S(2)}) async-start(), calls=%async_computation.11 | async-start | bytes 3760128
  348.3 8.3 %collective-permute-start.4 = (bf16[128,512]{1,0:T(8,128)(2,1)}, bf16[128,512]{1,0:T(8,128)(2,1)S(1)}, u32[]{:S(2)}, u32[]{:S(2)}) collective-permute-start(bf16[128,512]{1,0:T(8,128)(2,1)} %get-tuple-element.47), channel_id=1, source_target_pairs={{1,0},{2,1},{3,2},{4,3},{5,4},{6,5},{7,6},{9,8},{10,9},{11,10},{12... | collective-permute-start | bytes 393224 | tf_op jit(solution)/shard_map/ppermute | solution.py:26
  351.5 7.6 %collective-permute-start.5 = (bf16[128,512]{1,0:T(8,128)(2,1)}, bf16[128,512]{1,0:T(8,128)(2,1)S(1)}, u32[]{:S(2)}, u32[]{:S(2)}) collective-permute-start(bf16[128,512]{1,0:T(8,128)(2,1)} %get-tuple-element.50), channel_id=1, source_target_pairs={{2,0},{3,1},{4,2},{5,3},{6,4},{7,5},{10,8},{11,9},{12,10},{13,11},... | collective-permute-start | bytes 393224 | tf_op jit(solution)/shard_map/ppermute | solution.py:26
  352.8 8.2 %collective-permute-start.6 = (bf16[128,512]{1,0:T(8,128)(2,1)}, bf16[128,512]{1,0:T(8,128)(2,1)S(1)}, u32[]{:S(2)}, u32[]{:S(2)}) collective-permute-start(bf16[128,512]{1,0:T(8,128)(2,1)} %get-tuple-element.49), channel_id=1, source_target_pairs={{3,0},{4,1},{5,2},{6,3},{7,4},{11,8},{12,9},{13,10},{14,11},{15,12... | collective-permute-start | bytes 393224 | tf_op jit(solution)/shard_map/ppermute | solution.py:26
  354.1 9.6 %collective-permute-start.7 = (bf16[128,512]{1,0:T(8,128)(2,1)}, bf16[128,512]{1,0:T(8,128)(2,1)S(1)}, u32[]{:S(2)}, u32[]{:S(2)}) collective-permute-start(bf16[128,512]{1,0:T(8,128)(2,1)} %get-tuple-element.48), channel_id=1, source_target_pairs={{4,0},{5,1},{6,2},{7,3},{12,8},{13,9},{14,10},{15,11},{20,16},{21,... | collective-permute-start | bytes 393224 | tf_op jit(solution)/shard_map/ppermute | solution.py:26
  369.6 204.1 %reduce-scatter.8.cloned.1.call-start = ((), (), s32[]{:S(2)}) async-start(), calls=%async_computation.9 | async-start | bytes 7520256 | tf_op jit(solution)/shard_map/reduce_scatter | solution.py:399
  377.0 198.5 %copy-start.25 = (f32[1152]{0:T(1024)S(1)}, f32[1152]{0:T(1024)}, u32[]{:S(2)}) copy-start(f32[1152]{0:T(1024)} %get-tuple-element.21) | copy-start | bytes 13828
  377.0 198.5 %copy-start.24 = (f32[1152]{0:T(1024)S(1)}, f32[1152]{0:T(1024)}, u32[]{:S(2)}) copy-start(f32[1152]{0:T(1024)} %get-tuple-element.23) | copy-start | bytes 13828
  377.0 198.6 %copy-start.34 = (f32[1,1152]{1,0:T(1,128)S(1)}, f32[1,1152]{1,0:T(1,128)}, u32[]{:S(2)}) copy-start(f32[1,1152]{1,0:T(1,128)} %get-tuple-element.17) | copy-start | bytes 13828
  377.0 270.3 %all-reduce.13.cloned.1.call-start = ((), (), s32[]{:S(2)}) async-start(), calls=%async_computation.12 | async-start | bytes 737280 | tf_op jit(solution)/shard_map/psum | solution.py:468
  487.7 180.4 %all-gather.20.cloned.1.call-start = ((), (), s32[]{:S(2)}) async-start(), calls=%async_computation.10 | async-start | bytes 3483648 | tf_op jit(solution)/shard_map/all_gather | solution.py:400
  575.8 70.4 %copy-start.5 = (f32[128,1152]{1,0:T(8,128)S(1)}, f32[128,1152]{1,0:T(8,128)}, u32[]{:S(2)}) copy-start(f32[128,1152]{1,0:T(8,128)} %copy-done.4) | copy-start | bytes 1769476
  (43 other events, 524.9 us)
Sparse Core Ops, SparseCore 0:
  10.2 49.0 all-gather.9
  61.5 44.0 all-gather.11
  108.3 45.0 all-gather.13
  156.0 45.0 all-gather.15
  203.1 45.0 all-gather.17
  337.6 70.9 reduce-scatter.5
  412.0 75.6 reduce-scatter.9
  491.2 82.4 reduce-scatter.7
  576.2 60.3 all-reduce.12
  638.7 29.3 all-gather.19

commit v3 on v2

--- a/solution.py
+++ b/solution.py
@@ -72,7 +72,7 @@
 
 
 def ffn_kernel(
-    normed_ref, mid_ref, cot_ref, gain_ref, wg_hbm, wu_hbm, wd_hbm,
+    normed_ref, mid_ref, cot_ref, gain_ref, w_hbm,
     out_ref, gn_ref, ggain_ref, dg_hbm, du_hbm, dd_hbm,
     wg, wu, wd, seq, gseq, act_a, act_b, hid, dgate, dup, part,
     d2d_snd, d2d_in, ici_snd, ici_in, dw,
@@ -80,6 +80,7 @@
 ):
     rows = normed_ref.shape[0]
     units = wg.shape[0]
+    share = units // w_hbm.shape[0]
     tile = 256
     me = lax.axis_index("ctx")
     chip, core = me // 2, lax.rem(me, 2)
@@ -88,8 +89,11 @@
     order = (0, 1, 3, 2)
 
     loads = [
-        pltpu.make_async_copy(src, dst, w_sem.at[i])
-        for i, (src, dst) in enumerate(((wg_hbm, wg), (wu_hbm, wu), (wd_hbm, wd)))
+        pltpu.make_async_copy(
+            w_hbm.at[f, pl.ds(i * share, share), :], dst.at[pl.ds(f * share, share), :], w_sem.at[i, f]
+        )
+        for i, dst in enumerate((wg, wu, wd))
+        for f in range(w_hbm.shape[0])
     ]
     for load in loads:
         load.start()
@@ -239,9 +243,10 @@
         store.wait()
 
 
-def ffn(normed_two, mid, cot, gain, wg, wu, wd):
+def ffn(normed_two, mid, cot, gain, weights):
     rows = normed_two.shape[0]
-    units = wg.shape[0]
+    owners, lines = weights.shape[:2]
+    units = owners * lines // 3
     seq_rows = rows * 8
     bf, f32 = jnp.bfloat16, jnp.float32
     vm = pl.BlockSpec(memory_space=pltpu.VMEM)
@@ -256,7 +261,7 @@
             jax.ShapeDtypeStruct((1, D), f32),
             weight, weight, weight,
         ),
-        in_specs=[vm] * 4 + [hbm] * 3,
+        in_specs=[vm] * 4 + [hbm],
         out_specs=(vm, vm, vm, hbm, hbm, hbm),
         scratch_shapes=[
             pltpu.VMEM((units, D), bf),
@@ -275,7 +280,7 @@
             pltpu.VMEM((2, 3, rows, D), bf),
             pltpu.VMEM((2, 3, rows, D), bf),
             pltpu.VMEM((3, units, D), bf),
-            dma((3,)), dma((3,)),
+            dma((3, owners)), dma((3,)),
             dma((2, 8)), dma((2, 8)),
             dma((2, 4)), dma((2, 4)),
             dma((2, 4)), dma((2, 4)),
@@ -286,7 +291,404 @@
         cost_estimate=pl.CostEstimate(
             flops=18 * seq_rows * units * D, bytes_accessed=14 * units * D, transcendentals=0
         ),
-    )(normed_two, mid, cot, gain, wg, wu, wd)
+    )(normed_two, mid, cot, gain, weights)
+
+
+def place():
+    fsdp = lax.axis_index("fsdp")
+    ctx = lax.axis_index("ctx")
+    y, z = fsdp // 4, lax.rem(fsdp, 4)
+    chip, core = ctx // 2, lax.rem(ctx, 2)
+    return y, z, chip, core
+
+
+def shape_of(y, z, core):
+    first = (1 - core) * y + core * z
+    second = (1 - core) * z + core * y
+
+    def block(i, j):
+        return (1 - core) * (4 * i + j) + core * (4 * j + i)
+
+    return first, second, block
+
+
+def remote(src, dst, s_sem, r_sem, peer):
+    return pltpu.make_async_remote_copy(
+        src_ref=src, dst_ref=dst, send_sem=s_sem, recv_sem=r_sem,
+        device_id=peer, device_id_type=MESH,
+    )
+
+
+def greet(peers):
+    barrier = pltpu.get_barrier_semaphore()
+    for peer in peers:
+        pl.semaphore_signal(barrier, inc=1, device_id=peer, device_id_type=MESH)
+    pl.semaphore_wait(barrier, len(peers))
+
+
+def gather_kernel(
+    qkv_ref, wo_ref, qkv_out, wo_all, rows_out, qkv_all,
+    l_sem, s1, r1, s2, r2, sd, rd,
+):
+    y, z, chip, core = place()
+    a, b, block = shape_of(y, z, core)
+    _, _, block_there = shape_of(y, z, 1 - core)
+    q_rows, width = qkv_ref.shape
+    o_rows = wo_ref.shape[0]
+    q_half, o_half = width // 2, o_rows // 2
+    partner = {"ctx": chip * 2 + 1 - core}
+
+    def views(f, half):
+        return (
+            qkv_all.at[
+                pl.ds(pl.multiple_of(f * q_rows, 16), q_rows),
+                pl.ds(pl.multiple_of(half * q_half, 128), q_half),
+            ],
+            wo_all.at[pl.ds(pl.multiple_of(f * o_rows + half * o_half, 16), o_half), :],
+        )
+
+    mine = (
+        qkv_ref.at[:, pl.ds(pl.multiple_of(core * q_half, 128), q_half)],
+        wo_ref.at[pl.ds(pl.multiple_of(core * o_half, 16), o_half), :],
+    )
+    here = block(a, b)
+    locals_ = [
+        pltpu.make_async_copy(
+            qkv_ref, qkv_all.at[pl.ds(pl.multiple_of(here * q_rows, 16), q_rows), :], l_sem.at[0]
+        ),
+        pltpu.make_async_copy(
+            wo_ref, wo_all.at[pl.ds(pl.multiple_of(here * o_rows, 16), o_rows), :], l_sem.at[1]
+        ),
+    ]
+    for copy in locals_:
+        copy.start()
+
+    def first_peer(k):
+        return {"fsdp": block(lax.rem(a + k, 4), b)}
+
+    def second_peer(k):
+        return {"fsdp": block(a, lax.rem(b + k, 4))}
+
+    greet([first_peer(k) for k in (1, 2, 3)] + [second_peer(k) for k in (1, 2, 3)] + [partner])
+
+    def hop_one(k, t):
+        return remote(mine[t], views(here, core)[t], s1.at[k, t], r1.at[4 - k, t], first_peer(k))
+
+    def hop_two(j, k, t):
+        f = block(lax.rem(a + j, 4), b)
+        dst = views(f, core)[t]
+        src = dst if j else mine[t]
+        return remote(src, dst, s2.at[j, k, t], r2.at[j, 4 - k, t], second_peer(k))
+
+    def arrive_one(j, t):
+        dst = views(block(lax.rem(a + j, 4), b), core)[t]
+        return remote(dst, dst, s1.at[j, t], r1.at[j, t], partner)
+
+    def arrive_two(j, m, t):
+        dst = views(block(lax.rem(a + j, 4), lax.rem(b + m, 4)), core)[t]
+        return remote(dst, dst, s2.at[j, m, t], r2.at[j, m, t], partner)
+
+    def cross(j, m, t):
+        dst = views(block(lax.rem(a + j, 4), lax.rem(b + m, 4)), core)[t]
+        return remote(dst, dst, sd.at[j, m, t], rd.at[j, m, t], partner)
+
+    def arrive_cross(j, m, t):
+        dst = views(block_there(lax.rem(b + j, 4), lax.rem(a + m, 4)), 1 - core)[t]
+        return remote(dst, dst, sd.at[j, m, t], rd.at[j, m, t], partner)
+
+    both = (0, 1)
+    for k in (1, 3, 2):
+        for t in both:
+            hop_one(k, t).start()
+    for k in (1, 3, 2):
+        for t in both:
+            hop_two(0, k, t).start()
+    for j in (1, 3, 2):
+        for t in both:
+            arrive_one(j, t).wait_recv()
+            for k in (1, 3, 2):
+                hop_two(j, k, t).start()
+            cross(j, 0, t).start()
+
+    def pass_on(i, carry):
+        m, j = i // 4 + 1, lax.rem(i, 4)
+        for t in both:
+            arrive_two(j, m, t).wait_recv()
+            cross(j, m, t).start()
+        return carry
+
+    lax.fori_loop(0, 12, pass_on, 0)
+
+    def land(i, carry):
+        m, j = i // 4, lax.rem(i, 4)
+        for t in both:
+            arrive_cross(j, m, t).wait_recv()
+            cross(j, m, t).wait_send()
+        return carry
+
+    lax.fori_loop(1, 16, land, 0)
+    for copy in locals_:
+        copy.wait()
+    for k in (1, 2, 3):
+        for t in both:
+            hop_one(k, t).wait_send()
+            for j in range(4):
+                hop_two(j, k, t).wait_send()
+
+    keep = qkv_out.shape[0] // 16
+    for f in range(0, 16, 2):
+        left = qkv_all[pl.ds(f * q_rows, q_rows), :].astype(jnp.float32)
+        right = qkv_all[pl.ds((f + 1) * q_rows, q_rows), :].astype(jnp.float32)
+        qkv_out[pl.ds(f * keep, 2 * keep), :] = jnp.concatenate(
+            [left[:keep], right[:keep]], axis=0
+        ).astype(jnp.bfloat16)
+        rows_out[f] = left[keep:, : rows_out.shape[2]]
+        rows_out[f + 1] = right[keep:, : rows_out.shape[2]]
+
+
+def gather_attention(qkv_shard, wo_shard, keep, extra):
+    bf = jnp.bfloat16
+    vm = pl.BlockSpec(memory_space=pltpu.VMEM)
+    dma = pltpu.SemaphoreType.DMA
+    q_rows, width = qkv_shard.shape
+    o_rows, o_width = wo_shard.shape
+    return pl.pallas_call(
+        gather_kernel,
+        out_shape=(
+            jax.ShapeDtypeStruct((16 * keep, width), bf),
+            jax.ShapeDtypeStruct((16 * o_rows, o_width), bf),
+            jax.ShapeDtypeStruct((16, q_rows - keep, extra), jnp.float32),
+        ),
+        in_specs=[vm] * 2,
+        out_specs=(vm,) * 3,
+        scratch_shapes=[
+            pltpu.VMEM((16 * q_rows, width), bf),
+            dma((2,)),
+            dma((4, 2)), dma((4, 2)),
+            dma((4, 4, 2)), dma((4, 4, 2)),
+            dma((4, 4, 2)), dma((4, 4, 2)),
+        ],
+        compiler_params=pltpu.CompilerParams(
+            collective_id=2, has_side_effects=True, vmem_limit_bytes=40 * 1024 * 1024
+        ),
+        cost_estimate=pl.CostEstimate(
+            flops=0, bytes_accessed=64 * (q_rows * width + o_rows * o_width), transcendentals=0
+        ),
+    )(qkv_shard, wo_shard)
+
+
+def scatter_kernel(
+    gq_ref, small_ref, go_ref, oq_ref, oo_ref,
+    stage, dq, do, sq, so, iq1, io1, tq, to, iq2, io2, xq, xo,
+    sd, rd, s1, r1, s2, r2, sx, rx, sf, rf,
+):
+    y, z, chip, core = place()
+    a, b, block = shape_of(y, z, core)
+    _, _, block_there = shape_of(y, z, 1 - core)
+    q_rows, width = oq_ref.shape
+    keep = gq_ref.shape[0] // 16
+    o_rows = oo_ref.shape[0]
+    q_half, o_half = width // 2, o_rows // 2
+    chips = xq.shape[0]
+    f32, bf = jnp.float32, jnp.bfloat16
+    partner = {"ctx": chip * 2 + 1 - core}
+
+    def first_peer(k):
+        return {"fsdp": block(lax.rem(a + k, 4), b)}
+
+    def second_peer(k):
+        return {"fsdp": block(a, lax.rem(b + k, 4))}
+
+    def chip_peer(k):
+        return {"ctx": lax.rem(chip + k, chips) * 2 + core}
+
+    def q_cols(half):
+        return pl.ds(pl.multiple_of(half * q_half, 128), q_half)
+
+    def o_lines(half):
+        return pl.ds(pl.multiple_of(half * o_half, 16), o_half)
+
+    for f in range(16):
+        stage[f] = jnp.concatenate(
+            [
+                gq_ref[pl.ds(f * keep, keep), :],
+                jnp.concatenate(
+                    [
+                        small_ref[f],
+                        jnp.zeros((q_rows - keep, width - small_ref.shape[2]), f32),
+                    ],
+                    axis=1,
+                ),
+            ],
+            axis=0,
+        ).astype(bf)
+
+    greet(
+        [first_peer(k) for k in (1, 2, 3)]
+        + [second_peer(k) for k in (1, 2, 3)]
+        + [chip_peer(k) for k in range(1, chips)]
+        + [partner]
+    )
+
+    def away(i, t):
+        k, j = lax.rem(i // 4 + 1, 4), lax.rem(i, 4)
+        line = lax.rem(b + k, 4)
+        f = block_there(line, j)
+        slot = line * 4 + j
+        if t == 0:
+            src, dst = stage.at[f, :, q_cols(1 - core)], dq.at[slot]
+        else:
+            src, dst = go_ref.at[f, o_lines(1 - core), :], do.at[slot]
+        return remote(src, dst, sd.at[i, t], rd.at[i, t], partner)
+
+    def home(i, t):
+        k, j = lax.rem(i // 4 + 1, 4), lax.rem(i, 4)
+        slot = lax.rem(a + k, 4) * 4 + j
+        dst = (dq, do)[t].at[slot]
+        return remote(dst, dst, sd.at[i, t], rd.at[i, t], partner)
+
+    def start_away(i, carry):
+        for t in (0, 1):
+            away(i, t).start()
+        return carry
+
+    lax.fori_loop(0, 16, start_away, 0)
+
+    def hop_one(k, t):
+        src, dst = ((sq, iq1), (so, io1))[t]
+        line = pl.ds(lax.rem(a + k, 4) * 4, 4)
+        return remote(
+            src.at[line], dst.at[3 - k], s1.at[k, t], r1.at[4 - k, t], first_peer(k)
+        )
+
+    for k in (1, 2, 3, 0):
+        def add(j, carry, k=k):
+            i = (k + 3) % 4 * 4 + j
+            line = lax.rem(a + k, 4)
+            slot = line * 4 + j
+            f = block(line, j)
+            home(i, 0).wait_recv()
+            sq[slot] = (stage[f, :, q_cols(core)].astype(f32) + dq[slot].astype(f32)).astype(bf)
+            home(i, 1).wait_recv()
+            so[slot] = (go_ref[f, o_lines(core), :].astype(f32) + do[slot].astype(f32)).astype(bf)
+            return carry
+
+        lax.fori_loop(0, 4, add, 0)
+        if k:
+            for t in (0, 1):
+                hop_one(k, t).start()
+
+    for k in (1, 3, 2):
+        for t in (0, 1):
+            hop_one(4 - k, t).wait_recv()
+
+    def hop_two(k, t):
+        src, dst = ((tq, iq2), (to, io2))[t]
+        return remote(
+            src.at[lax.rem(b + k, 4)], dst.at[3 - k], s2.at[k, t], r2.at[4 - k, t], second_peer(k)
+        )
+
+    for k in (2, 1, 3, 0):
+        j = lax.rem(b + k, 4)
+        slot = a * 4 + j
+        for t, (own, got, dst) in enumerate(((sq, iq1, tq), (so, io1, to))):
+            total = own[slot].astype(f32)
+            for m in range(3):
+                total = total + got[m, j].astype(f32)
+            dst[j] = total.astype(bf)
+            if k:
+                hop_two(k, t).start()
+
+    def hop_chip(k, t):
+        buf = (xq, xo)[t]
+        return remote(
+            buf.at[chip], buf.at[chip], sx.at[k, t], rx.at[chips - k, t], chip_peer(k)
+        )
+
+    for t, (own, got, dst) in enumerate(((tq, iq2, xq), (to, io2, xo))):
+        for k in (1, 3, 2):
+            hop_two(4 - k, t).wait_recv()
+        total = own[b].astype(f32)
+        for m in range(3):
+            total = total + got[m].astype(f32)
+        dst[chip] = total.astype(bf)
+        for k in range(1, chips):
+            hop_chip(k, t).start()
+
+    def last(t):
+        part = (oq_ref.at[:, q_cols(core)], oo_ref.at[o_lines(core), :])[t]
+        return remote(part, part, sf.at[t], rf.at[t], partner)
+
+    def last_home(t):
+        part = (oq_ref.at[:, q_cols(1 - core)], oo_ref.at[o_lines(1 - core), :])[t]
+        return remote(part, part, sf.at[t], rf.at[t], partner)
+
+    for t, buf in enumerate((xq, xo)):
+        for k in range(1, chips):
+            dst = buf.at[lax.rem(chip + k, chips)]
+            remote(dst, dst, sx.at[k, t], rx.at[k, t], partner).wait_recv()
+        total = buf[0].astype(f32)
+        for m in range(1, chips):
+            total = total + buf[m].astype(f32)
+        if t == 0:
+            oq_ref[:, q_cols(core)] = total
+        else:
+            oo_ref[o_lines(core), :] = total
+        last(t).start()
+
+    def end_away(i, carry):
+        for t in (0, 1):
+            away(i, t).wait_send()
+        return carry
+
+    lax.fori_loop(0, 16, end_away, 0)
+    for t in (0, 1):
+        for k in (1, 2, 3):
+            hop_one(k, t).wait_send()
+            hop_two(k, t).wait_send()
+        for k in range(1, chips):
+            hop_chip(k, t).wait_send()
+        last(t).wait_send()
+        last_home(t).wait_recv()
+
+
+def scatter_attention(gq, small, go):
+    f32, bf = jnp.float32, jnp.bfloat16
+    vm = pl.BlockSpec(memory_space=pltpu.VMEM)
+    dma = pltpu.SemaphoreType.DMA
+    keep, width = gq.shape[0] // 16, gq.shape[1]
+    q_rows = keep + small.shape[1]
+    o_rows, o_width = go.shape[1:]
+    q_half, o_half = width // 2, o_rows // 2
+    chips = lax.axis_size("ctx") // 2
+
+    def two(*lead):
+        return [pltpu.VMEM(lead + (q_rows, q_half), bf), pltpu.VMEM(lead + (o_half, o_width), bf)]
+
+    return pl.pallas_call(
+        scatter_kernel,
+        out_shape=(
+            jax.ShapeDtypeStruct((q_rows, width), f32),
+            jax.ShapeDtypeStruct((o_rows, o_width), f32),
+        ),
+        in_specs=[vm] * 3,
+        out_specs=(vm,) * 2,
+        scratch_shapes=[
+            pltpu.VMEM((16, q_rows, width), bf),
+            *two(16), *two(16), *two(3, 4), *two(4), *two(3), *two(chips),
+            dma((16, 2)), dma((16, 2)),
+            dma((4, 2)), dma((4, 2)),
+            dma((4, 2)), dma((4, 2)),
+            dma((4, 2)), dma((4, 2)),
+            dma((2,)), dma((2,)),
+        ],
+        compiler_params=pltpu.CompilerParams(
+            collective_id=3, has_side_effects=True, vmem_limit_bytes=48 * 1024 * 1024
+        ),
+        cost_estimate=pl.CostEstimate(
+            flops=0, bytes_accessed=64 * (q_rows * width + o_rows * o_width), transcendentals=0
+        ),
+    )(gq, small, go)
 
 
 def on_device(
@@ -308,26 +710,27 @@
     own_rows = gate_weight.shape[0]
     slice_rows = own_rows // ctx_size
     padded = -(-slice_rows // 16) * 16
-    gains_flat = jnp.concatenate([norm_gains.reshape(-1), qk_gains.reshape(-1)])
-    gains_got = lax.all_gather(gains_flat, "fsdp")
-    n_gain = norm_gains.size
+    n_gain, n_qk = norm_gains.size, qk_gains.size
+    extra = -(-n_gain // 128) * 128
+    gain_rows = jnp.zeros((8, qkv_weight.shape[1]), jnp.bfloat16)
+    gain_rows = gain_rows.at[0, :n_gain].set(norm_gains.reshape(-1))
+    gain_rows = gain_rows.at[1, :n_qk].set(qk_gains.reshape(-1))
+    qkv_full, out_full, gain_got = gather_attention(
+        jnp.concatenate([qkv_weight, gain_rows], axis=0), out_weight, qkv_weight.shape[0], extra
+    )
     gains_all = (
-        gains_got[:, :n_gain]
+        gain_got[:, 0, :n_gain]
         .reshape(-1, 4, norm_gains.shape[1])
         .transpose(1, 0, 2)
         .reshape(4, D)
-        .astype(jnp.float32)
     )
     qk_all = (
-        gains_got[:, n_gain:]
+        gain_got[:, 1, :n_qk]
         .reshape(-1, 2, qk_gains.shape[1])
         .transpose(1, 0, 2)
         .reshape(2, HD)
-        .astype(jnp.float32)
     )
     seg_all = lax.all_gather(segments[0], "ctx", axis=0, tiled=True)
-    qkv_full = lax.all_gather(qkv_weight, "fsdp", axis=0, tiled=True)
-    out_full = lax.all_gather(out_weight, "fsdp", axis=0, tiled=True)
 
     def my_slice(weight):
         part = lax.dynamic_index_in_dim(
@@ -335,9 +738,10 @@
         )
         return jnp.pad(part, ((0, padded - slice_rows), (0, 0)))
 
-    gate_full = lax.all_gather(my_slice(gate_weight), "fsdp", axis=0, tiled=True)
-    up_full = lax.all_gather(my_slice(up_weight), "fsdp", axis=0, tiled=True)
-    down_full = lax.all_gather(my_slice(down_weight), "fsdp", axis=0, tiled=True)
+    ffn_shard = jnp.concatenate(
+        [my_slice(gate_weight), my_slice(up_weight), my_slice(down_weight)], axis=0
+    )
+    ffn_full = lax.all_gather(ffn_shard, "fsdp")
 
     offset = ctx_index * local_len
     positions = offset + jnp.arange(local_len, dtype=jnp.int32)
@@ -389,9 +793,7 @@
         mid_stream,
         cotangent.reshape(local_len, D),
         gains_all[3:4],
-        gate_full,
-        up_full,
-        down_full,
+        ffn_full,
     )
     output = output.reshape(1, local_len, D)
     grad_gain_three = grad_gain_three[0]
@@ -447,26 +849,25 @@
     grad_tokens = (grad_mid + grad_input_part).reshape(1, local_len, D)
     gain_grads = jnp.stack([grad_gain_zero, grad_gain_one, grad_gain_two, grad_gain_three])
     qk_grads = jnp.stack([grad_q_gain, grad_k_gain])
-    fsdp_size = lax.axis_size("fsdp")
+    owners = lax.axis_size("fsdp")
+
+    def by_owner(grads):
+        lines = grads.shape[0]
+        flat = grads.reshape(lines, owners, -1).transpose(1, 0, 2).reshape(owners, 1, -1)
+        return jnp.pad(flat, ((0, 0), (0, 0), (0, extra - flat.shape[2])))
+
     small = jnp.concatenate(
-        [
-            gain_grads.reshape(4, fsdp_size, -1).transpose(1, 0, 2).reshape(fsdp_size, -1),
-            qk_grads.reshape(2, fsdp_size, -1).transpose(1, 0, 2).reshape(fsdp_size, -1),
-        ],
+        [by_owner(gain_grads), by_owner(qk_grads), jnp.zeros((owners, 6, extra), jnp.float32)],
         axis=1,
     )
-    small_total = lax.psum(small, ("fsdp", "ctx"))
-    small_own = lax.dynamic_index_in_dim(small_total, lax.axis_index("fsdp"), 0, False)
-    total_gains = small_own[:n_gain].reshape(norm_gains.shape)
-    total_qk = small_own[n_gain:].reshape(qk_gains.shape)
-    share_qkv = lax.psum_scatter(
-        grad_qkv_weight.astype(jnp.bfloat16), "fsdp", scatter_dimension=0, tiled=True
-    )
-    share_out = lax.psum_scatter(
-        grad_out_weight.astype(jnp.bfloat16), "fsdp", scatter_dimension=0, tiled=True
-    )
-    total_qkv = lax.psum(share_qkv, "ctx").astype(jnp.float32)
-    total_out = lax.psum(share_out, "ctx").astype(jnp.float32)
+    own_qkv, total_out = scatter_attention(
+        grad_qkv_weight,
+        small,
+        grad_out_weight.astype(jnp.bfloat16).reshape(owners, out_weight.shape[0], D),
+    )
+    total_qkv = own_qkv[: qkv_weight.shape[0]]
+    total_gains = own_qkv[qkv_weight.shape[0], :n_gain].reshape(norm_gains.shape)
+    total_qk = own_qkv[qkv_weight.shape[0] + 1, :n_qk].reshape(qk_gains.shape)
     return (
         output,
         grad_tokens,

time: 688 us -> 385 us (0.56)
  waiting for transfers between devices: 359 us -> 77.4 us
  blocking collectives: 141 us -> 8.91 us
  Pallas kernels: 83.1 us -> 173 us
  local copies, waits for them, and re-layouts: 29.3 us -> 38.3 us
    all_gather x5 -> x1, waiting for transfers between devices: 133 us -> 0.01 us  [on_device(): ffn_full = lax.all_gather(ffn_shard, 'fsdp')]
    pallas_call x0 -> x2, Pallas kernels: none -> 91 us  [the longest x1 53 us: scatter_attention(): pl.pallas_call(scatter_kernel, out_shape=(jax.ShapeDtypeStruct((q_rows, w...]
    unnamed x11 -> x3, waiting for transfers between devices: 80.6 us -> 0.05 us
    psum x1 -> x0, blocking collectives: 65.1 us -> none  [on_device(): small_total = lax.psum(small, ('fsdp', 'ctx'))]
    unnamed x1 -> x0, blocking collectives: 52 us -> none
    reduce_scatter x1 -> x0, waiting for transfers between devices: 31.5 us -> none  [on_device(): lax.psum_scatter(grad_out_weight.astype(jnp.bfloat16), 'fsdp', scatter_di...]
    all_gather x1, waiting for transfers between devices: 17.4 us -> 0.01 us  [on_device(): lax.all_gather(mlp_share[:slice_rows], 'ctx', axis=0, tiled=True)]
    all_gather x1, blocking collectives: 24 us -> 8.91 us  [on_device(): seg_all = lax.all_gather(segments[0], 'ctx', axis=0, tiled=True)]
  transfers between devices with their start and end apart: 18 -> 11, of which waited for: 12 -> 3; matrix products, arithmetic and copies ran while one was open for 7% -> 15% of each run, Pallas kernels for 0% -> 24%
where the time goes in v3:
time: 385 us; the launch traced here: 380 us
  Pallas kernels  173 us (45%)
  waiting for transfers between devices  77.4 us (20%)
  local copies, waits for them, and re-layouts  38.3 us (10%)
  matrix products  24.2 us (6%)
  other arithmetic  23.2 us (6%)
  starting transfers between devices  19.7 us (5%)
  between operations  15 us (4%)
  blocking collectives  8.91 us (2%)
    pallas_call x1, Pallas kernels, ffn(): pl.pallas_call(ffn_kernel, out_shape=(jax.ShapeDtypeStruct((rows, D), bf)...  81.9 us
    reduce_scatter x1, waiting for transfers between devices, on_device(): lax.psum_scatter(mlp_grads, 'fsdp', scatter_dimension=0, tiled=True)  73.3 us
    pallas_call x1, Pallas kernels, scatter_attention(): pl.pallas_call(scatter_kernel, out_shape=(jax.ShapeDtypeStruct((q_rows, w...  53 us
    pallas_call x1, Pallas kernels, gather_attention(): pl.pallas_call(gather_kernel, out_shape=(jax.ShapeDtypeStruct((16 * keep,...  38 us
    ppermute x8, starting transfers between devices, from_behind(): return lax.ppermute(array, axis, pairs)  19.6 us
    unnamed x133, local copies, waits for them, and re-layouts  13.6 us
    all_gather x1, blocking collectives, on_device(): seg_all = lax.all_gather(segments[0], 'ctx', axis=0, tiled=True)  8.91 us
  transfers between devices with their start and end apart: 11, of which 3 were waited for; matrix products, arithmetic and copies ran while one was open for 15% of the time, Pallas kernels for 24%

profile of v3, /device:TPU:73, one launch (start us, length us, event | category | flops | bytes accessed | tf_op | source)
XLA Modules:
  0.0 379.7 jit_solution(15531140191836460955)
XLA Ops:
  11.9 38.0 %shard_map.169 = (bf16[1152,1536]{1,0:T(8,128)(2,1)S(1)}, bf16[1024,1152]{1,0:T(8,128)(2,1)S(1)}, f32[16,8,384]{2,1,0:T(8,128)S(1)}) custom-call(bf16[80,1536]{1,0:T(8,128)(2,1)S(1)} %pad_maximum_fusion.4.qkv_ref, bf16[64,1152]{1,0:T(8,128)(2,1)S(1)} %copy-done.1), custom_call_target="tpu_custom_call" | custom-call | bytes 12582912 | tf_op jit(solution)/shard_map/pallas_call | solution.py:455
  50.0 1.9 copy-done
  53.1 2.7 fusion.50
  57.9 5.3 %collective-permute-start = (bf16[128,512]{1,0:T(8,128)(2,1)}, bf16[128,512]{1,0:T(8,128)(2,1)}, u32[]{:S(2)}, u32[]{:S(2)}) collective-permute-start(bf16[128,512]{1,0:T(8,128)(2,1)} %pad_maximum_fusion.9), channel_id=1, source_target_pairs={{0,4},{1,5},{2,6},{3,7},{8,12},{9,13},{10,14},{11,15},{16,20},{17,... | collective-permute-start | bytes 393224 | tf_op jit(solution)/shard_map/ppermute | solution.py:26
  63.2 2.0 collective-permute-start.1
  65.2 2.8 collective-permute-start.2
  68.0 1.9 collective-permute-start.3
  72.2 8.9 %all-gather = s32[1,1024]{1,0:T(1,128)S(1)} all-gather(s32[1,128]{1,0:T(1,128)} %param.22), channel_id=2, replica_groups=mesh['fsdp'=16,'ctx'=8] {'ctx'}, dimensions={1}, use_global_device_ids=true | all-gather | bytes 4608 | tf_op jit(solution)/shard_map/all_gather | solution.py:733
  87.3 2.6 fusion.77
  89.9 2.7 convolution_convert_fusion.2
  96.1 81.9 %shard_map.170 = (bf16[128,1152]{1,0:T(8,128)(2,1)}, f32[128,1152]{1,0:T(8,128)}, f32[1,1152]{1,0:T(1,128)}, bf16[1024,1152]{1,0:T(8,128)(2,1)}, bf16[1024,1152]{1,0:T(8,128)(2,1)}, /*index=5*/bf16[1024,1152]{1,0:T(8,128)(2,1)}) custom-call(bf16[128,1152]{1,0:T(8,128)(2,1)} %multiply_convert_fusion.1.normed_ref, f32[128,1152]{1,0:T(8,128)} %copy-done.2, ...), custom_call_target="tpu_custom_call" | custom-call | flops 21743271936 | bytes 16515072 | tf_op jit(solution)/shard_map/pallas_call | solution.py:256
  178.0 6.3 %pad_maximum_fusion = bf16[1024,3456]{1,0:T(8,128)(2,1)} fusion(bf16[1024,1152]{1,0:T(8,128)(2,1)} %get-tuple-element.54, bf16[1024,1152]{1,0:T(8,128)(2,1)} %get-tuple-element.53, bf16[1024,1152]{1,0:T(8,128)(2,1)} %get-tuple-element.52), kind=kLoop, calls=%fused_computation.1 | loop fusion | flops 21233664 | bytes 14155776 | tf_op jit(solution)/shard_map/concatenate | solution.py:800
  185.1 2.0 multiply_reduce_fusion.1
  187.1 2.0 multiply_reduce_fusion.2
  193.9 73.3 %reduce-scatter.2.cloned.1.call-done = bf16[64,3456]{1,0:T(8,128)(2,1)} async-done(((bf16[1024,3456]{1,0:T(8,128)(2,1)}), bf16[64,3456]{1,0:T(8,128)(2,1)}) %reduce-scatter.2.cloned.1.call-update) | async-done | bytes 442384 | tf_op jit(solution)/shard_map/reduce_scatter | solution.py:801
  269.4 1.9 convolution_bitcast_fusion.1
  272.4 3.7 collective-permute-start.4
  288.3 3.3 collective-permute-done.7
  295.6 4.3 %fusion.15 = (f32[1152]{0:T(1024)S(1)}, f32[128]{0:T(128)S(1)}, f32[128,1152]{1,0:T(8,128)}) fusion(bf16[1,128,1152]{2,1,0:T(8,128)(2,1)S(1)} %copy-done.6, f32[128]{0:T(128)S(1)} %copy-done.47, f32[1152]{0:T(1024)S(1)} %mul.435, bf16[1152,1536]{1,0:T(8,128)(2,1)} %copy-done, bf16[128,256]{0,1:T(8,128)(2,1)S(1)} %copy.121, bf16[128,256]{0,1:T(8,128)(2,1)S(1)} %copy.120, ...), kind=kOutput, calls=%fused_computation.43 | convolution fusion | flops 455195392 | bytes 4827136 | tf_op jit(solution)/shard_map/dot_general | solution.py:842
  300.5 4.1 %fusion.38.gq_ref = f32[1152,1536]{1,0:T(8,128)} fusion(bf16[128,256]{0,1:T(8,128)(2,1)S(1)} %copy.121, bf16[128,256]{0,1:T(8,128)(2,1)S(1)} %copy.120, bf16[128,1024]{0,1:T(8,128)(2,1)S(1)} %bitcast.127, bf16[1,128,1152]{2,1,0:T(8,128)(2,1)S(1)} %copy-done.6, f32[1152]{0:T(1024)S(1)} %mul.435, f32[128]{0:T(128)S(1)} %copy-done.47), kind=kOutput, calls=%fused_computation.96 | convolution fusion | flops 454754304 | bytes 7771136 | tf_op jit(solution)/shard_map/dot_general | solution.py:845
  304.5 53.0 %shard_map.171 = (f32[80,1536]{1,0:T(8,128)S(1)}, f32[64,1152]{1,0:T(8,128)S(1)}) custom-call(f32[1152,1536]{1,0:T(8,128)} %fusion.38.gq_ref, f32[16,8,384]{2,1,0:T(8,128)S(1)} %fusion.36.small_ref, bf16[16,64,1152]{2,1,0:T(8,128)(2,1)S(1)} %bitcast.122), custom_call_target="tpu_custom_call" | custom-call | bytes 12582912 | tf_op jit(solution)/shard_map/pallas_call | solution.py:668
  359.7 2.1 fusion.19
  361.9 4.3 %reshape.407 = f32[432,3456]{1,0:T(8,128)} reshape(bf16[8,54,3456]{2,1,0:T(8,128)(2,1)} %all-gather.8.cloned.1.call-done) | data formatting | bytes 8957952 | tf_op jit(solution)/shard_map/convert_element_type | solution.py:802
  366.2 5.5 %fusion.74 = (f32[432,1152]{1,0:T(8,128)}, f32[432,1152]{1,0:T(8,128)}, f32[432,1152]{1,0:T(8,128)}) fusion(f32[432,3456]{1,0:T(8,128)} %reshape.407), kind=kLoop, calls=%fused_computation.169 | loop fusion | bytes 11943936 | tf_op jit(solution)/shard_map/slice | solution.py:880
  (246 shorter events, 48.0 us)
Async XLA Ops:
  7.2 89.0 %all-gather.6.cloned.1.call-start = ((), (), s32[]{:S(2)}) async-start(), calls=%async_computation.2 | async-start | bytes 7520256 | tf_op jit(solution)/shard_map/all_gather | solution.py:744
  10.6 42.3 %copy-start.4 = (bf16[1,128,1152]{2,1,0:T(8,128)(2,1)S(1)}, bf16[1,128,1152]{2,1,0:T(8,128)(2,1)}, u32[]{:S(2)}) copy-start(bf16[1,128,1152]{2,1,0:T(8,128)(2,1)} %param.14) | copy-start | bytes 884740
  11.5 255.8 %reduce-scatter.2.cloned.1.call-start = ((), (), s32[]{:S(2)}) async-start(), calls=%async_computation.1 | async-start | bytes 7520256 | tf_op jit(solution)/shard_map/reduce_scatter | solution.py:801
  55.9 14.0 %copy-start.9 = (f32[128,1536]{1,0:T(8,128)}, f32[128,1536]{1,0:T(8,128)S(1)}, u32[]{:S(2)}) copy-start(f32[128,1536]{1,0:T(8,128)S(1)} %fusion.50) | copy-start | bytes 2359300
  55.9 14.1 %copy-start.22 = (bf16[128,256]{1,0:T(8,128)(2,1)}, bf16[128,256]{1,0:T(8,128)(2,1)S(1)}, u32[]{:S(2)}) copy-start(bf16[128,256]{1,0:T(8,128)(2,1)S(1)} %slice.257) | copy-start | bytes 196612
  55.9 14.1 %copy-start.51 = (f32[128]{0:T(128)}, f32[128]{0:T(128)S(1)}, u32[]{:S(2)}) copy-start(f32[128]{0:T(128)S(1)} %multiply_power_fusion) | copy-start | bytes 1540
  55.9 14.0 %copy-start.53 = (f32[128]{0:T(128)}, f32[128]{0:T(128)S(1)}, u32[]{:S(2)}) copy-start(f32[128]{0:T(128)S(1)} %fusion.72) | copy-start | bytes 1540
  56.1 13.9 %copy-start.59 = (f32[128]{0:T(128)}, f32[128]{0:T(128)S(1)}, u32[]{:S(2)}) copy-start(f32[128]{0:T(128)S(1)} %multiply_reduce_fusion.11) | copy-start | bytes 1540
  57.2 12.8 %copy-start.31 = (bf16[128,128]{1,0:T(8,128)(2,1)}, bf16[128,128]{1,0:T(8,128)(2,1)S(1)}, u32[]{:S(2)}) copy-start(bf16[128,128]{1,0:T(8,128)(2,1)S(1)} %get-tuple-element.91) | copy-start | bytes 98308
  57.2 12.8 %copy-start.33 = (bf16[128,128]{1,0:T(8,128)(2,1)}, bf16[128,128]{1,0:T(8,128)(2,1)S(1)}, u32[]{:S(2)}) copy-start(bf16[128,128]{1,0:T(8,128)(2,1)S(1)} %get-tuple-element.92) | copy-start | bytes 98308
  57.2 24.2 %copy-start.18 = (f32[128,128]{1,0:T(8,128)}, f32[128,128]{1,0:T(8,128)S(1)}, u32[]{:S(2)}) copy-start(f32[128,128]{1,0:T(8,128)S(1)} %get-tuple-element.89) | copy-start | bytes 196612
  57.2 24.2 %copy-start.20 = (f32[128,128]{1,0:T(8,128)}, f32[128,128]{1,0:T(8,128)S(1)}, u32[]{:S(2)}) copy-start(f32[128,128]{1,0:T(8,128)S(1)} %get-tuple-element.90) | copy-start | bytes 196612
  57.9 24.8 %collective-permute-start = (bf16[128,512]{1,0:T(8,128)(2,1)}, bf16[128,512]{1,0:T(8,128)(2,1)}, u32[]{:S(2)}, u32[]{:S(2)}) collective-permute-start(bf16[128,512]{1,0:T(8,128)(2,1)} %pad_maximum_fusion.9), channel_id=1, source_target_pairs={{0,4},{1,5},{2,6},{3,7},{8,12},{9,13},{10,14},{11,15},{16,20},{17,... | collective-permute-start | bytes 393224 | tf_op jit(solution)/shard_map/ppermute | solution.py:26
  63.2 20.4 %collective-permute-start.1 = (bf16[128,512]{1,0:T(8,128)(2,1)}, bf16[128,512]{1,0:T(8,128)(2,1)}, u32[]{:S(2)}, u32[]{:S(2)}) collective-permute-start(bf16[128,512]{1,0:T(8,128)(2,1)} %pad_maximum_fusion.9), channel_id=1, source_target_pairs={{0,3},{1,4},{2,5},{3,6},{4,7},{8,11},{9,12},{10,13},{11,14},{12,15... | collective-permute-start | bytes 393224 | tf_op jit(solution)/shard_map/ppermute | solution.py:26
  65.2 19.4 %collective-permute-start.2 = (bf16[128,512]{1,0:T(8,128)(2,1)}, bf16[128,512]{1,0:T(8,128)(2,1)}, u32[]{:S(2)}, u32[]{:S(2)}) collective-permute-start(bf16[128,512]{1,0:T(8,128)(2,1)} %pad_maximum_fusion.9), channel_id=1, source_target_pairs={{0,2},{1,3},{2,4},{3,5},{4,6},{5,7},{8,10},{9,11},{10,12},{11,13},... | collective-permute-start | bytes 393224 | tf_op jit(solution)/shard_map/ppermute | solution.py:26
  68.0 17.5 %collective-permute-start.3 = (bf16[128,512]{1,0:T(8,128)(2,1)}, bf16[128,512]{1,0:T(8,128)(2,1)}, u32[]{:S(2)}, u32[]{:S(2)}) collective-permute-start(bf16[128,512]{1,0:T(8,128)(2,1)} %pad_maximum_fusion.9), channel_id=1, source_target_pairs={{0,1},{1,2},{2,3},{3,4},{4,5},{5,6},{6,7},{8,9},{9,10},{10,11},{11... | collective-permute-start | bytes 393224 | tf_op jit(solution)/shard_map/ppermute | solution.py:26
  184.3 177.6 %all-gather.8.cloned.1.call-start = ((), (), s32[]{:S(2)}) async-start(), calls=%async_computation.3 | async-start | bytes 3483648 | tf_op jit(solution)/shard_map/all_gather | solution.py:802
  193.7 75.4 %copy-start.25 = (bf16[128,4,128]{2,0,1:T(8,128)(2,1)S(1)}, bf16[128,4,128]{2,0,1:T(8,128)(2,1)}, u32[]{:S(2)}) copy-start(bf16[128,4,128]{2,0,1:T(8,128)(2,1)} %copy-done.24) | copy-start | bytes 393220
  193.7 75.4 %copy-start.27 = (bf16[128,4,128]{2,0,1:T(8,128)(2,1)S(1)}, bf16[128,4,128]{2,0,1:T(8,128)(2,1)}, u32[]{:S(2)}) copy-start(bf16[128,4,128]{2,0,1:T(8,128)(2,1)} %copy-done.26) | copy-start | bytes 393220
  272.4 15.2 %collective-permute-start.4 = (bf16[128,512]{1,0:T(8,128)(2,1)}, bf16[128,512]{1,0:T(8,128)(2,1)}, u32[]{:S(2)}, u32[]{:S(2)}) collective-permute-start(bf16[128,512]{1,0:T(8,128)(2,1)} %get-tuple-element.75), channel_id=1, source_target_pairs={{1,0},{2,1},{3,2},{4,3},{5,4},{6,5},{7,6},{9,8},{10,9},{11,10},{12... | collective-permute-start | bytes 393224 | tf_op jit(solution)/shard_map/ppermute | solution.py:26
  276.1 11.5 %collective-permute-start.5 = (bf16[128,512]{1,0:T(8,128)(2,1)}, bf16[128,512]{1,0:T(8,128)(2,1)}, u32[]{:S(2)}, u32[]{:S(2)}) collective-permute-start(bf16[128,512]{1,0:T(8,128)(2,1)} %get-tuple-element.78), channel_id=1, source_target_pairs={{2,0},{3,1},{4,2},{5,3},{6,4},{7,5},{10,8},{11,9},{12,10},{13,11},... | collective-permute-start | bytes 393224 | tf_op jit(solution)/shard_map/ppermute | solution.py:26
  277.4 10.9 %collective-permute-start.6 = (bf16[128,512]{1,0:T(8,128)(2,1)}, bf16[128,512]{1,0:T(8,128)(2,1)}, u32[]{:S(2)}, u32[]{:S(2)}) collective-permute-start(bf16[128,512]{1,0:T(8,128)(2,1)} %get-tuple-element.77), channel_id=1, source_target_pairs={{3,0},{4,1},{5,2},{6,3},{7,4},{11,8},{12,9},{13,10},{14,11},{15,12... | collective-permute-start | bytes 393224 | tf_op jit(solution)/shard_map/ppermute | solution.py:26
  278.7 12.9 %collective-permute-start.7 = (bf16[128,512]{1,0:T(8,128)(2,1)}, bf16[128,512]{1,0:T(8,128)(2,1)}, u32[]{:S(2)}, u32[]{:S(2)}) collective-permute-start(bf16[128,512]{1,0:T(8,128)(2,1)} %get-tuple-element.76), channel_id=1, source_target_pairs={{4,0},{5,1},{6,2},{7,3},{12,8},{13,9},{14,10},{15,11},{20,16},{21,... | collective-permute-start | bytes 393224 | tf_op jit(solution)/shard_map/ppermute | solution.py:26
  304.5 55.2 %copy-start.58 = (f32[128]{0:T(128)S(1)}, f32[128]{0:T(128)}, u32[]{:S(2)}) copy-start(f32[128]{0:T(128)} %copy-done.57) | copy-start | bytes 1540
  (50 other events, 251.7 us)
Sparse Core Ops, SparseCore 0:
  11.6 70.2 all-gather.5
  184.4 82.7 reduce-scatter.1
  269.2 34.0 all-gather.7

commit v4 on v3

--- a/solution.py
+++ b/solution.py
@@ -73,7 +73,7 @@
 
 def ffn_kernel(
     normed_ref, mid_ref, cot_ref, gain_ref, w_hbm,
-    out_ref, gn_ref, ggain_ref, dg_hbm, du_hbm, dd_hbm,
+    out_ref, gn_ref, ggain_ref, gff_hbm,
     wg, wu, wd, seq, gseq, act_a, act_b, hid, dgate, dup, part,
     d2d_snd, d2d_in, ici_snd, ici_in, dw,
     w_sem, o_sem, ag_s, ag_r, rd_s, rd_r, ri_s, ri_r,
@@ -223,24 +223,22 @@
         part[...] = dot32(dgate[pair(k), :], wg[...], NN) + dot32(dup[pair(k), :], wu[...], NN)
 
     sums = phase(gseq, 1, backward)
-    stores = []
-    for i, (left, right, dst) in enumerate(
-        ((hid, gseq, dd_hbm), (dgate, seq, dg_hbm), (dup, seq, du_hbm))
-    ):
+    for i, (left, right) in enumerate(((dgate, seq), (dup, seq), (hid, gseq))):
         def one(t, carry, i=i, left=left, right=right):
             cols = pl.ds(pl.multiple_of(t * tile, tile), tile)
-            dw[i, cols, :] = dot32(left[:, cols], right[...], TN).astype(jnp.bfloat16)
+            group = tile // share
+            dw[pl.ds(t * group, group), pl.ds(i * share, share), :] = (
+                dot32(left[:, cols], right[...], TN).reshape(group, share, -1).astype(jnp.bfloat16)
+            )
             return carry
 
         lax.fori_loop(0, units // tile, one, 0)
-        store = pltpu.make_async_copy(dw.at[i], dst, o_sem.at[i])
-        store.start()
-        stores.append(store)
+    store = pltpu.make_async_copy(dw, gff_hbm, o_sem)
+    store.start()
     gn_ref[...] = collect(1, sums)
     for copy in started:
         copy.wait_send()
-    for store in stores:
-        store.wait()
+    store.wait()
 
 
 def ffn(normed_two, mid, cot, gain, weights):
@@ -252,17 +250,16 @@
     vm = pl.BlockSpec(memory_space=pltpu.VMEM)
     hbm = pl.BlockSpec(memory_space=pl.ANY)
     dma = pltpu.SemaphoreType.DMA
-    weight = jax.ShapeDtypeStruct((units, D), bf)
     return pl.pallas_call(
         ffn_kernel,
         out_shape=(
             jax.ShapeDtypeStruct((rows, D), bf),
             jax.ShapeDtypeStruct((rows, D), f32),
             jax.ShapeDtypeStruct((1, D), f32),
-            weight, weight, weight,
+            jax.ShapeDtypeStruct(weights.shape, bf),
         ),
         in_specs=[vm] * 4 + [hbm],
-        out_specs=(vm, vm, vm, hbm, hbm, hbm),
+        out_specs=(vm, vm, vm, hbm),
         scratch_shapes=[
             pltpu.VMEM((units, D), bf),
             pltpu.VMEM((units, D), bf),
@@ -279,8 +276,8 @@
             pltpu.VMEM((2, 4, rows, D), bf),
             pltpu.VMEM((2, 3, rows, D), bf),
             pltpu.VMEM((2, 3, rows, D), bf),
-            pltpu.VMEM((3, units, D), bf),
-            dma((3, owners)), dma((3,)),
+            pltpu.VMEM(weights.shape, bf),
+            dma((3, owners)), dma,
             dma((2, 8)), dma((2, 8)),
             dma((2, 4)), dma((2, 4)),
             dma((2, 4)), dma((2, 4)),
@@ -477,19 +474,49 @@
     )(qkv_shard, wo_shard)
 
 
-def scatter_kernel(
-    gq_ref, small_ref, go_ref, oq_ref, oo_ref,
-    stage, dq, do, sq, so, iq1, io1, tq, to, iq2, io2, xq, xo,
+def rms_back(values, grad, gain):
+    r = lax.rsqrt(jnp.mean(values * values, axis=-1, keepdims=True) + EPS)
+    n = values * r
+    dyg = grad * gain
+    return (
+        r * (dyg - n * jnp.mean(dyg * n, axis=-1, keepdims=True)),
+        jnp.sum(grad * n, axis=0, keepdims=True),
+    )
+
+
+def stack_heads(values):
+    return jnp.concatenate([values[:, h * HD : (h + 1) * HD] for h in range(NH)], axis=0)
+
+
+def turn_back(grad, cos_table, sin_table):
+    left, right = grad[:, : HD // 2], grad[:, HD // 2 :]
+    return jnp.concatenate(
+        [left * cos_table + right * sin_table, right * cos_table - left * sin_table], axis=1
+    )
+
+
+def back_kernel(
+    gff, gn_ref, mid_ref, attn_ref, cot_ref, tok_ref, gains_ref, qk_ref, proj_ref, q_ref,
+    pair_ref, att_ref, normed_ref, qkv_ref, wo_ref, cos_ref, sin_ref, bias_ref, g3_ref,
+    gt_ref, oq_ref, oo_ref, og_ref, ou_ref, od_ref,
+    own_ff, in1_ff, t_ff, in2_ff, all_ff, kv_snd, kv_in, gmid, gpair, gproj, tail,
+    stage, go, dq, do, sq, so, iq1, io1, tq, to, iq2, io2, xq, xo,
+    l_sem, s1f, r1f, s2f, r2f, sag, rag, skv, rkv,
     sd, rd, s1, r1, s2, r2, sx, rx, sf, rf,
 ):
     y, z, chip, core = place()
     a, b, block = shape_of(y, z, core)
     _, _, block_there = shape_of(y, z, 1 - core)
+    me = chip * 2 + core
+    rows = gn_ref.shape[0]
     q_rows, width = oq_ref.shape
-    keep = gq_ref.shape[0] // 16
+    keep = normed_ref.shape[1] // 16
     o_rows = oo_ref.shape[0]
     q_half, o_half = width // 2, o_rows // 2
     chips = xq.shape[0]
+    members = 2 * chips
+    reach = kv_in.shape[0]
+    scale = HD ** (-0.5)
     f32, bf = jnp.float32, jnp.bfloat16
     partner = {"ctx": chip * 2 + 1 - core}
 
@@ -502,33 +529,52 @@
     def chip_peer(k):
         return {"ctx": lax.rem(chip + k, chips) * 2 + core}
 
+    def member(k):
+        return {"ctx": lax.rem(me + k, members)}
+
     def q_cols(half):
         return pl.ds(pl.multiple_of(half * q_half, 128), q_half)
 
     def o_lines(half):
         return pl.ds(pl.multiple_of(half * o_half, 16), o_half)
 
-    for f in range(16):
-        stage[f] = jnp.concatenate(
-            [
-                gq_ref[pl.ds(f * keep, keep), :],
-                jnp.concatenate(
-                    [
-                        small_ref[f],
-                        jnp.zeros((q_rows - keep, width - small_ref.shape[2]), f32),
-                    ],
-                    axis=1,
-                ),
-            ],
-            axis=0,
-        ).astype(bf)
-
+    own_loads = [
+        pltpu.make_async_copy(gff.at[block(a, j)], own_ff.at[j], l_sem.at[j]) for j in range(4)
+    ]
+    for copy in own_loads:
+        copy.start()
     greet(
         [first_peer(k) for k in (1, 2, 3)]
         + [second_peer(k) for k in (1, 2, 3)]
-        + [chip_peer(k) for k in range(1, chips)]
-        + [partner]
-    )
+        + [member(k) for k in range(1, members)]
+    )
+
+    def ff_one(k, j):
+        return remote(
+            gff.at[block(lax.rem(a + k, 4), j)], in1_ff.at[3 - k, j],
+            s1f.at[k, j], r1f.at[4 - k, j], first_peer(k),
+        )
+
+    for i in (2, 1, 3, 0):
+        for k in (1, 3, 2):
+            ff_one(k, lax.rem(b + i, 4)).start()
+
+    grad_final = cot_ref[...].astype(f32)
+    part, gain_two = rms_back(mid_ref[...], gn_ref[...], gains_ref[2:3, :])
+    grad_mid = grad_final + part
+    gmid[...] = grad_mid
+    grad_attn, gain_one = rms_back(attn_ref[...], grad_mid, gains_ref[1:2, :])
+    grad_attn_low = grad_attn.astype(bf)
+    grad_attended = dot32(grad_attn_low, wo_ref[...], NT).astype(bf)
+
+    def out_tile(t, carry):
+        cols = pl.ds(pl.multiple_of(t * 256, 256), 256)
+        go[pl.ds(t * 4, 4)] = (
+            dot32(att_ref[:, cols], grad_attn_low, TN).reshape(4, 64, D).astype(bf)
+        )
+        return carry
+
+    lax.fori_loop(0, NH * HD // 256, out_tile, 0)
 
     def away(i, t):
         k, j = lax.rem(i // 4 + 1, 4), lax.rem(i, 4)
@@ -538,7 +584,7 @@
         if t == 0:
             src, dst = stage.at[f, :, q_cols(1 - core)], dq.at[slot]
         else:
-            src, dst = go_ref.at[f, o_lines(1 - core), :], do.at[slot]
+            src, dst = go.at[f, o_lines(1 - core), :], do.at[slot]
         return remote(src, dst, sd.at[i, t], rd.at[i, t], partner)
 
     def home(i, t):
@@ -547,12 +593,46 @@
         dst = (dq, do)[t].at[slot]
         return remote(dst, dst, sd.at[i, t], rd.at[i, t], partner)
 
-    def start_away(i, carry):
-        for t in (0, 1):
+    def start_away(t):
+        def one(i, carry):
             away(i, t).start()
-        return carry
-
-    lax.fori_loop(0, 16, start_away, 0)
+            return carry
+
+        lax.fori_loop(0, 16, one, 0)
+
+    start_away(1)
+
+    keys, vals = pair_ref[:, :HD], pair_ref[:, HD:]
+    queries = stack_heads(q_ref[...])
+    grad_heads = stack_heads(grad_attended)
+    scores = dot32(queries, keys, NT) * scale + jnp.concatenate([bias_ref[...]] * NH, axis=0)
+    expo = jnp.exp(scores - jnp.max(scores, axis=-1, keepdims=True))
+    probs = expo / jnp.sum(expo, axis=-1, keepdims=True)
+    grad_probs = dot32(grad_heads, vals, NT)
+    row_total = jnp.sum(probs * grad_probs, axis=-1, keepdims=True)
+    grad_scores = (probs * (grad_probs - row_total)).astype(bf)
+    gpair[:, HD:] = dot32(probs.astype(bf), grad_heads, TN)
+    gpair[:, :HD] = dot32(grad_scores, queries, TN) * scale
+
+    def kv_send(d):
+        return remote(
+            kv_snd.at[d - 1], kv_in.at[d - 1], skv.at[d - 1], rkv.at[d - 1], member(members - d)
+        )
+
+    for d in range(1, reach + 1):
+        kv_snd[d - 1] = gpair[pl.ds((reach - d) * rows, rows), :].astype(bf)
+        kv_send(d).start()
+
+    cos_all = jnp.concatenate([cos_ref[...]] * NH, axis=0)
+    sin_all = jnp.concatenate([sin_ref[...]] * NH, axis=0)
+    grad_queries = dot32(grad_scores, keys, NN) * scale
+    grad_q, qk_gain_q = rms_back(
+        stack_heads(proj_ref[:, : NH * HD]),
+        turn_back(grad_queries, cos_all, sin_all),
+        qk_ref[0:1, :],
+    )
+    for h in range(NH):
+        gproj[:, h * HD : (h + 1) * HD] = grad_q[h * rows : (h + 1) * rows].astype(bf)
 
     def hop_one(k, t):
         src, dst = ((sq, iq1), (so, io1))[t]
@@ -561,26 +641,82 @@
             src.at[line], dst.at[3 - k], s1.at[k, t], r1.at[4 - k, t], first_peer(k)
         )
 
-    for k in (1, 2, 3, 0):
-        def add(j, carry, k=k):
-            i = (k + 3) % 4 * 4 + j
-            line = lax.rem(a + k, 4)
-            slot = line * 4 + j
-            f = block(line, j)
-            home(i, 0).wait_recv()
-            sq[slot] = (stage[f, :, q_cols(core)].astype(f32) + dq[slot].astype(f32)).astype(bf)
-            home(i, 1).wait_recv()
-            so[slot] = (go_ref[f, o_lines(core), :].astype(f32) + do[slot].astype(f32)).astype(bf)
-            return carry
-
-        lax.fori_loop(0, 4, add, 0)
+    def fold_cores(t):
+        for k in (1, 2, 3, 0):
+            def add(j, carry, k=k):
+                line = lax.rem(a + k, 4)
+                slot = line * 4 + j
+                f = block(line, j)
+                home((k + 3) % 4 * 4 + j, t).wait_recv()
+                if t == 0:
+                    sq[slot] = (
+                        stage[f, :, q_cols(core)].astype(f32) + dq[slot].astype(f32)
+                    ).astype(bf)
+                else:
+                    so[slot] = (
+                        go[f, o_lines(core), :].astype(f32) + do[slot].astype(f32)
+                    ).astype(bf)
+                return carry
+
+            lax.fori_loop(0, 4, add, 0)
+            if k:
+                hop_one(k, t).start()
+
+    fold_cores(1)
+
+    total = gpair[pl.ds(reach * rows, rows), :]
+    for d in range(1, reach + 1):
+        kv_send(d).wait_recv()
+        total = total + kv_in[d - 1].astype(f32)
+    grad_k, qk_gain_k = rms_back(
+        proj_ref[:, NH * HD : NH * HD + HD],
+        turn_back(total[:, :HD], cos_ref[...], sin_ref[...]),
+        qk_ref[1:2, :],
+    )
+    gproj[:, NH * HD : NH * HD + HD] = grad_k.astype(bf)
+    gproj[:, NH * HD + HD :] = total[:, HD:].astype(bf)
+    stream = tok_ref[...].astype(f32)
+    grad_in, gain_zero = rms_back(stream, dot32(gproj[...], qkv_ref[...], NT), gains_ref[0:1, :])
+    gt_ref[...] = gmid[...] + grad_in
+    tail[...] = jnp.zeros_like(tail)
+    for i, line in enumerate((gain_zero, gain_one, gain_two, g3_ref[...])):
+        tail[i : i + 1, :D] = line
+    tail[4:5, :HD] = qk_gain_q
+    tail[5:6, :HD] = qk_gain_k
+
+    def qkv_tile(t, carry):
+        cols = pl.ds(pl.multiple_of(t * 256, 256), 256)
+        res = dot32(normed_ref[...], gproj[:, cols], TN)
+        low = tail[:, cols]
+        for f in range(16):
+            stage[f, :, cols] = jnp.concatenate(
+                [res[f * keep : (f + 1) * keep], low], axis=0
+            ).astype(bf)
+        return carry
+
+    lax.fori_loop(0, width // 256, qkv_tile, 0)
+    start_away(0)
+    fold_cores(0)
+
+    for copy in own_loads:
+        copy.wait()
+
+    def ff_two(k):
+        return remote(
+            t_ff.at[lax.rem(b + k, 4)], in2_ff.at[3 - k], s2f.at[k], r2f.at[4 - k], second_peer(k)
+        )
+
+    for k in (2, 1, 3, 0):
+        j = lax.rem(b + k, 4)
+        for m in (1, 2, 3):
+            dst = in1_ff.at[m - 1, j]
+            remote(dst, dst, s1f.at[m, j], r1f.at[m, j], partner).wait_recv()
+        total = own_ff[j].astype(f32)
+        for m in range(3):
+            total = total + in1_ff[m, j].astype(f32)
+        t_ff[j] = total.astype(bf)
         if k:
-            for t in (0, 1):
-                hop_one(k, t).start()
-
-    for k in (1, 3, 2):
-        for t in (0, 1):
-            hop_one(4 - k, t).wait_recv()
+            ff_two(k).start()
 
     def hop_two(k, t):
         src, dst = ((tq, iq2), (to, io2))[t]
@@ -588,24 +724,55 @@
             src.at[lax.rem(b + k, 4)], dst.at[3 - k], s2.at[k, t], r2.at[4 - k, t], second_peer(k)
         )
 
-    for k in (2, 1, 3, 0):
-        j = lax.rem(b + k, 4)
-        slot = a * 4 + j
-        for t, (own, got, dst) in enumerate(((sq, iq1, tq), (so, io1, to))):
-            total = own[slot].astype(f32)
+    for t in (1, 0):
+        own, got, dst = ((sq, iq1, tq), (so, io1, to))[t]
+        for k in (1, 3, 2):
+            hop_one(4 - k, t).wait_recv()
+        for k in (2, 1, 3, 0):
+            j = lax.rem(b + k, 4)
+            total = own[a * 4 + j].astype(f32)
             for m in range(3):
                 total = total + got[m, j].astype(f32)
             dst[j] = total.astype(bf)
             if k:
                 hop_two(k, t).start()
 
+    for k in (1, 3, 2):
+        ff_two(4 - k).wait_recv()
+    total = t_ff[b].astype(f32)
+    for m in range(3):
+        total = total + in2_ff[m].astype(f32)
+    all_ff[me] = total.astype(bf)
+
+    def ff_all(k):
+        peer = chip_peer(k) if k else partner
+        return remote(
+            all_ff.at[me], all_ff.at[me], sag.at[k], rag.at[(chips - k) % chips], peer
+        )
+
+    def ff_from(k):
+        dst = all_ff.at[lax.rem(chip + k, chips) * 2 + core]
+        return remote(dst, dst, sag.at[chips + k], rag.at[k], partner)
+
+    def ff_cross(k):
+        dst = all_ff.at[lax.rem(chip + k, chips) * 2 + core]
+        return remote(dst, dst, sag.at[chips + k], rag.at[chips + k], partner)
+
+    def ff_crossed(k):
+        dst = all_ff.at[lax.rem(chip + k, chips) * 2 + 1 - core]
+        return remote(dst, dst, sag.at[k], rag.at[chips + k if k else 0], partner)
+
+    for k in (*range(1, chips), 0):
+        ff_all(k).start()
+
     def hop_chip(k, t):
         buf = (xq, xo)[t]
         return remote(
             buf.at[chip], buf.at[chip], sx.at[k, t], rx.at[chips - k, t], chip_peer(k)
         )
 
-    for t, (own, got, dst) in enumerate(((tq, iq2, xq), (to, io2, xo))):
+    for t in (1, 0):
+        own, got, dst = ((tq, iq2, xq), (to, io2, xo))[t]
         for k in (1, 3, 2):
             hop_two(4 - k, t).wait_recv()
         total = own[b].astype(f32)
@@ -615,15 +782,16 @@
         for k in range(1, chips):
             hop_chip(k, t).start()
 
-    def last(t):
-        part = (oq_ref.at[:, q_cols(core)], oo_ref.at[o_lines(core), :])[t]
+    def last(t, half):
+        part = (oq_ref.at[:, q_cols(half)], oo_ref.at[o_lines(half), :])[t]
         return remote(part, part, sf.at[t], rf.at[t], partner)
 
-    def last_home(t):
-        part = (oq_ref.at[:, q_cols(1 - core)], oo_ref.at[o_lines(1 - core), :])[t]
-        return remote(part, part, sf.at[t], rf.at[t], partner)
-
-    for t, buf in enumerate((xq, xo)):
+    for k in range(1, chips):
+        ff_from(k).wait_recv()
+        ff_cross(k).start()
+
+    for t in (1, 0):
+        buf = (xq, xo)[t]
         for k in range(1, chips):
             dst = buf.at[lax.rem(chip + k, chips)]
             remote(dst, dst, sx.at[k, t], rx.at[k, t], partner).wait_recv()
@@ -634,7 +802,17 @@
             oq_ref[:, q_cols(core)] = total
         else:
             oo_ref[o_lines(core), :] = total
-        last(t).start()
+        last(t, core).start()
+
+    for k in range(chips):
+        ff_crossed(k).wait_recv()
+    lines = og_ref.shape[0] // members
+    share = all_ff.shape[1] // 3
+    for i, dst in enumerate((og_ref, ou_ref, od_ref)):
+        for m in range(members):
+            dst[m * lines : (m + 1) * lines, :] = all_ff[
+                m, i * share : (i + 1) * share, :
+            ].astype(f32)[:lines]
 
     def end_away(i, carry):
         for t in (0, 1):
@@ -642,40 +820,73 @@
         return carry
 
     lax.fori_loop(0, 16, end_away, 0)
+    for k in (1, 2, 3):
+        for j in range(4):
+            ff_one(k, j).wait_send()
+        ff_two(k).wait_send()
+    for d in range(1, reach + 1):
+        kv_send(d).wait_send()
+    for k in range(chips):
+        ff_all(k).wait_send()
+        if k:
+            ff_cross(k).wait_send()
     for t in (0, 1):
         for k in (1, 2, 3):
             hop_one(k, t).wait_send()
             hop_two(k, t).wait_send()
         for k in range(1, chips):
             hop_chip(k, t).wait_send()
-        last(t).wait_send()
-        last_home(t).wait_recv()
-
-
-def scatter_attention(gq, small, go):
+        last(t, core).wait_send()
+        last(t, 1 - core).wait_recv()
+
+
+def backward_rest(gff, values, keep, lines):
     f32, bf = jnp.float32, jnp.bfloat16
     vm = pl.BlockSpec(memory_space=pltpu.VMEM)
+    hbm = pl.BlockSpec(memory_space=pl.ANY)
     dma = pltpu.SemaphoreType.DMA
-    keep, width = gq.shape[0] // 16, gq.shape[1]
-    q_rows = keep + small.shape[1]
-    o_rows, o_width = go.shape[1:]
+    rows = values[0].shape[0]
+    owners, ff_rows = gff.shape[:2]
+    q_rows, width = keep + 8, (NH + 2) * HD
+    o_rows, o_width = NH * HD // owners, D
     q_half, o_half = width // 2, o_rows // 2
     chips = lax.axis_size("ctx") // 2
+    pairs = values[9].shape[0]
+    reach = pairs // rows - 1
 
     def two(*lead):
         return [pltpu.VMEM(lead + (q_rows, q_half), bf), pltpu.VMEM(lead + (o_half, o_width), bf)]
 
+    def ff(*lead):
+        return pltpu.VMEM(lead + (ff_rows, D), bf)
+
+    weight = jax.ShapeDtypeStruct((lines, D), f32)
     return pl.pallas_call(
-        scatter_kernel,
+        back_kernel,
         out_shape=(
+            jax.ShapeDtypeStruct((rows, D), f32),
             jax.ShapeDtypeStruct((q_rows, width), f32),
             jax.ShapeDtypeStruct((o_rows, o_width), f32),
-        ),
-        in_specs=[vm] * 3,
-        out_specs=(vm,) * 2,
+            weight, weight, weight,
+        ),
+        in_specs=[hbm] + [vm] * len(values),
+        out_specs=(vm,) * 6,
         scratch_shapes=[
+            ff(4), ff(3, 4), ff(4), ff(3), ff(2 * chips),
+            pltpu.VMEM((reach, rows, 2 * HD), bf),
+            pltpu.VMEM((reach, rows, 2 * HD), bf),
+            pltpu.VMEM((rows, D), f32),
+            pltpu.VMEM((pairs, 2 * HD), f32),
+            pltpu.VMEM((rows, width), bf),
+            pltpu.VMEM((8, width), f32),
             pltpu.VMEM((16, q_rows, width), bf),
+            pltpu.VMEM((16, o_rows, o_width), bf),
             *two(16), *two(16), *two(3, 4), *two(4), *two(3), *two(chips),
+            dma((4,)),
+            dma((4, 4)), dma((4, 4)),
+            dma((4,)), dma((4,)),
+            dma((2 * chips,)), dma((2 * chips,)),
+            dma((reach,)), dma((reach,)),
             dma((16, 2)), dma((16, 2)),
             dma((4, 2)), dma((4, 2)),
             dma((4, 2)), dma((4, 2)),
@@ -683,12 +894,12 @@
             dma((2,)), dma((2,)),
         ],
         compiler_params=pltpu.CompilerParams(
-            collective_id=3, has_side_effects=True, vmem_limit_bytes=48 * 1024 * 1024
+            collective_id=3, has_side_effects=True, vmem_limit_bytes=62 * 1024 * 1024
         ),
         cost_estimate=pl.CostEstimate(
-            flops=0, bytes_accessed=64 * (q_rows * width + o_rows * o_width), transcendentals=0
-        ),
-    )(gq, small, go)
+            flops=12 * rows * width * D, bytes_accessed=64 * ff_rows * D, transcendentals=0
+        ),
+    )(gff, *values)
 
 
 def on_device(
@@ -753,7 +964,7 @@
     k_raw = projected[:, NH * HD : NH * HD + HD]
     values = projected[:, NH * HD + HD :].astype(jnp.bfloat16)
     prep_fixed = partial(head_prep, cos_table=cos_table, sin_table=sin_table)
-    (q_rot, k_rot), prep_back = jax.vjp(prep_fixed, q_raw, k_raw, qk_all[0], qk_all[1])
+    q_rot, k_rot = prep_fixed(q_raw, k_raw, qk_all[0], qk_all[1])
     queries = q_rot.astype(jnp.bfloat16)
     own_pair = jnp.concatenate([k_rot.astype(jnp.bfloat16), values], axis=-1)
     reach = min(-(-(WINDOW - 1) // local_len), ctx_size - 1)
@@ -787,97 +998,40 @@
     mid_stream = stream + rms_norm(attn, gains_all[1])
     normed_two = rms_norm(mid_stream, gains_all[2]).astype(jnp.bfloat16)
 
-    grad_final = cotangent.astype(jnp.float32).reshape(local_len, D)
-    output, grad_normed_two, grad_gain_three, d_gate, d_up, d_down = ffn(
-        normed_two,
-        mid_stream,
-        cotangent.reshape(local_len, D),
-        gains_all[3:4],
-        ffn_full,
-    )
-    output = output.reshape(1, local_len, D)
-    grad_gain_three = grad_gain_three[0]
-    mlp_grads = jnp.concatenate([d_gate, d_up, d_down], axis=1)
-    mlp_share = lax.psum_scatter(mlp_grads, "fsdp", scatter_dimension=0, tiled=True)
-    mlp_total = lax.all_gather(mlp_share[:slice_rows], "ctx", axis=0, tiled=True).astype(
-        jnp.float32
-    )
-
-    grad_mid_part, grad_gain_two = jax.vjp(rms_norm, mid_stream, gains_all[2])[1](grad_normed_two)
-    grad_mid = grad_final + grad_mid_part
-    grad_attn, grad_gain_one = jax.vjp(rms_norm, attn, gains_all[1])[1](grad_mid)
-    grad_attn_low = grad_attn.astype(jnp.bfloat16)
-    grad_attended = lax.dot_general(
-        grad_attn_low, out_full, CONTRACT_LAST, preferred_element_type=jnp.float32
-    ).astype(jnp.bfloat16)
-    grad_out_weight = lax.dot_general(
-        attended, grad_attn_low, CONTRACT_FIRST, preferred_element_type=jnp.float32
-    )
-    grad_heads = grad_attended.reshape(local_len, NH, HD)
-    grad_probs = jnp.einsum(
-        "qhd,kd->hqk", grad_heads, value_all, preferred_element_type=jnp.float32
-    )
-    row_total = jnp.sum(probs * grad_probs, axis=-1, keepdims=True)
-    grad_scores = (probs * (grad_probs - row_total)).astype(jnp.bfloat16)
-    grad_queries = (
-        jnp.einsum("hqk,kd->qhd", grad_scores, key_all, preferred_element_type=jnp.float32) * scale
-    )
-    grad_keys = (
-        jnp.einsum("hqk,qhd->kd", grad_scores, queries, preferred_element_type=jnp.float32) * scale
-    )
-    grad_values = jnp.einsum(
-        "hqk,qhd->kd", probs_low, grad_heads, preferred_element_type=jnp.float32
-    )
-    grad_pairs = jnp.concatenate([grad_keys, grad_values], axis=-1)
-    own_grad = grad_pairs[reach * local_len :]
-    for distance in range(1, reach + 1):
-        block_grad = grad_pairs[(reach - distance) * local_len : (reach - distance + 1) * local_len]
-        own_grad = own_grad + from_behind(block_grad.astype(jnp.bfloat16), "ctx", -distance).astype(
-            jnp.float32
-        )
-    grad_q_raw, grad_k_raw, grad_q_gain, grad_k_gain = prep_back((grad_queries, own_grad[:, :HD]))
-    grad_projected = jnp.concatenate(
-        [grad_q_raw.reshape(local_len, NH * HD), grad_k_raw, own_grad[:, HD:]], axis=1
-    ).astype(jnp.bfloat16)
-    grad_normed = lax.dot_general(
-        grad_projected, qkv_full, CONTRACT_LAST, preferred_element_type=jnp.float32
-    )
-    grad_qkv_weight = lax.dot_general(
-        flat_normed, grad_projected, CONTRACT_FIRST, preferred_element_type=jnp.float32
-    )
-    grad_input_part, grad_gain_zero = jax.vjp(rms_norm, stream, gains_all[0])[1](grad_normed)
-    grad_tokens = (grad_mid + grad_input_part).reshape(1, local_len, D)
-    gain_grads = jnp.stack([grad_gain_zero, grad_gain_one, grad_gain_two, grad_gain_three])
-    qk_grads = jnp.stack([grad_q_gain, grad_k_gain])
-    owners = lax.axis_size("fsdp")
-
-    def by_owner(grads):
-        lines = grads.shape[0]
-        flat = grads.reshape(lines, owners, -1).transpose(1, 0, 2).reshape(owners, 1, -1)
-        return jnp.pad(flat, ((0, 0), (0, 0), (0, extra - flat.shape[2])))
-
-    small = jnp.concatenate(
-        [by_owner(gain_grads), by_owner(qk_grads), jnp.zeros((owners, 6, extra), jnp.float32)],
-        axis=1,
-    )
-    own_qkv, total_out = scatter_attention(
-        grad_qkv_weight,
-        small,
-        grad_out_weight.astype(jnp.bfloat16).reshape(owners, out_weight.shape[0], D),
-    )
-    total_qkv = own_qkv[: qkv_weight.shape[0]]
-    total_gains = own_qkv[qkv_weight.shape[0], :n_gain].reshape(norm_gains.shape)
-    total_qk = own_qkv[qkv_weight.shape[0] + 1, :n_qk].reshape(qk_gains.shape)
+    cot = cotangent.reshape(local_len, D)
+    output, grad_normed_two, grad_gain_three, ffn_grads = ffn(
+        normed_two, mid_stream, cot, gains_all[3:4], ffn_full
+    )
+    bias = jnp.where(allowed, 0.0, NEG_FILL)
+    keep = qkv_weight.shape[0]
+    grad_tokens, own_qkv, total_out, total_gate, total_up, total_down = backward_rest(
+        ffn_grads,
+        (
+            grad_normed_two, mid_stream, attn, cot, tokens.reshape(local_len, D), gains_all,
+            qk_all, projected, queries.reshape(local_len, NH * HD), pair_all, attended,
+            flat_normed, qkv_full, out_full, cos_table, sin_table, bias, grad_gain_three,
+        ),
+        keep,
+        own_rows,
+    )
+    owner = lax.axis_index("fsdp")
+    gain_lines, qk_lines = norm_gains.shape, qk_gains.shape
+    total_gains = lax.dynamic_slice(
+        own_qkv[keep : keep + 4, :D], (0, owner * gain_lines[1]), gain_lines
+    )
+    total_qk = lax.dynamic_slice(
+        own_qkv[keep + 4 : keep + 6, :HD], (0, owner * qk_lines[1]), qk_lines
+    )
     return (
-        output,
-        grad_tokens,
+        output.reshape(tokens.shape),
+        grad_tokens.reshape(tokens.shape),
         total_gains,
         total_qk,
-        total_qkv,
+        own_qkv[:keep],
         total_out,
-        mlp_total[:, :D],
-        mlp_total[:, D : 2 * D],
-        mlp_total[:, 2 * D :],
+        total_gate,
+        total_up,
+        total_down,
     )
 
 

time: 385 us -> 325 us (0.84)
  waiting for transfers between devices: 77.4 us -> 0.03 us
  Pallas kernels: 173 us -> 236 us
  matrix products: 24.2 us -> 5.03 us
  other arithmetic: 23.2 us -> 9.7 us
  starting transfers between devices: 19.7 us -> 11 us
    reduce_scatter x1 -> x0, waiting for transfers between devices: 73.3 us -> none  [on_device(): lax.psum_scatter(mlp_grads, 'fsdp', scatter_dimension=0, tiled=True)]
    pallas_call x1, Pallas kernels: 53 us -> 115 us  [backward_rest(): pl.pallas_call(back_kernel, out_shape=(jax.ShapeDtypeStruct((rows, D), f3...]
    dot_general x8 -> x0, matrix products: 14.6 us -> none  [the longest x1 4.31 us: on_device(): lax.dot_general(grad_projected, qkv_full, CONTRACT_LAST, preferred_elemen...]
    ppermute x8 -> x4, starting transfers between devices: 19.6 us -> 10.9 us  [from_behind(): return lax.ppermute(array, axis, pairs)]
    concatenate x2 -> x0, other arithmetic: 6.37 us -> none  [the longest x1 6.29 us: on_device(): mlp_grads = jnp.concatenate([d_gate, d_up, d_down], axis=1)]
    reduce_sum x4 -> x0, other arithmetic: 5.29 us -> none  [rms_norm(): values * lax.rsqrt(jnp.mean(values * values, axis=-1, keepdims=True) + EPS)]
    another operation x12 -> x2, local copies, waits for them, and re-layouts: 5.32 us -> 0.17 us
    ppermute x8 -> x4, waiting for transfers between devices: 4.01 us -> 0.01 us  [from_behind(): return lax.ppermute(array, axis, pairs)]
  transfers between devices with their start and end apart: 11 -> 5, of which waited for: 3 -> 0; matrix products, arithmetic and copies ran while one was open for 15% -> 9% of each run, Pallas kernels for 24% -> 12%
where the time goes in v4:
time: 325 us; the launch traced here: 319 us
  Pallas kernels  236 us (73%)
  local copies, waits for them, and re-layouts  35.2 us (11%)
  between operations  14.5 us (4%)
  starting transfers between devices  11 us (3%)
  other arithmetic  9.7 us (3%)
  blocking collectives  8.13 us (3%)
  matrix products  5.03 us (2%)
    pallas_call x1, Pallas kernels, backward_rest(): pl.pallas_call(back_kernel, out_shape=(jax.ShapeDtypeStruct((rows, D), f3...  115 us
    pallas_call x1, Pallas kernels, ffn(): pl.pallas_call(ffn_kernel, out_shape=(jax.ShapeDtypeStruct((rows, D), bf)...  82.8 us
    pallas_call x1, Pallas kernels, gather_attention(): pl.pallas_call(gather_kernel, out_shape=(jax.ShapeDtypeStruct((16 * keep,...  37.9 us
    unnamed x66, local copies, waits for them, and re-layouts  14.6 us
    ppermute x4, starting transfers between devices, from_behind(): return lax.ppermute(array, axis, pairs)  10.9 us
    all_gather x1, blocking collectives, on_device(): seg_all = lax.all_gather(segments[0], 'ctx', axis=0, tiled=True)  8.13 us
  transfers between devices with their start and end apart: 5, of which 0 were waited for; matrix products, arithmetic and copies ran while one was open for 9% of the time, Pallas kernels for 12%

profile of v4, /device:TPU:73, one launch (start us, length us, event | category | flops | bytes accessed | tf_op | source)
XLA Modules:
  0.0 319.2 jit_solution(8841329709903672785)
XLA Ops:
  7.2 1.5 reshape.310
  9.1 1.5 reshape.308
  12.8 37.9 %shard_map.169 = (bf16[1152,1536]{1,0:T(8,128)(2,1)S(1)}, bf16[1024,1152]{1,0:T(8,128)(2,1)S(1)}, f32[16,8,384]{2,1,0:T(8,128)S(1)}) custom-call(bf16[80,1536]{1,0:T(8,128)(2,1)S(1)} %pad_maximum_fusion.qkv_ref, bf16[64,1152]{1,0:T(8,128)(2,1)S(1)} %copy-done.3), custom_call_target="tpu_custom_call" | custom-call | bytes 12582912 | tf_op jit(solution)/shard_map/pallas_call | solution.py:452
  50.7 1.4 copy-done.1
  52.7 1.2 slice_reduce_fusion
  53.9 1.4 reshape_squeeze.6
  55.3 1.4 copy.62
  56.7 1.4 fusion.26
  58.9 1.1 fusion.9
  60.0 1.1 fusion.11.normed_ref
  63.8 1.0 multiply_reduce_fusion.3
  67.1 4.6 %collective-permute-start = (bf16[128,512]{1,0:T(8,128)(2,1)S(1)}, bf16[128,512]{1,0:T(8,128)(2,1)S(1)}, u32[]{:S(2)}, u32[]{:S(2)}) collective-permute-start(bf16[128,512]{1,0:T(8,128)(2,1)S(1)} %pad_maximum_fusion.1), channel_id=1, source_target_pairs={{0,4},{1,5},{2,6},{3,7},{8,12},{9,13},{10,14},{11,15},{16,20},{17,... | collective-permute-start | bytes 393224 | tf_op jit(solution)/shard_map/ppermute | solution.py:26
  71.8 1.3 collective-permute-start.1
  73.1 2.8 collective-permute-start.2
  75.9 2.1 collective-permute-start.3
  78.8 8.1 %all-gather = s32[1,1024]{1,0:T(1,128)S(1)} all-gather(s32[1,128]{1,0:T(1,128)S(1)} %copy-done.25), channel_id=2, replica_groups=mesh['fsdp'=16,'ctx'=8] {'ctx'}, dimensions={1}, use_global_device_ids=true | all-gather | bytes 4608 | tf_op jit(solution)/shard_map/all_gather | solution.py:944
  95.1 1.6 fusion.28
  96.7 2.2 convolution_convert_fusion
  101.9 82.8 %shard_map.170 = (bf16[128,1152]{1,0:T(8,128)(2,1)}, f32[128,1152]{1,0:T(8,128)}, f32[1,1152]{1,0:T(1,128)}, bf16[16,192,1152]{2,1,0:T(8,128)(2,1)}) custom-call(bf16[128,1152]{1,0:T(8,128)(2,1)} %multiply_convert_fusion.normed_ref, f32[128,1152]{1,0:T(8,128)} %copy-done.7, bf16[128,1152]{1,0:T(8,128)(2,1)} %bitcast.77, f32[1,1152]{1,0:T(1,128)} %slice.121.gain_ref, ...), custom_call_target="tpu_custom_call" | custom-call | flops 21743271936 | bytes 16515072 | tf_op jit(solution)/shard_map/pallas_call | solution.py:253
  184.7 114.9 %shard_map.171 = (f32[128,1152]{1,0:T(8,128)}, f32[80,1536]{1,0:T(8,128)}, f32[64,1152]{1,0:T(8,128)}, f32[432,1152]{1,0:T(8,128)}, f32[432,1152]{1,0:T(8,128)}, /*index=5*/f32[432,1152]{1,0:T(8,128)}) custom-call(bf16[16,192,1152]{2,1,0:T(8,128)(2,1)} %get-tuple-element.50.gff, f32[128,1152]{1,0:T(8,128)} %get-tuple-element.51.gn_ref, ...), custom_call_target="tpu_custom_call" | custom-call | flops 2717908992 | bytes 14155776 | tf_op jit(solution)/shard_map/pallas_call | solution.py:864
  301.1 1.8 slice.124
  306.5 1.3 copy.78
  308.8 1.3 copy.79
  311.1 1.3 copy.80
  (125 shorter events, 27.6 us)
Async XLA Ops:
  7.2 1.6 copy-start.14
  7.2 94.7 %all-gather.4.cloned.1.call-start = ((), (), s32[]{:S(2)}) async-start(), calls=%async_computation | async-start | bytes 7520256 | tf_op jit(solution)/shard_map/all_gather | solution.py:955
  10.5 1.0 copy-start.27
  10.6 1.3 copy-start.22
  50.7 1.4 copy-start.1
  52.1 9.7 %copy-start = (bf16[1152,1536]{1,0:T(8,128)(2,1)}, bf16[1152,1536]{1,0:T(8,128)(2,1)S(1)}, u32[]{:S(2)}) copy-start(bf16[1152,1536]{1,0:T(8,128)(2,1)S(1)} %get-tuple-element.47.qkv_ref) | copy-start | bytes 10616836
  63.6 14.5 %copy-start.6 = (f32[128,1536]{1,0:T(8,128)S(1)}, f32[128,1536]{1,0:T(8,128)}, u32[]{:S(2)}) copy-start(f32[128,1536]{1,0:T(8,128)} %copy-done.5) | copy-start | bytes 2359300
  66.2 21.8 %copy-start.15 = (f32[128,128]{1,0:T(8,128)}, f32[128,128]{1,0:T(8,128)S(1)}, u32[]{:S(2)}) copy-start(f32[128,128]{1,0:T(8,128)S(1)} %get-tuple-element.71.sin_ref) | copy-start | bytes 196612
  66.2 21.8 %copy-start.16 = (f32[128,128]{1,0:T(8,128)}, f32[128,128]{1,0:T(8,128)S(1)}, u32[]{:S(2)}) copy-start(f32[128,128]{1,0:T(8,128)S(1)} %get-tuple-element.72.cos_ref) | copy-start | bytes 196612
  67.1 24.7 %collective-permute-start = (bf16[128,512]{1,0:T(8,128)(2,1)S(1)}, bf16[128,512]{1,0:T(8,128)(2,1)S(1)}, u32[]{:S(2)}, u32[]{:S(2)}) collective-permute-start(bf16[128,512]{1,0:T(8,128)(2,1)S(1)} %pad_maximum_fusion.1), channel_id=1, source_target_pairs={{0,4},{1,5},{2,6},{3,7},{8,12},{9,13},{10,14},{11,15},{16,20},{17,... | collective-permute-start | bytes 393224 | tf_op jit(solution)/shard_map/ppermute | solution.py:26
  71.8 20.7 %collective-permute-start.1 = (bf16[128,512]{1,0:T(8,128)(2,1)S(1)}, bf16[128,512]{1,0:T(8,128)(2,1)S(1)}, u32[]{:S(2)}, u32[]{:S(2)}) collective-permute-start(bf16[128,512]{1,0:T(8,128)(2,1)S(1)} %pad_maximum_fusion.1), channel_id=1, source_target_pairs={{0,3},{1,4},{2,5},{3,6},{4,7},{8,11},{9,12},{10,13},{11,14},{12,15... | collective-permute-start | bytes 393224 | tf_op jit(solution)/shard_map/ppermute | solution.py:26
  73.1 20.0 %collective-permute-start.2 = (bf16[128,512]{1,0:T(8,128)(2,1)S(1)}, bf16[128,512]{1,0:T(8,128)(2,1)S(1)}, u32[]{:S(2)}, u32[]{:S(2)}) collective-permute-start(bf16[128,512]{1,0:T(8,128)(2,1)S(1)} %pad_maximum_fusion.1), channel_id=1, source_target_pairs={{0,2},{1,3},{2,4},{3,5},{4,6},{5,7},{8,10},{9,11},{10,12},{11,13},... | collective-permute-start | bytes 393224 | tf_op jit(solution)/shard_map/ppermute | solution.py:26
  75.9 17.8 %collective-permute-start.3 = (bf16[128,512]{1,0:T(8,128)(2,1)S(1)}, bf16[128,512]{1,0:T(8,128)(2,1)S(1)}, u32[]{:S(2)}, u32[]{:S(2)}) collective-permute-start(bf16[128,512]{1,0:T(8,128)(2,1)S(1)} %pad_maximum_fusion.1), channel_id=1, source_target_pairs={{0,1},{1,2},{2,3},{3,4},{4,5},{5,6},{6,7},{8,9},{9,10},{10,11},{11... | collective-permute-start | bytes 393224 | tf_op jit(solution)/shard_map/ppermute | solution.py:26
  87.8 2.1 copy-start.24
  87.8 2.4 copy-start.23
  88.1 6.4 %copy-start.18 = (bf16[128,256]{1,0:T(8,128)(2,1)S(1)}, bf16[128,256]{1,0:T(8,128)(2,1)}, u32[]{:S(2)}) copy-start(bf16[128,256]{1,0:T(8,128)(2,1)} %slice.165) | copy-start | bytes 196612
  96.7 3.0 copy-start.2
  100.3 84.4 %copy-start.8 = (f32[128,1152]{1,0:T(8,128)}, f32[128,1152]{1,0:T(8,128)S(1)}, u32[]{:S(2)}) copy-start(f32[128,1152]{1,0:T(8,128)S(1)} %get-tuple-element.74.attn_ref) | copy-start | bytes 1769476
  184.7 119.6 %copy-start.19 = (bf16[128,1152]{1,0:T(8,128)(2,1)S(1)}, bf16[128,1152]{1,0:T(8,128)(2,1)}, u32[]{:S(2)}) copy-start(bf16[128,1152]{1,0:T(8,128)(2,1)} %get-tuple-element.49) | copy-start | bytes 884740
  299.6 5.4 %copy-start.17 = (f32[128,1152]{1,0:T(8,128)S(1)}, f32[128,1152]{1,0:T(8,128)}, u32[]{:S(2)}) copy-start(f32[128,1152]{1,0:T(8,128)} %get-tuple-element.53) | copy-start | bytes 1769476
  301.1 4.7 %copy-start.20 = (f32[64,1152]{1,0:T(8,128)S(1)}, f32[64,1152]{1,0:T(8,128)}, u32[]{:S(2)}) copy-start(f32[64,1152]{1,0:T(8,128)} %get-tuple-element.91) | copy-start | bytes 884740
  303.0 3.5 %copy-start.13 = (f32[432,1152]{1,0:T(8,128)S(1)}, f32[432,1152]{1,0:T(8,128)}, u32[]{:S(2)}) copy-start(f32[432,1152]{1,0:T(8,128)} %get-tuple-element.92) | copy-start | bytes 5971972
  306.5 2.3 copy-start.12
  308.8 2.3 copy-start.11
  (9 other events, 7.4 us)
Sparse Core Ops, SparseCore 0:
  11.6 69.4 all-gather.3

commit v5 on v4

--- a/solution.py
+++ b/solution.py
@@ -1,6 +1,5 @@
-from functools import partial
-
 import jax
+import numpy as np
 import jax.numpy as jnp
 from jax import lax
 from jax.experimental import pallas as pl
@@ -16,47 +15,10 @@
 EPS = 1e-06
 ROPE_BASE = 10000.0
 NEG_FILL = -1e30
-CONTRACT_LAST = (((1,), (1,)), ((), ()))
-CONTRACT_FIRST = (((0,), (0,)), ((), ()))
-
-
-def from_behind(array, axis, by):
-    devices = lax.axis_size(axis)
-    pairs = [(i, i + by) for i in range(devices) if 0 <= i + by < devices]
-    return lax.ppermute(array, axis, pairs)
 
 
 def rms_norm(values, gain_vec):
     return values * lax.rsqrt(jnp.mean(values * values, axis=-1, keepdims=True) + EPS) * gain_vec
-
-
-def rotate(values, cos_table, sin_table):
-    half_size = values.shape[-1] // 2
-    first_half = values[..., :half_size]
-    second_half = values[..., half_size:]
-    return jnp.concatenate(
-        [
-            first_half * cos_table - second_half * sin_table,
-            second_half * cos_table + first_half * sin_table,
-        ],
-        axis=-1,
-    )
-
-
-def rope_tables(positions):
-    frequency = ROPE_BASE ** (-(2.0 * jnp.arange(HD // 2).astype(jnp.float32)) / HD)
-    angles = positions.astype(jnp.float32)[..., None] * frequency
-    return (jnp.cos(angles), jnp.sin(angles))
-
-
-def head_prep(q_raw, k_raw, q_gain, k_gain, cos_table, sin_table):
-    queries = rotate(rms_norm(q_raw, q_gain), cos_table[:, None, :], sin_table[:, None, :])
-    key_rows = rotate(rms_norm(k_raw, k_gain), cos_table, sin_table)
-    return (queries, key_rows)
-
-
-def gelu_product(gate_pre, up_pre):
-    return jax.nn.gelu(gate_pre, approximate=True) * up_pre
 
 
 MESH = pl.DeviceIdType.MESH
@@ -203,7 +165,7 @@
     mlp = collect(0, sums)
     r = lax.rsqrt(jnp.mean(mlp * mlp, axis=-1, keepdims=True) + EPS)
     n = mlp * r
-    gain = gain_ref[...]
+    gain = gain_ref[3:4, :]
     out_ref[...] = (mid_ref[...] + n * gain).astype(jnp.bfloat16)
     dy = cot_ref[...].astype(jnp.float32)
     ggain_ref[...] = jnp.sum(dy * n, axis=0, keepdims=True)
@@ -323,10 +285,35 @@
     pl.semaphore_wait(barrier, len(peers))
 
 
-def gather_kernel(
-    qkv_ref, wo_ref, qkv_out, wo_all, rows_out, qkv_all,
-    l_sem, s1, r1, s2, r2, sd, rd,
+def rms_back(values, grad, gain):
+    r = lax.rsqrt(jnp.mean(values * values, axis=-1, keepdims=True) + EPS)
+    n = values * r
+    dyg = grad * gain
+    return (
+        r * (dyg - n * jnp.mean(dyg * n, axis=-1, keepdims=True)),
+        jnp.sum(grad * n, axis=0, keepdims=True),
+    )
+
+
+def stack_heads(values):
+    return jnp.concatenate([values[:, h * HD : (h + 1) * HD] for h in range(NH)], axis=0)
+
+
+def turn_back(grad, cos_table, sin_table):
+    left, right = grad[:, : HD // 2], grad[:, HD // 2 :]
+    return jnp.concatenate(
+        [left * cos_table + right * sin_table, right * cos_table - left * sin_table], axis=1
+    )
+
+
+def front_kernel(
+    qkv_ref, wo_ref, ffn_ref, tok_ref, seg_ref, seg_col, table_ref,
+    qkv_out, wo_all, ffn_all, gains_ref, qk_ref, normed_ref, proj_ref, q_ref, pair_ref, att_ref,
+    attn_ref, mid_ref, low_ref, bias_ref, turn_ref,
+    qkv_all, seg_in,
+    l_sem, s1, r1, s2, r2, sd, rd, s1f, r1f, s2f, r2f, skv, rkv, ssg, rsg,
 ):
+    f32, bf = jnp.float32, jnp.bfloat16
     y, z, chip, core = place()
     a, b, block = shape_of(y, z, core)
     _, _, block_there = shape_of(y, z, 1 - core)
@@ -334,6 +321,13 @@
     o_rows = wo_ref.shape[0]
     q_half, o_half = width // 2, o_rows // 2
     partner = {"ctx": chip * 2 + 1 - core}
+    me = chip * 2 + core
+    rows = tok_ref.shape[0]
+    reach = pair_ref.shape[0] // rows - 1
+    members = 2 * (lax.axis_size("ctx") // 2)
+
+    def member(k):
+        return {"ctx": lax.rem(me + k, members)}
 
     def views(f, half):
         return (
@@ -356,6 +350,8 @@
         pltpu.make_async_copy(
             wo_ref, wo_all.at[pl.ds(pl.multiple_of(here * o_rows, 16), o_rows), :], l_sem.at[1]
         ),
+        pltpu.make_async_copy(ffn_ref, ffn_all.at[here], l_sem.at[2]),
+        pltpu.make_async_copy(table_ref.at[me], turn_ref, l_sem.at[3]),
     ]
     for copy in locals_:
         copy.start()
@@ -366,7 +362,36 @@
     def second_peer(k):
         return {"fsdp": block(a, lax.rem(b + k, 4))}
 
-    greet([first_peer(k) for k in (1, 2, 3)] + [second_peer(k) for k in (1, 2, 3)] + [partner])
+    greet(
+        [first_peer(k) for k in (1, 2, 3)]
+        + [second_peer(k) for k in (1, 2, 3)]
+        + [member(k) for k in range(1, members)]
+    )
+
+    def seg_send(d):
+        return remote(
+            seg_ref, seg_in.at[reach - d], ssg.at[d - 1], rsg.at[d - 1], member(d)
+        )
+
+    def ffn_one(k):
+        return remote(ffn_ref, ffn_all.at[here], s1f.at[k], r1f.at[4 - k], first_peer(k))
+
+    def ffn_block(j, m):
+        return ffn_all.at[block(lax.rem(a + j, 4), lax.rem(b + m, 4))]
+
+    def ffn_two(j, k):
+        dst = ffn_block(j, 0)
+        src = dst if j else ffn_ref
+        return remote(src, dst, s2f.at[j, k], r2f.at[j, 4 - k], second_peer(k))
+
+    def ffn_pass(j):
+        dst, k = (ffn_block(j, 3), 1) if j < 2 else (ffn_block(j, 1), 3)
+        return remote(dst, dst, s2f.at[j, 2], r2f.at[j, 2], second_peer(k))
+
+    def ffn_got(j, m):
+        dst = ffn_block(j, m)
+        sems = (s1f.at[j], r1f.at[j]) if m == 0 else (s2f.at[j, m], r2f.at[j, m])
+        return remote(dst, dst, *sems, partner)
 
     def hop_one(k, t):
         return remote(mine[t], views(here, core)[t], s1.at[k, t], r1.at[4 - k, t], first_peer(k))
@@ -407,6 +432,13 @@
                 hop_two(j, k, t).start()
             cross(j, 0, t).start()
 
+    for d in range(1, reach + 1):
+        seg_send(d).start()
+    for k in (1, 3, 2):
+        ffn_one(k).start()
+    for k in (1, 3):
+        ffn_two(0, k).start()
+
     def pass_on(i, carry):
         m, j = i // 4 + 1, lax.rem(i, 4)
         for t in both:
@@ -433,73 +465,161 @@
                 hop_two(j, k, t).wait_send()
 
     keep = qkv_out.shape[0] // 16
+    extra = jnp.zeros((q_rows - keep, width), f32)
     for f in range(0, 16, 2):
-        left = qkv_all[pl.ds(f * q_rows, q_rows), :].astype(jnp.float32)
-        right = qkv_all[pl.ds((f + 1) * q_rows, q_rows), :].astype(jnp.float32)
+        left = qkv_all[pl.ds(f * q_rows, q_rows), :].astype(f32)
+        right = qkv_all[pl.ds((f + 1) * q_rows, q_rows), :].astype(f32)
         qkv_out[pl.ds(f * keep, 2 * keep), :] = jnp.concatenate(
             [left[:keep], right[:keep]], axis=0
-        ).astype(jnp.bfloat16)
-        rows_out[f] = left[keep:, : rows_out.shape[2]]
-        rows_out[f + 1] = right[keep:, : rows_out.shape[2]]
-
-
-def gather_attention(qkv_shard, wo_shard, keep, extra):
-    bf = jnp.bfloat16
+        ).astype(bf)
+        extra = extra + left[keep:] + right[keep:]
+    gains = extra[:4, :D]
+    gains_ref[...] = gains
+    qk_ref[...] = extra[4:6, :HD]
+
+    stream = tok_ref[...].astype(f32)
+    normed_ref[...] = rms_norm(stream, gains[0:1]).astype(bf)
+    proj_ref[...] = dot32(normed_ref[...], qkv_out[...], NN)
+    cos_table, sin_table = turn_ref[:, : HD // 2], turn_ref[:, HD // 2 :]
+
+    def turn(values, gain, cos_part, sin_part):
+        values = rms_norm(values, gain)
+        left, right = values[:, : HD // 2], values[:, HD // 2 :]
+        return jnp.concatenate(
+            [left * cos_part - right * sin_part, right * cos_part + left * sin_part], axis=1
+        ).astype(bf)
+
+    own = pl.ds(reach * rows, rows)
+    pair_ref[own, :HD] = turn(
+        proj_ref[:, NH * HD : NH * HD + HD], extra[5:6, :HD], cos_table, sin_table
+    )
+    pair_ref[own, HD:] = proj_ref[:, NH * HD + HD :].astype(bf)
+
+    def kv_send(d):
+        return remote(
+            pair_ref.at[own],
+            pair_ref.at[pl.ds((reach - d) * rows, rows)],
+            skv.at[d - 1], rkv.at[d - 1], member(d),
+        )
+
+    for d in range(1, reach + 1):
+        kv_send(d).start()
+    for j in (1, 3, 2):
+        ffn_got(j, 0).wait_recv()
+        for k in (1, 3):
+            ffn_two(j, k).start()
+    queries = turn(
+        stack_heads(proj_ref[:, : NH * HD]),
+        extra[4:5, :HD],
+        jnp.concatenate([cos_table] * NH, axis=0),
+        jnp.concatenate([sin_table] * NH, axis=0),
+    )
+    for h in range(NH):
+        q_ref[:, h * HD : (h + 1) * HD] = queries[h * rows : (h + 1) * rows]
+
+    for d in range(1, reach + 1):
+        seg_send(d).wait_recv()
+    seg_in[reach] = seg_ref[...]
+    key_seg = jnp.concatenate([seg_in[p][0:1, :] for p in range(reach + 1)], axis=1)
+    shape = (rows, (reach + 1) * rows)
+    spacing = (
+        reach * rows + lax.broadcasted_iota(jnp.int32, shape, 0)
+        - lax.broadcasted_iota(jnp.int32, shape, 1)
+    )
+    begun = lax.broadcasted_iota(jnp.int32, shape, 1) + (me - reach) * rows >= 0
+    allowed = (spacing >= 0) & (spacing < WINDOW) & begun & (seg_col[...] == key_seg)
+    bias_ref[...] = jnp.where(allowed, 0.0, NEG_FILL)
+    for d in range(1, reach + 1):
+        kv_send(d).wait_recv()
+    scores = dot32(queries, pair_ref[:, :HD], NT) * (HD ** (-0.5)) + jnp.concatenate(
+        [bias_ref[...]] * NH, axis=0
+    )
+    expo = jnp.exp(scores - jnp.max(scores, axis=-1, keepdims=True))
+    probs = expo / jnp.sum(expo, axis=-1, keepdims=True)
+    heads = dot32(probs.astype(bf), pair_ref[:, HD:], NN).astype(bf)
+    for h in range(NH):
+        att_ref[:, h * HD : (h + 1) * HD] = heads[h * rows : (h + 1) * rows]
+    attn = dot32(att_ref[...], wo_all[...], NN)
+    attn_ref[...] = attn
+    mid = stream + rms_norm(attn, gains[1:2])
+    mid_ref[...] = mid
+    low_ref[...] = rms_norm(mid, gains[2:3]).astype(bf)
+
+    for j in range(4):
+        ffn_got(j, 3 if j < 2 else 1).wait_recv()
+        ffn_pass(j).start()
+    for j in range(4):
+        ffn_got(j, 1 if j < 2 else 3).wait_recv()
+        ffn_got(j, 2).wait_recv()
+    for j in range(4):
+        ffn_pass(j).wait_send()
+        for k in (1, 3):
+            ffn_two(j, k).wait_send()
+    for k in (1, 2, 3):
+        ffn_one(k).wait_send()
+    for d in range(1, reach + 1):
+        seg_send(d).wait_send()
+        kv_send(d).wait_send()
+
+
+def front(qkv_shard, wo_shard, ffn_shard, tokens, seg_rows, seg_col, table, keep):
+    f32, bf = jnp.float32, jnp.bfloat16
     vm = pl.BlockSpec(memory_space=pltpu.VMEM)
+    hbm = pl.BlockSpec(memory_space=pl.ANY)
     dma = pltpu.SemaphoreType.DMA
     q_rows, width = qkv_shard.shape
     o_rows, o_width = wo_shard.shape
+    rows = tokens.shape[0]
+    reach = min(-(-(WINDOW - 1) // rows), lax.axis_size("ctx") - 1)
+    pairs = (reach + 1) * rows
+    shapes = (
+        ((16 * keep, width), bf),
+        ((16 * o_rows, o_width), bf),
+        ((16, *ffn_shard.shape), bf),
+        ((4, D), f32),
+        ((2, HD), f32),
+        ((rows, D), bf),
+        ((rows, width), f32),
+        ((rows, NH * HD), bf),
+        ((pairs, 2 * HD), bf),
+        ((rows, NH * HD), bf),
+        ((rows, D), f32),
+        ((rows, D), f32),
+        ((rows, D), bf),
+        ((rows, pairs), f32),
+        ((rows, HD), f32),
+    )
     return pl.pallas_call(
-        gather_kernel,
-        out_shape=(
-            jax.ShapeDtypeStruct((16 * keep, width), bf),
-            jax.ShapeDtypeStruct((16 * o_rows, o_width), bf),
-            jax.ShapeDtypeStruct((16, q_rows - keep, extra), jnp.float32),
-        ),
-        in_specs=[vm] * 2,
-        out_specs=(vm,) * 3,
+        front_kernel,
+        out_shape=tuple(jax.ShapeDtypeStruct(*s) for s in shapes),
+        in_specs=[vm, vm, hbm, vm, vm, vm, hbm],
+        out_specs=(vm, vm, hbm) + (vm,) * (len(shapes) - 3),
         scratch_shapes=[
             pltpu.VMEM((16 * q_rows, width), bf),
-            dma((2,)),
+            pltpu.VMEM((reach + 1, 8, rows), jnp.int32),
+            dma((4,)),
             dma((4, 2)), dma((4, 2)),
             dma((4, 4, 2)), dma((4, 4, 2)),
             dma((4, 4, 2)), dma((4, 4, 2)),
+            dma((4,)), dma((4,)),
+            dma((4, 4)), dma((4, 4)),
+            dma((reach,)), dma((reach,)),
+            dma((reach,)), dma((reach,)),
         ],
         compiler_params=pltpu.CompilerParams(
-            collective_id=2, has_side_effects=True, vmem_limit_bytes=40 * 1024 * 1024
+            collective_id=2, has_side_effects=True, vmem_limit_bytes=48 * 1024 * 1024
         ),
         cost_estimate=pl.CostEstimate(
-            flops=0, bytes_accessed=64 * (q_rows * width + o_rows * o_width), transcendentals=0
+            flops=6 * rows * width * D, bytes_accessed=64 * q_rows * width, transcendentals=0
         ),
-    )(qkv_shard, wo_shard)
-
-
-def rms_back(values, grad, gain):
-    r = lax.rsqrt(jnp.mean(values * values, axis=-1, keepdims=True) + EPS)
-    n = values * r
-    dyg = grad * gain
-    return (
-        r * (dyg - n * jnp.mean(dyg * n, axis=-1, keepdims=True)),
-        jnp.sum(grad * n, axis=0, keepdims=True),
-    )
-
-
-def stack_heads(values):
-    return jnp.concatenate([values[:, h * HD : (h + 1) * HD] for h in range(NH)], axis=0)
-
-
-def turn_back(grad, cos_table, sin_table):
-    left, right = grad[:, : HD // 2], grad[:, HD // 2 :]
-    return jnp.concatenate(
-        [left * cos_table + right * sin_table, right * cos_table - left * sin_table], axis=1
-    )
+    )(qkv_shard, wo_shard, ffn_shard, tokens, seg_rows, seg_col, table)
 
 
 def back_kernel(
     gff, gn_ref, mid_ref, attn_ref, cot_ref, tok_ref, gains_ref, qk_ref, proj_ref, q_ref,
-    pair_ref, att_ref, normed_ref, qkv_ref, wo_ref, cos_ref, sin_ref, bias_ref, g3_ref,
-    gt_ref, oq_ref, oo_ref, og_ref, ou_ref, od_ref,
-    own_ff, in1_ff, t_ff, in2_ff, all_ff, kv_snd, kv_in, gmid, gpair, gproj, tail,
+    pair_ref, att_ref, normed_ref, qkv_ref, wo_ref, turn_ref, bias_ref, g3_ref,
+    gt_ref, oq_out, tail_out, oo_ref, og_ref, ou_ref, od_ref,
+    oq_ref, own_ff, in1_ff, t_ff, in2_ff, all_ff, kv_snd, kv_in, gmid, gpair, gproj, tail,
     stage, go, dq, do, sq, so, iq1, io1, tq, to, iq2, io2, xq, xo,
     l_sem, s1f, r1f, s2f, r2f, sag, rag, skv, rkv,
     sd, rd, s1, r1, s2, r2, sx, rx, sf, rf,
@@ -623,8 +743,9 @@
         kv_snd[d - 1] = gpair[pl.ds((reach - d) * rows, rows), :].astype(bf)
         kv_send(d).start()
 
-    cos_all = jnp.concatenate([cos_ref[...]] * NH, axis=0)
-    sin_all = jnp.concatenate([sin_ref[...]] * NH, axis=0)
+    cos_table, sin_table = turn_ref[:, : HD // 2], turn_ref[:, HD // 2 :]
+    cos_all = jnp.concatenate([cos_table] * NH, axis=0)
+    sin_all = jnp.concatenate([sin_table] * NH, axis=0)
     grad_queries = dot32(grad_scores, keys, NN) * scale
     grad_q, qk_gain_q = rms_back(
         stack_heads(proj_ref[:, : NH * HD]),
@@ -670,7 +791,7 @@
         total = total + kv_in[d - 1].astype(f32)
     grad_k, qk_gain_k = rms_back(
         proj_ref[:, NH * HD : NH * HD + HD],
-        turn_back(total[:, :HD], cos_ref[...], sin_ref[...]),
+        turn_back(total[:, :HD], cos_table, sin_table),
         qk_ref[1:2, :],
     )
     gproj[:, NH * HD : NH * HD + HD] = grad_k.astype(bf)
@@ -838,6 +959,8 @@
             hop_chip(k, t).wait_send()
         last(t, core).wait_send()
         last(t, 1 - core).wait_recv()
+    oq_out[...] = oq_ref[:keep, :]
+    tail_out[...] = oq_ref[keep:, :]
 
 
 def backward_rest(gff, values, keep, lines):
@@ -865,13 +988,15 @@
         back_kernel,
         out_shape=(
             jax.ShapeDtypeStruct((rows, D), f32),
-            jax.ShapeDtypeStruct((q_rows, width), f32),
+            jax.ShapeDtypeStruct((keep, width), f32),
+            jax.ShapeDtypeStruct((8, width), f32),
             jax.ShapeDtypeStruct((o_rows, o_width), f32),
             weight, weight, weight,
         ),
         in_specs=[hbm] + [vm] * len(values),
-        out_specs=(vm,) * 6,
+        out_specs=(vm,) * 7,
         scratch_shapes=[
+            pltpu.VMEM((q_rows, width), f32),
             ff(4), ff(3, 4), ff(4), ff(3), ff(2 * chips),
             pltpu.VMEM((reach, rows, 2 * HD), bf),
             pltpu.VMEM((reach, rows, 2 * HD), bf),
@@ -915,33 +1040,17 @@
     cotangent,
 ):
     local_len = tokens.shape[1]
-    scale = HD ** (-0.5)
     ctx_index = lax.axis_index("ctx")
+    owner = lax.axis_index("fsdp")
     ctx_size = lax.axis_size("ctx")
     own_rows = gate_weight.shape[0]
     slice_rows = own_rows // ctx_size
     padded = -(-slice_rows // 16) * 16
-    n_gain, n_qk = norm_gains.size, qk_gains.size
-    extra = -(-n_gain // 128) * 128
-    gain_rows = jnp.zeros((8, qkv_weight.shape[1]), jnp.bfloat16)
-    gain_rows = gain_rows.at[0, :n_gain].set(norm_gains.reshape(-1))
-    gain_rows = gain_rows.at[1, :n_qk].set(qk_gains.reshape(-1))
-    qkv_full, out_full, gain_got = gather_attention(
-        jnp.concatenate([qkv_weight, gain_rows], axis=0), out_weight, qkv_weight.shape[0], extra
-    )
-    gains_all = (
-        gain_got[:, 0, :n_gain]
-        .reshape(-1, 4, norm_gains.shape[1])
-        .transpose(1, 0, 2)
-        .reshape(4, D)
-    )
-    qk_all = (
-        gain_got[:, 1, :n_qk]
-        .reshape(-1, 2, qk_gains.shape[1])
-        .transpose(1, 0, 2)
-        .reshape(2, HD)
-    )
-    seg_all = lax.all_gather(segments[0], "ctx", axis=0, tiled=True)
+    keep, width = qkv_weight.shape
+    gain_lines, qk_lines = norm_gains.shape, qk_gains.shape
+    gain_rows = jnp.zeros((8, width), jnp.bfloat16)
+    gain_rows = lax.dynamic_update_slice(gain_rows, norm_gains, (0, owner * gain_lines[1]))
+    gain_rows = lax.dynamic_update_slice(gain_rows, qk_gains, (4, owner * qk_lines[1]))
 
     def my_slice(weight):
         part = lax.dynamic_index_in_dim(
@@ -952,82 +1061,49 @@
     ffn_shard = jnp.concatenate(
         [my_slice(gate_weight), my_slice(up_weight), my_slice(down_weight)], axis=0
     )
-    ffn_full = lax.all_gather(ffn_shard, "fsdp")
-
-    offset = ctx_index * local_len
-    positions = offset + jnp.arange(local_len, dtype=jnp.int32)
-    cos_table, sin_table = rope_tables(positions)
-    stream = tokens.astype(jnp.float32).reshape(local_len, D)
-    flat_normed = rms_norm(stream, gains_all[0]).astype(jnp.bfloat16)
-    projected = jnp.dot(flat_normed, qkv_full, preferred_element_type=jnp.float32)
-    q_raw = projected[:, : NH * HD].reshape(local_len, NH, HD)
-    k_raw = projected[:, NH * HD : NH * HD + HD]
-    values = projected[:, NH * HD + HD :].astype(jnp.bfloat16)
-    prep_fixed = partial(head_prep, cos_table=cos_table, sin_table=sin_table)
-    q_rot, k_rot = prep_fixed(q_raw, k_raw, qk_all[0], qk_all[1])
-    queries = q_rot.astype(jnp.bfloat16)
-    own_pair = jnp.concatenate([k_rot.astype(jnp.bfloat16), values], axis=-1)
-    reach = min(-(-(WINDOW - 1) // local_len), ctx_size - 1)
-    pieces = [own_pair]
-    for distance in range(1, reach + 1):
-        pieces.insert(0, from_behind(own_pair, "ctx", distance))
-    pair_all = jnp.concatenate(pieces, axis=0)
-    key_all = pair_all[:, :HD]
-    value_all = pair_all[:, HD:]
-    key_index = offset - reach * local_len + jnp.arange((reach + 1) * local_len, dtype=jnp.int32)
-    seg_padded = jnp.concatenate([jnp.full((reach * local_len,), -1, jnp.int32), seg_all])
-    key_seg = lax.dynamic_slice_in_dim(seg_padded, offset, (reach + 1) * local_len, 0)
-    spacing = positions[:, None] - key_index[None, :]
-    allowed = (
-        (spacing >= 0) & (spacing < WINDOW) & (segments[0][:, None] == key_seg[None, :])
-    )
-    raw_scores = (
-        jnp.einsum("qhd,kd->hqk", queries, key_all, preferred_element_type=jnp.float32) * scale
-    )
-    scores = jnp.where(allowed[None], raw_scores, NEG_FILL)
-    top_score = jnp.max(scores, axis=-1, keepdims=True)
-    expo = jnp.exp(scores - top_score)
-    probs = expo / jnp.sum(expo, axis=-1, keepdims=True)
-    probs_low = probs.astype(jnp.bfloat16)
-    attended = (
-        jnp.einsum("hqk,kd->qhd", probs_low, value_all, preferred_element_type=jnp.float32)
-        .astype(jnp.bfloat16)
-        .reshape(local_len, NH * HD)
-    )
-    attn = jnp.dot(attended, out_full, preferred_element_type=jnp.float32)
-    mid_stream = stream + rms_norm(attn, gains_all[1])
-    normed_two = rms_norm(mid_stream, gains_all[2]).astype(jnp.bfloat16)
-
+    places = np.arange(ctx_size * local_len, dtype=np.float32)
+    rates = (ROPE_BASE ** (-(2.0 * np.arange(HD // 2)) / HD)).astype(np.float32)
+    angles = (places[:, None] * rates).astype(np.float64)
+    table = jnp.asarray(
+        np.concatenate([np.cos(angles), np.sin(angles)], axis=1)
+        .astype(np.float32)
+        .reshape(ctx_size, local_len, HD)
+    )
+    flat = tokens.reshape(local_len, D)
     cot = cotangent.reshape(local_len, D)
+    (
+        qkv_full, out_full, ffn_full, gains_all, qk_all, normed, projected, queries, pair_all,
+        attended, attn, mid, normed_two, bias, turn_table,
+    ) = front(
+        jnp.concatenate([qkv_weight, gain_rows], axis=0),
+        out_weight,
+        ffn_shard,
+        flat,
+        jnp.broadcast_to(segments, (8, local_len)),
+        segments.reshape(local_len, 1),
+        table,
+        keep,
+    )
     output, grad_normed_two, grad_gain_three, ffn_grads = ffn(
-        normed_two, mid_stream, cot, gains_all[3:4], ffn_full
-    )
-    bias = jnp.where(allowed, 0.0, NEG_FILL)
-    keep = qkv_weight.shape[0]
-    grad_tokens, own_qkv, total_out, total_gate, total_up, total_down = backward_rest(
+        normed_two, mid, cot, gains_all, ffn_full
+    )
+    grad_tokens, total_qkv, tail, total_out, total_gate, total_up, total_down = backward_rest(
         ffn_grads,
         (
-            grad_normed_two, mid_stream, attn, cot, tokens.reshape(local_len, D), gains_all,
-            qk_all, projected, queries.reshape(local_len, NH * HD), pair_all, attended,
-            flat_normed, qkv_full, out_full, cos_table, sin_table, bias, grad_gain_three,
+            grad_normed_two, mid, attn, cot, flat, gains_all, qk_all, projected, queries,
+            pair_all, attended, normed, qkv_full, out_full, turn_table, bias, grad_gain_three,
         ),
         keep,
         own_rows,
     )
-    owner = lax.axis_index("fsdp")
-    gain_lines, qk_lines = norm_gains.shape, qk_gains.shape
-    total_gains = lax.dynamic_slice(
-        own_qkv[keep : keep + 4, :D], (0, owner * gain_lines[1]), gain_lines
-    )
-    total_qk = lax.dynamic_slice(
-        own_qkv[keep + 4 : keep + 6, :HD], (0, owner * qk_lines[1]), qk_lines
-    )
+    total_gains = lax.dynamic_slice(tail[:4, :D], (0, owner * gain_lines[1]), gain_lines)
+    total_qk = lax.dynamic_slice(tail[4:6, :HD], (0, owner * qk_lines[1]), qk_lines)
     return (
         output.reshape(tokens.shape),
         grad_tokens.reshape(tokens.shape),
         total_gains,
         total_qk,
-        own_qkv[:keep],
+        total_qkv,
         total_out,
         total_gate,
         total_up,

time: 325 us -> 307 us (0.945)
  Pallas kernels: 236 us -> 270 us
  between operations: 14.5 us -> 0.83 us
  starting transfers between devices: 11 us -> 0 us
  other arithmetic: 9.7 us -> 0.99 us
  blocking collectives: 8.13 us -> 0 us
  matrix products: 5.03 us -> 0 us
  local copies, waits for them, and re-layouts: 35.2 us -> 30.7 us
    pallas_call x1, Pallas kernels: 37.9 us -> 74.7 us  [front(): pl.pallas_call(front_kernel, out_shape=tuple((jax.ShapeDtypeStruct(*s) fo...]
    ppermute x4 -> x0, starting transfers between devices: 10.9 us -> none  [from_behind(): return lax.ppermute(array, axis, pairs)]
    all_gather x1 -> x0, blocking collectives: 8.13 us -> none  [on_device(): seg_all = lax.all_gather(segments[0], 'ctx', axis=0, tiled=True)]
    slice x10 -> x2, local copies, waits for them, and re-layouts: 8.18 us -> 1.62 us  [the longest x1 0.85 us: on_device(): tail[4:6, :HD]]
    unnamed x66 -> x47, local copies, waits for them, and re-layouts: 14.6 us -> 19.7 us
    dot_general x3 -> x0, matrix products: 3.46 us -> none  [the longest x1 2.16 us: on_device(): jnp.einsum('hqk,kd->qhd', probs_low, value_all, preferred_element_type=jn...]
    dynamic_update_slice x0 -> x2, local copies, waits for them, and re-layouts: none -> 3.3 us  [the longest x1 1.66 us: on_device(): lax.dynamic_update_slice(gain_rows, qk_gains, (4, owner * qk_lines[1]))]
  transfers between devices with their start and end apart: 5 -> 0, of which waited for: 0 -> 0; matrix products, arithmetic and copies ran while one was open for 9% -> 0% of each run, Pallas kernels for 12% -> 0%
where the time goes in v5:
time: 307 us; the launch traced here: 303 us
  Pallas kernels  270 us (88%)
  local copies, waits for them, and re-layouts  30.7 us (10%)
    pallas_call x1, Pallas kernels, backward_rest(): pl.pallas_call(back_kernel, out_shape=(jax.ShapeDtypeStruct((rows, D), f3...  112 us
    pallas_call x1, Pallas kernels, ffn(): pl.pallas_call(ffn_kernel, out_shape=(jax.ShapeDtypeStruct((rows, D), bf)...  83.4 us
    pallas_call x1, Pallas kernels, front(): pl.pallas_call(front_kernel, out_shape=tuple((jax.ShapeDtypeStruct(*s) fo...  74.7 us
    unnamed x47, local copies, waits for them, and re-layouts  19.7 us

profile of v5, /device:TPU:73, one launch (start us, length us, event | category | flops | bytes accessed | tf_op | source)
XLA Modules:
  0.0 302.7 jit_solution(12645878279831989108)
XLA Ops:
  0.7 0.7 broadcast_in_dim.12.seg_ref
  1.4 1.6 dynamic_update_slice.6
  3.0 1.7 dynamic_update_slice.7
  4.7 0.8 copy.21.seg_col
  5.5 1.0 pad_maximum_fusion.qkv_ref
  6.4 1.5 reshape.42
  8.2 1.5 reshape.44
  9.9 74.7 %shard_map.178 = (bf16[1152,1536]{1,0:T(8,128)(2,1)}, bf16[1024,1152]{1,0:T(8,128)(2,1)}, bf16[16,192,1152]{2,1,0:T(8,128)(2,1)}, f32[4,1152]{1,0:T(4,128)S(1)},...) custom-call(bf16[80,1536]{1,0:T(8,128)(2,1)S(1)} %pad_maximum_fusion, ...), custom_call_target="tpu_custom_call" | custom-call | flops 1358954496 | bytes 7864320 | tf_op jit(solution)/shard_map/pallas_call | solution.py:592
  84.6 0.9 copy-done
  85.5 0.8 copy-done.1
  86.3 0.8 copy-done.2
  87.1 0.8 copy-done.3
  89.4 0.7 copy-done.7
  93.4 83.4 %shard_map.179 = (bf16[128,1152]{1,0:T(8,128)(2,1)}, f32[128,1152]{1,0:T(8,128)}, f32[1,1152]{1,0:T(1,128)}, bf16[16,192,1152]{2,1,0:T(8,128)(2,1)}) custom-call(bf16[128,1152]{1,0:T(8,128)(2,1)} %copy-done.13, f32[128,1152]{1,0:T(8,128)} %copy-done.3, bf16[128,1152]{1,0:T(8,128)(2,1)} %bitcast.16, f32[4,1152]{1,0:T(4,128)} %copy-done.10, ...), custom_call_target="tpu_custom_call" | custom-call | flops 21743271936 | bytes 16515072 | tf_op jit(solution)/shard_map/pallas_call | solution.py:215
  176.8 112.0 %shard_map.180 = (f32[128,1152]{1,0:T(8,128)}, f32[72,1536]{1,0:T(8,128)}, f32[8,1536]{1,0:T(8,128)}, f32[64,1152]{1,0:T(8,128)}, f32[432,1152]{1,0:T(8,128)}, /*index=5*/f32[432,1152]{1,0:T(8,128)}, f32[432,1152]{1,0:T(8,128)}) custom-call(bf16[16,192,1152]{2,1,0:T(8,128)(2,1)} %get-tuple-element.40.gff, f32[128,1152]{1,0:T(8,128)} %get-tuple-element.41.gn_ref, ...), custom_call_target="tpu_custom_call" | custom-call | flops 2717908992 | bytes 14155776 | tf_op jit(solution)/shard_map/pallas_call | solution.py:987
  288.8 0.9 slice.7
  289.7 0.8 slice.6
  292.4 1.9 copy.32
  294.4 1.8 copy.33
  296.9 1.3 copy.35
  298.2 1.0 copy-done.15
  299.2 1.3 copy.36
  300.4 1.0 copy-done.14
  301.4 1.3 copy.37
  (42 shorter events, 7.8 us)
Async XLA Ops:
  0.6 7.3 %copy-start.17 = (bf16[432,1152]{1,0:T(8,128)(2,1)S(1)}, bf16[432,1152]{1,0:T(8,128)(2,1)}, u32[]{:S(2)}) copy-start(bf16[432,1152]{1,0:T(8,128)(2,1)} %param.17) | copy-start | bytes 2985988
  8.2 1.6 copy-start.5
  8.2 1.6 copy-start.12
  84.6 0.9 copy-start
  85.5 0.8 copy-start.1
  86.3 0.8 copy-start.2
  87.1 0.8 copy-start.3
  88.0 0.7 copy-start.4
  88.7 0.7 copy-start.6
  89.4 0.7 copy-start.7
  90.1 0.7 copy-start.8
  90.8 0.7 copy-start.9
  91.5 0.6 copy-start.10
  92.1 0.6 copy-start.11
  92.6 0.7 copy-start.13
  176.8 115.0 %copy-start.18 = (bf16[128,1152]{1,0:T(8,128)(2,1)S(1)}, bf16[128,1152]{1,0:T(8,128)(2,1)}, u32[]{:S(2)}) copy-start(bf16[128,1152]{1,0:T(8,128)(2,1)} %get-tuple-element.39) | copy-start | bytes 884740
  288.8 7.4 %copy-start.19 = (f32[64,1152]{1,0:T(8,128)S(1)}, f32[64,1152]{1,0:T(8,128)}, u32[]{:S(2)}) copy-start(f32[64,1152]{1,0:T(8,128)} %get-tuple-element.77) | copy-start | bytes 884740
  288.8 8.1 %copy-start.16 = (f32[432,1152]{1,0:T(8,128)S(1)}, f32[432,1152]{1,0:T(8,128)}, u32[]{:S(2)}) copy-start(f32[432,1152]{1,0:T(8,128)} %get-tuple-element.78) | copy-start | bytes 5971972
  296.9 2.3 copy-start.15
  299.1 2.3 copy-start.14

commit v6 on v5

--- a/solution.py
+++ b/solution.py
@@ -88,17 +88,33 @@
     def spread(buf, ph):
         own = buf.at[mine(0)]
         got = {}
-        for k in (1, 3, 2):
+        for k in (1, 3):
             back = 4 - k
             got[back] = send(own, buf.at[mine(back)], ag_s.at[ph, k], ag_r.at[ph, back], chips[k])
         got[0] = send(own, buf.at[other(0)], ag_s.at[ph, 0], ag_r.at[ph, 0], partner)
         return got
 
+    def half_of(k, h, offset=0):
+        return pl.ds(k * 2 * rows + offset + h * (rows // 2), rows // 2)
+
     def relay(buf, ph, got, k):
         got[k].wait_recv()
+        h = 0 if k == 3 else 1
+        got[2, h] = send(
+            buf.at[half_of(k, h)], buf.at[half_of(2, h)],
+            ag_s.at[ph, 2 + 2 * h], ag_r.at[ph, 2 + 2 * h], chips[4 - k],
+        )
         got[k] = send(
             buf.at[mine(k)], buf.at[other(k)], ag_s.at[ph, 4 + k], ag_r.at[ph, 4 + k], partner
         )
+
+    def relay_far(buf, ph, got):
+        for h in (0, 1):
+            got[2, h].wait_recv()
+            got[2, h] = send(
+                buf.at[half_of(2, h)], buf.at[half_of(2, h, rows)],
+                ag_s.at[ph, 6 + 2 * h], ag_r.at[ph, 6 + 2 * h], partner,
+            )
 
     def sum_out(ph, k):
         d2d_snd[ph, k] = part[pl.ds(rows, rows), :].astype(jnp.bfloat16)
@@ -127,8 +143,11 @@
                 relay(buf, ph, got, 1)
                 relay(buf, ph, got, 3)
             if k == 2:
-                relay(buf, ph, got, 2)
-            got[k].wait_recv()
+                relay_far(buf, ph, got)
+                got[2, 0].wait_recv()
+                got[2, 1].wait_recv()
+            else:
+                got[k].wait_recv()
             work(k)
             sums[k] = sum_out(ph, k)
         return sums
@@ -240,12 +259,12 @@
             pltpu.VMEM((2, 3, rows, D), bf),
             pltpu.VMEM(weights.shape, bf),
             dma((3, owners)), dma,
-            dma((2, 8)), dma((2, 8)),
+            dma((2, 10)), dma((2, 10)),
             dma((2, 4)), dma((2, 4)),
             dma((2, 4)), dma((2, 4)),
         ],
         compiler_params=pltpu.CompilerParams(
-            collective_id=1, has_side_effects=True, vmem_limit_bytes=58 * 1024 * 1024
+            collective_id=1, has_side_effects=True, vmem_limit_bytes=62 * 1024 * 1024
         ),
         cost_estimate=pl.CostEstimate(
             flops=18 * seq_rows * units * D, bytes_accessed=14 * units * D, transcendentals=0
@@ -607,7 +626,7 @@
             dma((reach,)), dma((reach,)),
         ],
         compiler_params=pltpu.CompilerParams(
-            collective_id=2, has_side_effects=True, vmem_limit_bytes=48 * 1024 * 1024
+            collective_id=2, has_side_effects=True, vmem_limit_bytes=62 * 1024 * 1024
         ),
         cost_estimate=pl.CostEstimate(
             flops=6 * rows * width * D, bytes_accessed=64 * q_rows * width, transcendentals=0
@@ -617,11 +636,11 @@
 
 def back_kernel(
     gff, gn_ref, mid_ref, attn_ref, cot_ref, tok_ref, gains_ref, qk_ref, proj_ref, q_ref,
-    pair_ref, att_ref, normed_ref, qkv_ref, wo_ref, turn_ref, bias_ref, g3_ref,
-    gt_ref, oq_out, tail_out, oo_ref, og_ref, ou_ref, od_ref,
-    oq_ref, own_ff, in1_ff, t_ff, in2_ff, all_ff, kv_snd, kv_in, gmid, gpair, gproj, tail,
+    pair_ref, att_ref, normed_ref, turn_ref, bias_ref, g3_ref, qkv_hbm, wo_hbm,
+    gt_ref, oq_out, tail_out, oo_ref, all_ff,
+    qkv_ref, wo_ref, oq_ref, own_ff, far_own, far_in, in1_ff, t_ff, in2_ff, kv_snd, kv_in, gmid, gpair, gproj, tail,
     stage, go, dq, do, sq, so, iq1, io1, tq, to, iq2, io2, xq, xo,
-    l_sem, s1f, r1f, s2f, r2f, sag, rag, skv, rkv,
+    l_sem, sfar, rfar, s1f, r1f, s2f, r2f, sag, rag, skv, rkv,
     sd, rd, s1, r1, s2, r2, sx, rx, sf, rf,
 ):
     y, z, chip, core = place()
@@ -658,10 +677,22 @@
     def o_lines(half):
         return pl.ds(pl.multiple_of(half * o_half, 16), o_half)
 
+    def line(k):
+        return lax.rem(a + k, 4)
+
     own_loads = [
         pltpu.make_async_copy(gff.at[block(a, j)], own_ff.at[j], l_sem.at[j]) for j in range(4)
+    ] + [
+        pltpu.make_async_copy(
+            gff.at[block(line(1 if j < 2 else 3), j)], far_own.at[j], l_sem.at[4 + j]
+        )
+        for j in range(4)
     ]
-    for copy in own_loads:
+    weight_loads = [
+        pltpu.make_async_copy(wo_hbm, wo_ref, l_sem.at[8]),
+        pltpu.make_async_copy(qkv_hbm, qkv_ref, l_sem.at[9]),
+    ]
+    for copy in own_loads + weight_loads:
         copy.start()
     greet(
         [first_peer(k) for k in (1, 2, 3)]
@@ -669,15 +700,32 @@
         + [member(k) for k in range(1, members)]
     )
 
-    def ff_one(k, j):
+    def ff_far(j):
+        k = 1 if j < 2 else 3
         return remote(
-            gff.at[block(lax.rem(a + k, 4), j)], in1_ff.at[3 - k, j],
-            s1f.at[k, j], r1f.at[4 - k, j], first_peer(k),
-        )
-
-    for i in (2, 1, 3, 0):
-        for k in (1, 3, 2):
-            ff_one(k, lax.rem(b + i, 4)).start()
+            gff.at[block(line(2), j)], far_in.at[j], sfar.at[j], rfar.at[j], first_peer(k)
+        )
+
+    def ff_near(k, j):
+        side = 0 if k == 1 else 1
+        direct = (j >= 2) == (k == 1)
+        src = gff.at[block(line(k), j)] if direct else far_own.at[j]
+        return remote(src, in1_ff.at[side, j], s1f.at[side, j], r1f.at[side, j], first_peer(k))
+
+    for j in (0, 2, 1, 3):
+        ff_far(j).start()
+    for k, j in ((1, 2), (3, 0), (1, 3), (3, 1)):
+        ff_near(k, j).start()
+
+    def pass_far(js):
+        for j in js:
+            ff_far(j).wait_recv()
+            own_loads[4 + j].wait()
+            far_own[j] = (far_own[j].astype(f32) + far_in[j].astype(f32)).astype(bf)
+            ff_near(1 if j < 2 else 3, j).start()
+
+    for copy in weight_loads[:1]:
+        copy.wait()
 
     grad_final = cot_ref[...].astype(f32)
     part, gain_two = rms_back(mid_ref[...], gn_ref[...], gains_ref[2:3, :])
@@ -698,9 +746,9 @@
 
     def away(i, t):
         k, j = lax.rem(i // 4 + 1, 4), lax.rem(i, 4)
-        line = lax.rem(b + k, 4)
-        f = block_there(line, j)
-        slot = line * 4 + j
+        there = lax.rem(b + k, 4)
+        f = block_there(there, j)
+        slot = there * 4 + j
         if t == 0:
             src, dst = stage.at[f, :, q_cols(1 - core)], dq.at[slot]
         else:
@@ -743,6 +791,7 @@
         kv_snd[d - 1] = gpair[pl.ds((reach - d) * rows, rows), :].astype(bf)
         kv_send(d).start()
 
+    pass_far((0, 2))
     cos_table, sin_table = turn_ref[:, : HD // 2], turn_ref[:, HD // 2 :]
     cos_all = jnp.concatenate([cos_table] * NH, axis=0)
     sin_all = jnp.concatenate([sin_table] * NH, axis=0)
@@ -757,17 +806,15 @@
 
     def hop_one(k, t):
         src, dst = ((sq, iq1), (so, io1))[t]
-        line = pl.ds(lax.rem(a + k, 4) * 4, 4)
         return remote(
-            src.at[line], dst.at[3 - k], s1.at[k, t], r1.at[4 - k, t], first_peer(k)
+            src.at[pl.ds(line(k) * 4, 4)], dst.at[3 - k], s1.at[k, t], r1.at[4 - k, t], first_peer(k)
         )
 
     def fold_cores(t):
         for k in (1, 2, 3, 0):
             def add(j, carry, k=k):
-                line = lax.rem(a + k, 4)
-                slot = line * 4 + j
-                f = block(line, j)
+                slot = line(k) * 4 + j
+                f = block(line(k), j)
                 home((k + 3) % 4 * 4 + j, t).wait_recv()
                 if t == 0:
                     sq[slot] = (
@@ -783,7 +830,7 @@
             if k:
                 hop_one(k, t).start()
 
-    fold_cores(1)
+    pass_far((1, 3))
 
     total = gpair[pl.ds(reach * rows, rows), :]
     for d in range(1, reach + 1):
@@ -796,12 +843,14 @@
     )
     gproj[:, NH * HD : NH * HD + HD] = grad_k.astype(bf)
     gproj[:, NH * HD + HD :] = total[:, HD:].astype(bf)
+    for copy in weight_loads[1:]:
+        copy.wait()
     stream = tok_ref[...].astype(f32)
     grad_in, gain_zero = rms_back(stream, dot32(gproj[...], qkv_ref[...], NT), gains_ref[0:1, :])
     gt_ref[...] = gmid[...] + grad_in
     tail[...] = jnp.zeros_like(tail)
-    for i, line in enumerate((gain_zero, gain_one, gain_two, g3_ref[...])):
-        tail[i : i + 1, :D] = line
+    for i, total_gain in enumerate((gain_zero, gain_one, gain_two, g3_ref[...])):
+        tail[i : i + 1, :D] = total_gain
     tail[4:5, :HD] = qk_gain_q
     tail[5:6, :HD] = qk_gain_k
 
@@ -817,9 +866,8 @@
 
     lax.fori_loop(0, width // 256, qkv_tile, 0)
     start_away(0)
-    fold_cores(0)
-
-    for copy in own_loads:
+
+    for copy in own_loads[:4]:
         copy.wait()
 
     def ff_two(k):
@@ -829,21 +877,68 @@
 
     for k in (2, 1, 3, 0):
         j = lax.rem(b + k, 4)
-        for m in (1, 2, 3):
-            dst = in1_ff.at[m - 1, j]
+        for m in (0, 1):
+            dst = in1_ff.at[m, j]
             remote(dst, dst, s1f.at[m, j], r1f.at[m, j], partner).wait_recv()
         total = own_ff[j].astype(f32)
-        for m in range(3):
+        for m in (0, 1):
             total = total + in1_ff[m, j].astype(f32)
         t_ff[j] = total.astype(bf)
         if k:
             ff_two(k).start()
 
+    fold_cores(1)
+    fold_cores(0)
+
     def hop_two(k, t):
         src, dst = ((tq, iq2), (to, io2))[t]
         return remote(
             src.at[lax.rem(b + k, 4)], dst.at[3 - k], s2.at[k, t], r2.at[4 - k, t], second_peer(k)
         )
+
+    for k in (1, 3, 2):
+        ff_two(4 - k).wait_recv()
+    total = t_ff[b].astype(f32)
+    for m in range(3):
+        total = total + in2_ff[m].astype(f32)
+    all_ff[me] = total.astype(bf)
+
+    half = all_ff.shape[1] // 2
+
+    def ff_slot(k, there=0):
+        return lax.rem(chip + k, chips) * 2 + (1 - core if there else core)
+
+    def ff_all(k):
+        peer = chip_peer(k) if k else partner
+        return remote(
+            all_ff.at[me], all_ff.at[me], sag.at[k], rag.at[(chips - k) % chips], peer
+        )
+
+    def ff_from(k):
+        dst = all_ff.at[ff_slot(k)]
+        return remote(dst, dst, sag.at[k], rag.at[k], partner)
+
+    def ff_half(k, h, there=0):
+        return all_ff.at[ff_slot(k, there), pl.ds(h * half, half), :]
+
+    def ff_on(k):
+        h = 0 if k == 3 else 1
+        dst = ff_half(k, h)
+        return remote(dst, dst, sag.at[8 + h], rag.at[8 + h], chip_peer(4 - k))
+
+    def ff_far_got(h):
+        dst = ff_half(2, h)
+        return remote(dst, dst, sag.at[8 + h], rag.at[8 + h], partner)
+
+    def ff_cross(k, h=None, there=0):
+        if h is None:
+            dst, i = all_ff.at[ff_slot(k, there)], 4 + k
+        else:
+            dst, i = ff_half(2, h, there), 10 + h
+        return remote(dst, dst, sag.at[i], rag.at[i], partner)
+
+    for k in (1, 3, 0):
+        ff_all(k).start()
 
     for t in (1, 0):
         own, got, dst = ((sq, iq1, tq), (so, io1, to))[t]
@@ -858,33 +953,10 @@
             if k:
                 hop_two(k, t).start()
 
-    for k in (1, 3, 2):
-        ff_two(4 - k).wait_recv()
-    total = t_ff[b].astype(f32)
-    for m in range(3):
-        total = total + in2_ff[m].astype(f32)
-    all_ff[me] = total.astype(bf)
-
-    def ff_all(k):
-        peer = chip_peer(k) if k else partner
-        return remote(
-            all_ff.at[me], all_ff.at[me], sag.at[k], rag.at[(chips - k) % chips], peer
-        )
-
-    def ff_from(k):
-        dst = all_ff.at[lax.rem(chip + k, chips) * 2 + core]
-        return remote(dst, dst, sag.at[chips + k], rag.at[k], partner)
-
-    def ff_cross(k):
-        dst = all_ff.at[lax.rem(chip + k, chips) * 2 + core]
-        return remote(dst, dst, sag.at[chips + k], rag.at[chips + k], partner)
-
-    def ff_crossed(k):
-        dst = all_ff.at[lax.rem(chip + k, chips) * 2 + 1 - core]
-        return remote(dst, dst, sag.at[k], rag.at[chips + k if k else 0], partner)
-
-    for k in (*range(1, chips), 0):
-        ff_all(k).start()
+    for k in (1, 3):
+        ff_from(k).wait_recv()
+        ff_on(k).start()
+        ff_cross(k).start()
 
     def hop_chip(k, t):
         buf = (xq, xo)[t]
@@ -907,9 +979,9 @@
         part = (oq_ref.at[:, q_cols(half)], oo_ref.at[o_lines(half), :])[t]
         return remote(part, part, sf.at[t], rf.at[t], partner)
 
-    for k in range(1, chips):
-        ff_from(k).wait_recv()
-        ff_cross(k).start()
+    for h in (0, 1):
+        ff_far_got(h).wait_recv()
+        ff_cross(2, h).start()
 
     for t in (1, 0):
         buf = (xq, xo)[t]
@@ -925,15 +997,12 @@
             oo_ref[o_lines(core), :] = total
         last(t, core).start()
 
-    for k in range(chips):
-        ff_crossed(k).wait_recv()
-    lines = og_ref.shape[0] // members
-    share = all_ff.shape[1] // 3
-    for i, dst in enumerate((og_ref, ou_ref, od_ref)):
-        for m in range(members):
-            dst[m * lines : (m + 1) * lines, :] = all_ff[
-                m, i * share : (i + 1) * share, :
-            ].astype(f32)[:lines]
+    everywhere = all_ff.at[ff_slot(0, 1)]
+    remote(everywhere, everywhere, sag.at[0], rag.at[0], partner).wait_recv()
+    for k in (1, 3):
+        ff_cross(k, there=1).wait_recv()
+    for h in (0, 1):
+        ff_cross(2, h, there=1).wait_recv()
 
     def end_away(i, carry):
         for t in (0, 1):
@@ -941,16 +1010,21 @@
         return carry
 
     lax.fori_loop(0, 16, end_away, 0)
+    for j in range(4):
+        ff_far(j).wait_send()
+        ff_near(1, j).wait_send()
+        ff_near(3, j).wait_send()
     for k in (1, 2, 3):
-        for j in range(4):
-            ff_one(k, j).wait_send()
         ff_two(k).wait_send()
     for d in range(1, reach + 1):
         kv_send(d).wait_send()
-    for k in range(chips):
+    for k in (1, 3, 0):
         ff_all(k).wait_send()
-        if k:
-            ff_cross(k).wait_send()
+    for k in (1, 3):
+        ff_on(k).wait_send()
+        ff_cross(k).wait_send()
+    for h in (0, 1):
+        ff_cross(2, h).wait_send()
     for t in (0, 1):
         for k in (1, 2, 3):
             hop_one(k, t).wait_send()
@@ -963,7 +1037,7 @@
     tail_out[...] = oq_ref[keep:, :]
 
 
-def backward_rest(gff, values, keep, lines):
+def backward_rest(gff, values, weights, keep):
     f32, bf = jnp.float32, jnp.bfloat16
     vm = pl.BlockSpec(memory_space=pltpu.VMEM)
     hbm = pl.BlockSpec(memory_space=pl.ANY)
@@ -983,7 +1057,6 @@
     def ff(*lead):
         return pltpu.VMEM(lead + (ff_rows, D), bf)
 
-    weight = jax.ShapeDtypeStruct((lines, D), f32)
     return pl.pallas_call(
         back_kernel,
         out_shape=(
@@ -991,13 +1064,15 @@
             jax.ShapeDtypeStruct((keep, width), f32),
             jax.ShapeDtypeStruct((8, width), f32),
             jax.ShapeDtypeStruct((o_rows, o_width), f32),
-            weight, weight, weight,
+            jax.ShapeDtypeStruct((2 * chips, ff_rows, D), bf),
         ),
-        in_specs=[hbm] + [vm] * len(values),
-        out_specs=(vm,) * 7,
+        in_specs=[hbm] + [vm] * len(values) + [hbm] * 2,
+        out_specs=(vm,) * 5,
         scratch_shapes=[
+            pltpu.VMEM((16 * keep, width), bf),
+            pltpu.VMEM((16 * o_rows, o_width), bf),
             pltpu.VMEM((q_rows, width), f32),
-            ff(4), ff(3, 4), ff(4), ff(3), ff(2 * chips),
+            ff(4), ff(4), ff(4), ff(2, 4), ff(4), ff(3),
             pltpu.VMEM((reach, rows, 2 * HD), bf),
             pltpu.VMEM((reach, rows, 2 * HD), bf),
             pltpu.VMEM((rows, D), f32),
@@ -1007,10 +1082,11 @@
             pltpu.VMEM((16, q_rows, width), bf),
             pltpu.VMEM((16, o_rows, o_width), bf),
             *two(16), *two(16), *two(3, 4), *two(4), *two(3), *two(chips),
-            dma((4,)),
-            dma((4, 4)), dma((4, 4)),
+            dma((10,)),
             dma((4,)), dma((4,)),
-            dma((2 * chips,)), dma((2 * chips,)),
+            dma((2, 4)), dma((2, 4)),
+            dma((4,)), dma((4,)),
+            dma((12,)), dma((12,)),
             dma((reach,)), dma((reach,)),
             dma((16, 2)), dma((16, 2)),
             dma((4, 2)), dma((4, 2)),
@@ -1024,7 +1100,61 @@
         cost_estimate=pl.CostEstimate(
             flops=12 * rows * width * D, bytes_accessed=64 * ff_rows * D, transcendentals=0
         ),
-    )(gff, *values)
+    )(gff, *values, *weights)
+
+
+def finish_kernel(
+    all_hbm, gt_hbm, oq_hbm, oo_hbm, out_hbm,
+    og, ou, od, gt, oq, oo, out,
+    buf, wide, i_sem, o_sem,
+):
+    through = [
+        pltpu.make_async_copy(src, dst, o_sem.at[3 + i])
+        for i, (src, dst) in enumerate(((gt_hbm, gt), (oq_hbm, oq), (oo_hbm, oo), (out_hbm, out)))
+    ]
+    members = buf.shape[0]
+    share = buf.shape[1] // 3
+    lines = wide.shape[1] // members
+    loads = [
+        pltpu.make_async_copy(
+            all_hbm.at[:, pl.ds(i * share, share), :],
+            buf.at[:, pl.ds(i * share, share), :],
+            i_sem.at[i],
+        )
+        for i in range(3)
+    ]
+    for copy in loads + through:
+        copy.start()
+    stores = []
+    for i, dst in enumerate((og, ou, od)):
+        loads[i].wait()
+        for m in range(members):
+            wide[i, m * lines : (m + 1) * lines, :] = buf[
+                m, i * share : (i + 1) * share, :
+            ].astype(jnp.float32)[:lines]
+        store = pltpu.make_async_copy(wide.at[i], dst, o_sem.at[i])
+        store.start()
+        stores.append(store)
+    for copy in through + stores:
+        copy.wait()
+
+
+def finish(all_ff, lines, *rest):
+    hbm = pl.BlockSpec(memory_space=pl.ANY)
+    weight = jax.ShapeDtypeStruct((lines, D), jnp.float32)
+    return pl.pallas_call(
+        finish_kernel,
+        out_shape=(weight,) * 3 + tuple(jax.ShapeDtypeStruct(r.shape, r.dtype) for r in rest),
+        in_specs=[hbm] * (1 + len(rest)),
+        out_specs=(hbm,) * (3 + len(rest)),
+        scratch_shapes=[
+            pltpu.VMEM(all_ff.shape, all_ff.dtype),
+            pltpu.VMEM((3, lines, D), jnp.float32),
+            pltpu.SemaphoreType.DMA((3,)),
+            pltpu.SemaphoreType.DMA((3 + len(rest),)),
+        ],
+        compiler_params=pltpu.CompilerParams(vmem_limit_bytes=62 * 1024 * 1024),
+    )(all_ff, *rest)
 
 
 def on_device(
@@ -1048,14 +1178,19 @@
     padded = -(-slice_rows // 16) * 16
     keep, width = qkv_weight.shape
     gain_lines, qk_lines = norm_gains.shape, qk_gains.shape
-    gain_rows = jnp.zeros((8, width), jnp.bfloat16)
-    gain_rows = lax.dynamic_update_slice(gain_rows, norm_gains, (0, owner * gain_lines[1]))
-    gain_rows = lax.dynamic_update_slice(gain_rows, qk_gains, (4, owner * qk_lines[1]))
+    def placed(lines):
+        count, own = lines.shape
+        room = (lax.axis_size("fsdp") - 1) * own
+        padded_lines = jnp.pad(lines, ((0, 0), (room, room)))
+        spread = lax.dynamic_slice(padded_lines, (0, room - owner * own), (count, room + own))
+        return jnp.pad(spread, ((0, 0), (0, width - room - own)))
+
+    gain_rows = jnp.concatenate(
+        [placed(norm_gains), placed(qk_gains), jnp.zeros((2, width), jnp.bfloat16)], axis=0
+    )
 
     def my_slice(weight):
-        part = lax.dynamic_index_in_dim(
-            weight.reshape(ctx_size, slice_rows, D), ctx_index, 0, False
-        )
+        part = lax.dynamic_slice(weight, (ctx_index * slice_rows, 0), (slice_rows, D))
         return jnp.pad(part, ((0, padded - slice_rows), (0, 0)))
 
     ffn_shard = jnp.concatenate(
@@ -1087,17 +1222,20 @@
     output, grad_normed_two, grad_gain_three, ffn_grads = ffn(
         normed_two, mid, cot, gains_all, ffn_full
     )
-    grad_tokens, total_qkv, tail, total_out, total_gate, total_up, total_down = backward_rest(
+    grad_tokens, total_qkv, tail, total_out, all_ff = backward_rest(
         ffn_grads,
         (
             grad_normed_two, mid, attn, cot, flat, gains_all, qk_all, projected, queries,
-            pair_all, attended, normed, qkv_full, out_full, turn_table, bias, grad_gain_three,
+            pair_all, attended, normed, turn_table, bias, grad_gain_three,
         ),
+        (qkv_full, out_full),
         keep,
-        own_rows,
-    )
-    total_gains = lax.dynamic_slice(tail[:4, :D], (0, owner * gain_lines[1]), gain_lines)
-    total_qk = lax.dynamic_slice(tail[4:6, :HD], (0, owner * qk_lines[1]), qk_lines)
+    )
+    total_gate, total_up, total_down, grad_tokens, total_qkv, total_out, output = finish(
+        all_ff, own_rows, grad_tokens, total_qkv, total_out, output
+    )
+    total_gains = lax.dynamic_slice(tail, (0, owner * gain_lines[1]), gain_lines)
+    total_qk = lax.dynamic_slice(tail, (4, owner * qk_lines[1]), qk_lines)
     return (
         output.reshape(tokens.shape),
         grad_tokens.reshape(tokens.shape),

time: 307 us -> 310 us (level); the launches traced: 303 us -> 310 us
  Pallas kernels: 270 us -> 299 us
  local copies, waits for them, and re-layouts: 30.7 us -> 8.06 us
    pallas_call x0 -> x1, Pallas kernels: none -> 50.3 us  [finish(): pl.pallas_call(finish_kernel, out_shape=(weight,) * 3 + tuple((jax.ShapeD...]
    unnamed x47 -> x2, local copies, waits for them, and re-layouts: 19.7 us -> 0.01 us
    pallas_call x1, Pallas kernels: 112 us -> 94.1 us  [backward_rest(): pl.pallas_call(back_kernel, out_shape=(jax.ShapeDtypeStruct((rows, D), f3...]
    pallas_call x1, Pallas kernels: 83.4 us -> 77.2 us  [ffn(): pl.pallas_call(ffn_kernel, out_shape=(jax.ShapeDtypeStruct((rows, D), bf)...]
    dynamic_slice x2 -> x6, local copies, waits for them, and re-layouts: 1.28 us -> 5.34 us  [the longest x2 1.59 us: placed(): lax.dynamic_slice(padded_lines, (0, room - owner * own), (count, room + o...]
    dynamic_update_slice x2 -> x0, local copies, waits for them, and re-layouts: 3.3 us -> none  [the longest x1 1.66 us: on_device(): lax.dynamic_update_slice(gain_rows, qk_gains, (4, owner * qk_lines[1]))]
    reshape x3 -> x0, local copies, waits for them, and re-layouts: 3.25 us -> none  [my_slice(): weight.reshape(ctx_size, slice_rows, D)]
where the time goes in v6:
time: 310 us
  Pallas kernels  299 us (96%)
  local copies, waits for them, and re-layouts  8.06 us (3%)
    pallas_call x1, Pallas kernels, backward_rest(): pl.pallas_call(back_kernel, out_shape=(jax.ShapeDtypeStruct((rows, D), f3...  94.1 us
    pallas_call x1, Pallas kernels, ffn(): pl.pallas_call(ffn_kernel, out_shape=(jax.ShapeDtypeStruct((rows, D), bf)...  77.2 us
    pallas_call x1, Pallas kernels, front(): pl.pallas_call(front_kernel, out_shape=tuple((jax.ShapeDtypeStruct(*s) fo...  77 us
    pallas_call x1, Pallas kernels, finish(): pl.pallas_call(finish_kernel, out_shape=(weight,) * 3 + tuple((jax.ShapeD...  50.3 us

profile of v6, /device:TPU:73, one launch (start us, length us, event | category | flops | bytes accessed | tf_op | source)
XLA Modules:
  0.0 310.1 jit_solution(15705566733911930976)
XLA Ops:
  0.6 0.0 copy-start
  0.7 0.8 pad_dynamic-slice_fusion.1
  1.5 0.1 pad.39.clone
  1.6 1.2 broadcast_in_dim.12.seg_ref
  2.8 0.8 pad_dynamic-slice_fusion
  3.6 1.4 copy.20.seg_col
  5.0 0.0 copy-done
  5.0 1.7 fusion.11.qkv_ref
  6.8 1.0 constant_dynamic-slice_fusion.1
  7.8 0.8 fusion.9.ffn_ref
  8.6 77.0 %shard_map.178 = (bf16[1152,1536]{1,0:T(8,128)(2,1)}, bf16[1024,1152]{1,0:T(8,128)(2,1)}, bf16[16,192,1152]{2,1,0:T(8,128)(2,1)}, f32[4,1152]{1,0:T(4,128)}, f32...) custom-call(bf16[80,1536]{1,0:T(8,128)(2,1)} %fusion.11.qkv_ref, ...), custom_call_target="tpu_custom_call" | custom-call | flops 1358954496 | bytes 7864320 | tf_op jit(solution)/shard_map/pallas_call | solution.py:611
  85.6 77.2 %shard_map.179 = (bf16[128,1152]{1,0:T(8,128)(2,1)}, f32[128,1152]{1,0:T(8,128)}, f32[1,1152]{1,0:T(1,128)}, bf16[16,192,1152]{2,1,0:T(8,128)(2,1)}) custom-call(bf16[128,1152]{1,0:T(8,128)(2,1)} %get-tuple-element.40.normed_ref, f32[128,1152]{1,0:T(8,128)} %get-tuple-element.41.mid_ref, bf16[128,1152]{1,0:T(8,128)(2,1)} %bitcast.8, ...), custom_call_target="tpu_custom_call" | custom-call | flops 21743271936 | bytes 16515072 | tf_op jit(solution)/shard_map/pallas_call | solution.py:234
  162.8 94.1 %shard_map.180 = (f32[128,1152]{1,0:T(8,128)}, f32[72,1536]{1,0:T(8,128)}, f32[8,1536]{1,0:T(8,128)}, f32[64,1152]{1,0:T(8,128)}, bf16[8,192,1152]{2,1,0:T(8,128)(2,1)}) custom-call(bf16[16,192,1152]{2,1,0:T(8,128)(2,1)} %get-tuple-element.44.gff, f32[128,1152]{1,0:T(8,128)} %get-tuple-element.45.gn_ref, f32[128,1152]{1,0:T(8,128)} %get-tuple-element.41.mid_ref, ...), custom_call_target="tpu_custom_call" | custom-call | flops 2717908992 | bytes 14155776 | tf_op jit(solution)/shard_map/pallas_call | solution.py:1060
  256.9 1.3 constant_dynamic-slice_fusion.4
  258.3 1.3 constant_dynamic-slice_fusion
  259.6 50.3 %shard_map.181 = (f32[432,1152]{1,0:T(8,128)}, f32[432,1152]{1,0:T(8,128)}, f32[432,1152]{1,0:T(8,128)}, f32[128,1152]{1,0:T(8,128)}, f32[72,1536]{1,0:T(8,128)}...) custom-call(bf16[8,192,1152]{2,1,0:T(8,128)(2,1)} %get-tuple-element.58.all_hbm, f32[128,1152]{1,0:T(8,128)} %get-tuple-element.59.gt_hbm, ...), custom_call_target="tpu_custom_call" | custom-call | tf_op jit(solution)/shard_map/pallas_call | solution.py:1145
  (2 shorter events, 0.0 us)
Async XLA Ops:
  0.6 4.3 %copy-start = (bf16[432,1152]{1,0:T(8,128)(2,1)S(1)}, bf16[432,1152]{1,0:T(8,128)(2,1)}, u32[]{:S(2)}) copy-start(bf16[432,1152]{1,0:T(8,128)(2,1)} %param.16) | copy-start | bytes 2985988

commit v7 on v6

--- a/solution.py
+++ b/solution.py
@@ -36,7 +36,7 @@
 def ffn_kernel(
     normed_ref, mid_ref, cot_ref, gain_ref, w_hbm,
     out_ref, gn_ref, ggain_ref, gff_hbm,
-    wg, wu, wd, seq, gseq, act_a, act_b, hid, dgate, dup, part,
+    wg, wu, wd, seq, gseq, act_a, act_b, hid, dgate, dup, part, keep, base,
     d2d_snd, d2d_in, ici_snd, ici_in, dw,
     w_sem, o_sem, ag_s, ag_r, rd_s, rd_r, ri_s, ri_r,
 ):
@@ -116,15 +116,17 @@
                 ag_s.at[ph, 6 + 2 * h], ag_r.at[ph, 6 + 2 * h], partner,
             )
 
-    def sum_out(ph, k):
+    def swap(ph, k):
         d2d_snd[ph, k] = part[pl.ds(rows, rows), :].astype(jnp.bfloat16)
-        copy = send(
-            d2d_snd.at[ph, k], d2d_in.at[ph, k], rd_s.at[ph, k], rd_r.at[ph, k], partner
-        )
+        keep[order.index(k) % 2] = part[pl.ds(0, rows), :]
+        return send(d2d_snd.at[ph, k], d2d_in.at[ph, k], rd_s.at[ph, k], rd_r.at[ph, k], partner)
+
+    def sum_out(ph, k, copy):
         copy.wait_recv()
-        total = part[pl.ds(0, rows), :] + d2d_in[ph, k].astype(jnp.float32)
+        total = keep[order.index(k) % 2] + d2d_in[ph, k].astype(jnp.float32)
         if k == 0:
-            return total
+            base[...] = total
+            return None
         ici_snd[ph, k - 1] = total.astype(jnp.bfloat16)
         back = 4 - k
         return send(
@@ -138,6 +140,7 @@
             for load in loads:
                 load.wait()
         sums = {}
+        copy = waiting = None
         for k in order:
             if k == 1:
                 relay(buf, ph, got, 1)
@@ -148,12 +151,18 @@
                 got[2, 1].wait_recv()
             else:
                 got[k].wait_recv()
+            if waiting is not None and k == 2:
+                sums[waiting] = sum_out(ph, waiting, copy)
+                waiting = None
             work(k)
-            sums[k] = sum_out(ph, k)
+            if waiting is not None:
+                sums[waiting] = sum_out(ph, waiting, copy)
+            copy, waiting = swap(ph, k), k
+        sums[waiting] = sum_out(ph, waiting, copy)
         return sums
 
     def collect(ph, sums):
-        total = sums[0]
+        total = base[...]
         for k in (1, 3, 2):
             sums[k].wait_recv()
         for k in (1, 2, 3):
@@ -253,6 +262,8 @@
             pltpu.VMEM((seq_rows, units), bf),
             pltpu.VMEM((seq_rows, units), bf),
             pltpu.VMEM((2 * rows, D), f32),
+            pltpu.VMEM((2, rows, D), f32),
+            pltpu.VMEM((rows, D), f32),
             pltpu.VMEM((2, 4, rows, D), bf),
             pltpu.VMEM((2, 4, rows, D), bf),
             pltpu.VMEM((2, 3, rows, D), bf),
@@ -1103,56 +1114,30 @@
     )(gff, *values, *weights)
 
 
-def finish_kernel(
-    all_hbm, gt_hbm, oq_hbm, oo_hbm, out_hbm,
-    og, ou, od, gt, oq, oo, out,
-    buf, wide, i_sem, o_sem,
-):
-    through = [
-        pltpu.make_async_copy(src, dst, o_sem.at[3 + i])
-        for i, (src, dst) in enumerate(((gt_hbm, gt), (oq_hbm, oq), (oo_hbm, oo), (out_hbm, out)))
-    ]
-    members = buf.shape[0]
-    share = buf.shape[1] // 3
-    lines = wide.shape[1] // members
-    loads = [
-        pltpu.make_async_copy(
-            all_hbm.at[:, pl.ds(i * share, share), :],
-            buf.at[:, pl.ds(i * share, share), :],
-            i_sem.at[i],
-        )
-        for i in range(3)
-    ]
-    for copy in loads + through:
-        copy.start()
-    stores = []
-    for i, dst in enumerate((og, ou, od)):
-        loads[i].wait()
+def finish_kernel(*refs):
+    count = (len(refs) - 3 - 1) // 2
+    all_ref, sources = refs[0], refs[1 : 1 + count]
+    weights, results = refs[1 + count : 4 + count], refs[4 + count :]
+    for src, dst in zip(sources, results):
+        dst[...] = src[...]
+    members = all_ref.shape[0]
+    share = all_ref.shape[1] // 3
+    lines = weights[0].shape[0] // members
+    for i, dst in enumerate(weights):
         for m in range(members):
-            wide[i, m * lines : (m + 1) * lines, :] = buf[
+            dst[m * lines : (m + 1) * lines, :] = all_ref[
                 m, i * share : (i + 1) * share, :
             ].astype(jnp.float32)[:lines]
-        store = pltpu.make_async_copy(wide.at[i], dst, o_sem.at[i])
-        store.start()
-        stores.append(store)
-    for copy in through + stores:
-        copy.wait()
 
 
 def finish(all_ff, lines, *rest):
-    hbm = pl.BlockSpec(memory_space=pl.ANY)
+    vm = pl.BlockSpec(memory_space=pltpu.VMEM)
     weight = jax.ShapeDtypeStruct((lines, D), jnp.float32)
     return pl.pallas_call(
         finish_kernel,
         out_shape=(weight,) * 3 + tuple(jax.ShapeDtypeStruct(r.shape, r.dtype) for r in rest),
-        in_specs=[hbm] * (1 + len(rest)),
-        out_specs=(hbm,) * (3 + len(rest)),
-        scratch_shapes=[
-            pltpu.VMEM(all_ff.shape, all_ff.dtype),
-            pltpu.VMEM((3, lines, D), jnp.float32),
-            pltpu.SemaphoreType.DMA((3,)),
-            pltpu.SemaphoreType.DMA((3 + len(rest),)),
-        ],
+        in_specs=[vm] * (1 + len(rest)),
+        out_specs=(vm,) * (3 + len(rest)),
         compiler_params=pltpu.CompilerParams(vmem_limit_bytes=62 * 1024 * 1024),
     )(all_ff, *rest)
 

time: 310 us -> 263 us (0.85)
  Pallas kernels: 299 us -> 249 us
    pallas_call x1, Pallas kernels: 50.3 us -> 5.6 us  [finish(): pl.pallas_call(finish_kernel, out_shape=(weight,) * 3 + tuple((jax.ShapeD...]
where the time goes in v7:
time: 263 us; the launch traced here: 261 us
  Pallas kernels  249 us (95%)
  local copies, waits for them, and re-layouts  8.06 us (3%)
    pallas_call x1, Pallas kernels, backward_rest(): pl.pallas_call(back_kernel, out_shape=(jax.ShapeDtypeStruct((rows, D), f3...  92.6 us
    pallas_call x1, Pallas kernels, front(): pl.pallas_call(front_kernel, out_shape=tuple((jax.ShapeDtypeStruct(*s) fo...  77 us
    pallas_call x1, Pallas kernels, ffn(): pl.pallas_call(ffn_kernel, out_shape=(jax.ShapeDtypeStruct((rows, D), bf)...  74.3 us
    pallas_call x1, Pallas kernels, finish(): pl.pallas_call(finish_kernel, out_shape=(weight,) * 3 + tuple((jax.ShapeD...  5.6 us

profile of v7, /device:TPU:73, one launch (start us, length us, event | category | flops | bytes accessed | tf_op | source)
XLA Modules:
  0.0 260.8 jit_solution(10300640528658985223)
XLA Ops:
  0.6 0.0 copy-start
  0.7 0.8 pad_dynamic-slice_fusion.1
  1.5 0.1 pad.39.clone
  1.6 1.2 broadcast_in_dim.12.seg_ref
  2.8 0.8 pad_dynamic-slice_fusion
  3.6 1.4 copy.20.seg_col
  5.0 0.0 copy-done
  5.0 1.7 fusion.11.qkv_ref
  6.8 1.0 constant_dynamic-slice_fusion.1
  7.8 0.8 fusion.9.ffn_ref
  8.6 77.0 %shard_map.178 = (bf16[1152,1536]{1,0:T(8,128)(2,1)}, bf16[1024,1152]{1,0:T(8,128)(2,1)}, bf16[16,192,1152]{2,1,0:T(8,128)(2,1)}, f32[4,1152]{1,0:T(4,128)}, f32...) custom-call(bf16[80,1536]{1,0:T(8,128)(2,1)} %fusion.11.qkv_ref, ...), custom_call_target="tpu_custom_call" | custom-call | flops 1358954496 | bytes 7864320 | tf_op jit(solution)/shard_map/pallas_call | solution.py:622
  85.6 74.3 %shard_map.179 = (bf16[128,1152]{1,0:T(8,128)(2,1)}, f32[128,1152]{1,0:T(8,128)}, f32[1,1152]{1,0:T(1,128)}, bf16[16,192,1152]{2,1,0:T(8,128)(2,1)}) custom-call(bf16[128,1152]{1,0:T(8,128)(2,1)} %get-tuple-element.40.normed_ref, f32[128,1152]{1,0:T(8,128)} %get-tuple-element.41.mid_ref, bf16[128,1152]{1,0:T(8,128)(2,1)} %bitcast.8, ...), custom_call_target="tpu_custom_call" | custom-call | flops 21743271936 | bytes 16515072 | tf_op jit(solution)/shard_map/pallas_call | solution.py:243
  159.9 92.6 %shard_map.180 = (f32[128,1152]{1,0:T(8,128)}, f32[72,1536]{1,0:T(8,128)}, f32[8,1536]{1,0:T(8,128)}, f32[64,1152]{1,0:T(8,128)}, bf16[8,192,1152]{2,1,0:T(8,128)(2,1)}) custom-call(bf16[16,192,1152]{2,1,0:T(8,128)(2,1)} %get-tuple-element.44.gff, f32[128,1152]{1,0:T(8,128)} %get-tuple-element.45.gn_ref, f32[128,1152]{1,0:T(8,128)} %get-tuple-element.41.mid_ref, ...), custom_call_target="tpu_custom_call" | custom-call | flops 2717908992 | bytes 14155776 | tf_op jit(solution)/shard_map/pallas_call | solution.py:1071
  252.5 1.3 constant_dynamic-slice_fusion.4
  253.8 1.3 constant_dynamic-slice_fusion
  255.2 5.6 %shard_map.181 = (f32[432,1152]{1,0:T(8,128)}, f32[432,1152]{1,0:T(8,128)}, f32[432,1152]{1,0:T(8,128)}, f32[128,1152]{1,0:T(8,128)}, f32[72,1536]{1,0:T(8,128)}...) custom-call(bf16[8,192,1152]{2,1,0:T(8,128)(2,1)} %get-tuple-element.58.refs_0_, f32[128,1152]{1,0:T(8,128)} %get-tuple-element.59.refs_1_, ...), custom_call_target="tpu_custom_call" | custom-call | tf_op jit(solution)/shard_map/pallas_call | solution.py:1136
  (2 shorter events, 0.0 us)
Async XLA Ops:
  0.6 4.3 %copy-start = (bf16[432,1152]{1,0:T(8,128)(2,1)S(1)}, bf16[432,1152]{1,0:T(8,128)(2,1)}, u32[]{:S(2)}) copy-start(bf16[432,1152]{1,0:T(8,128)(2,1)} %param.16) | copy-start | bytes 2985988

commit v8 on v7

--- a/solution.py
+++ b/solution.py
@@ -213,6 +213,7 @@
         part[...] = dot32(dgate[pair(k), :], wg[...], NN) + dot32(dup[pair(k), :], wu[...], NN)
 
     sums = phase(gseq, 1, backward)
+    stores = []
     for i, (left, right) in enumerate(((dgate, seq), (dup, seq), (hid, gseq))):
         def one(t, carry, i=i, left=left, right=right):
             cols = pl.ds(pl.multiple_of(t * tile, tile), tile)
@@ -223,12 +224,16 @@
             return carry
 
         lax.fori_loop(0, units // tile, one, 0)
-    store = pltpu.make_async_copy(dw, gff_hbm, o_sem)
-    store.start()
+        third = pl.ds(i * share, share)
+        stores.append(
+            pltpu.make_async_copy(dw.at[:, third, :], gff_hbm.at[:, third, :], o_sem.at[i])
+        )
+        stores[-1].start()
     gn_ref[...] = collect(1, sums)
     for copy in started:
         copy.wait_send()
-    store.wait()
+    for store in stores:
+        store.wait()
 
 
 def ffn(normed_two, mid, cot, gain, weights):
@@ -269,7 +274,7 @@
             pltpu.VMEM((2, 3, rows, D), bf),
             pltpu.VMEM((2, 3, rows, D), bf),
             pltpu.VMEM(weights.shape, bf),
-            dma((3, owners)), dma,
+            dma((3, owners)), dma((3,)),
             dma((2, 10)), dma((2, 10)),
             dma((2, 4)), dma((2, 4)),
             dma((2, 4)), dma((2, 4)),
@@ -337,10 +342,10 @@
 
 
 def front_kernel(
-    qkv_ref, wo_ref, ffn_ref, tok_ref, seg_ref, seg_col, table_ref,
-    qkv_out, wo_all, ffn_all, gains_ref, qk_ref, normed_ref, proj_ref, q_ref, pair_ref, att_ref,
+    qkv_ref, wo_ref, ffn_ref, tok_ref, seg_line, table_ref,
+    qkv_hbm, wo_hbm, ffn_all, gains_ref, qk_ref, normed_ref, proj_ref, q_ref, pair_ref, att_ref,
     attn_ref, mid_ref, low_ref, bias_ref, turn_ref,
-    qkv_all, seg_in,
+    qkv_all, qkv_out, wo_all, seg_ref, seg_in,
     l_sem, s1, r1, s2, r2, sd, rd, s1f, r1f, s2f, r2f, skv, rkv, ssg, rsg,
 ):
     f32, bf = jnp.float32, jnp.bfloat16
@@ -359,6 +364,8 @@
     def member(k):
         return {"ctx": lax.rem(me + k, members)}
 
+    seg_ref[...] = jnp.broadcast_to(seg_line[...], seg_ref.shape)
+
     def views(f, half):
         return (
             qkv_all.at[
@@ -452,13 +459,18 @@
     for k in (1, 3, 2):
         for t in both:
             hop_one(k, t).start()
-    for k in (1, 3, 2):
+    def hop_pass(j, t):
+        m, k = (3, 1) if j < 2 else (1, 3)
+        dst = views(block(lax.rem(a + j, 4), lax.rem(b + m, 4)), core)[t]
+        return remote(dst, dst, s2.at[j, 2, t], r2.at[j, 2, t], second_peer(k))
+
+    for k in (1, 3):
         for t in both:
             hop_two(0, k, t).start()
     for j in (1, 3, 2):
         for t in both:
             arrive_one(j, t).wait_recv()
-            for k in (1, 3, 2):
+            for k in (1, 3):
                 hop_two(j, k, t).start()
             cross(j, 0, t).start()
 
@@ -469,14 +481,17 @@
     for k in (1, 3):
         ffn_two(0, k).start()
 
-    def pass_on(i, carry):
-        m, j = i // 4 + 1, lax.rem(i, 4)
+    for j in (0, 1, 3, 2):
+        for m in (3, 1) if j < 2 else (1, 3):
+            for t in both:
+                arrive_two(j, m, t).wait_recv()
+                if m == (3 if j < 2 else 1):
+                    hop_pass(j, t).start()
+                cross(j, m, t).start()
+    for j in (0, 1, 3, 2):
         for t in both:
-            arrive_two(j, m, t).wait_recv()
-            cross(j, m, t).start()
-        return carry
-
-    lax.fori_loop(0, 12, pass_on, 0)
+            arrive_two(j, 2, t).wait_recv()
+            cross(j, 2, t).start()
 
     def land(i, carry):
         m, j = i // 4, lax.rem(i, 4)
@@ -486,13 +501,20 @@
         return carry
 
     lax.fori_loop(1, 16, land, 0)
-    for copy in locals_:
+    for copy in locals_[:2]:
         copy.wait()
-    for k in (1, 2, 3):
-        for t in both:
+    for t in both:
+        for k in (1, 2, 3):
             hop_one(k, t).wait_send()
-            for j in range(4):
+        for j in range(4):
+            hop_pass(j, t).wait_send()
+            for k in (1, 3):
                 hop_two(j, k, t).wait_send()
+    saves = [
+        pltpu.make_async_copy(qkv_out, qkv_hbm, l_sem.at[4]),
+        pltpu.make_async_copy(wo_all, wo_hbm, l_sem.at[5]),
+    ]
+    saves[1].start()
 
     keep = qkv_out.shape[0] // 16
     extra = jnp.zeros((q_rows - keep, width), f32)
@@ -503,6 +525,7 @@
             [left[:keep], right[:keep]], axis=0
         ).astype(bf)
         extra = extra + left[keep:] + right[keep:]
+    saves[0].start()
     gains = extra[:4, :D]
     gains_ref[...] = gains
     qk_ref[...] = extra[4:6, :HD]
@@ -510,6 +533,7 @@
     stream = tok_ref[...].astype(f32)
     normed_ref[...] = rms_norm(stream, gains[0:1]).astype(bf)
     proj_ref[...] = dot32(normed_ref[...], qkv_out[...], NN)
+    locals_[3].wait()
     cos_table, sin_table = turn_ref[:, : HD // 2], turn_ref[:, HD // 2 :]
 
     def turn(values, gain, cos_part, sin_part):
@@ -557,8 +581,17 @@
         - lax.broadcasted_iota(jnp.int32, shape, 1)
     )
     begun = lax.broadcasted_iota(jnp.int32, shape, 1) + (me - reach) * rows >= 0
-    allowed = (spacing >= 0) & (spacing < WINDOW) & begun & (seg_col[...] == key_seg)
+    wide = jnp.broadcast_to(seg_line[...], (rows, rows)).astype(f32)
+    query_seg = jnp.concatenate([wide.T] * (reach + 1), axis=1)
+    allowed = (
+        (spacing >= 0) & (spacing < WINDOW) & begun & (query_seg == key_seg.astype(f32))
+    )
     bias_ref[...] = jnp.where(allowed, 0.0, NEG_FILL)
+    def ffn_onward(j):
+        ffn_got(j, 3 if j < 2 else 1).wait_recv()
+        ffn_pass(j).start()
+
+    ffn_onward(0)
     for d in range(1, reach + 1):
         kv_send(d).wait_recv()
     scores = dot32(queries, pair_ref[:, :HD], NT) * (HD ** (-0.5)) + jnp.concatenate(
@@ -569,15 +602,17 @@
     heads = dot32(probs.astype(bf), pair_ref[:, HD:], NN).astype(bf)
     for h in range(NH):
         att_ref[:, h * HD : (h + 1) * HD] = heads[h * rows : (h + 1) * rows]
+    ffn_onward(1)
+    ffn_onward(3)
     attn = dot32(att_ref[...], wo_all[...], NN)
     attn_ref[...] = attn
     mid = stream + rms_norm(attn, gains[1:2])
     mid_ref[...] = mid
     low_ref[...] = rms_norm(mid, gains[2:3]).astype(bf)
 
-    for j in range(4):
-        ffn_got(j, 3 if j < 2 else 1).wait_recv()
-        ffn_pass(j).start()
+    ffn_onward(2)
+    for copy in saves + locals_[2:3]:
+        copy.wait()
     for j in range(4):
         ffn_got(j, 1 if j < 2 else 3).wait_recv()
         ffn_got(j, 2).wait_recv()
@@ -592,7 +627,7 @@
         kv_send(d).wait_send()
 
 
-def front(qkv_shard, wo_shard, ffn_shard, tokens, seg_rows, seg_col, table, keep):
+def front(qkv_shard, wo_shard, ffn_shard, tokens, seg_line, table, keep):
     f32, bf = jnp.float32, jnp.bfloat16
     vm = pl.BlockSpec(memory_space=pltpu.VMEM)
     hbm = pl.BlockSpec(memory_space=pl.ANY)
@@ -622,12 +657,15 @@
     return pl.pallas_call(
         front_kernel,
         out_shape=tuple(jax.ShapeDtypeStruct(*s) for s in shapes),
-        in_specs=[vm, vm, hbm, vm, vm, vm, hbm],
-        out_specs=(vm, vm, hbm) + (vm,) * (len(shapes) - 3),
+        in_specs=[vm, vm, hbm, vm, vm, hbm],
+        out_specs=(hbm,) * 3 + (vm,) * (len(shapes) - 3),
         scratch_shapes=[
             pltpu.VMEM((16 * q_rows, width), bf),
+            pltpu.VMEM((16 * keep, width), bf),
+            pltpu.VMEM((16 * o_rows, o_width), bf),
+            pltpu.VMEM((8, rows), jnp.int32),
             pltpu.VMEM((reach + 1, 8, rows), jnp.int32),
-            dma((4,)),
+            dma((6,)),
             dma((4, 2)), dma((4, 2)),
             dma((4, 4, 2)), dma((4, 4, 2)),
             dma((4, 4, 2)), dma((4, 4, 2)),
@@ -642,7 +680,7 @@
         cost_estimate=pl.CostEstimate(
             flops=6 * rows * width * D, bytes_accessed=64 * q_rows * width, transcendentals=0
         ),
-    )(qkv_shard, wo_shard, ffn_shard, tokens, seg_rows, seg_col, table)
+    )(qkv_shard, wo_shard, ffn_shard, tokens, seg_line, table)
 
 
 def back_kernel(
@@ -650,9 +688,9 @@
     pair_ref, att_ref, normed_ref, turn_ref, bias_ref, g3_ref, qkv_hbm, wo_hbm,
     gt_ref, oq_out, tail_out, oo_ref, all_ff,
     qkv_ref, wo_ref, oq_ref, own_ff, far_own, far_in, in1_ff, t_ff, in2_ff, kv_snd, kv_in, gmid, gpair, gproj, tail,
-    stage, go, dq, do, sq, so, iq1, io1, tq, to, iq2, io2, xq, xo,
+    stage, go, dq, do, sq, so, fq, fo, iq1, io1, tq, to, iq2, io2, xq, xo,
     l_sem, sfar, rfar, s1f, r1f, s2f, r2f, sag, rag, skv, rkv,
-    sd, rd, s1, r1, s2, r2, sx, rx, sf, rf,
+    sd, rd, sfa, rfa, s1, r1, s2, r2, sx, rx, sf, rf,
 ):
     y, z, chip, core = place()
     a, b, block = shape_of(y, z, core)
@@ -756,7 +794,7 @@
     lax.fori_loop(0, NH * HD // 256, out_tile, 0)
 
     def away(i, t):
-        k, j = lax.rem(i // 4 + 1, 4), lax.rem(i, 4)
+        k, j = lax.rem(i // 4 + 2, 4), lax.rem(i, 4)
         there = lax.rem(b + k, 4)
         f = block_there(there, j)
         slot = there * 4 + j
@@ -767,7 +805,7 @@
         return remote(src, dst, sd.at[i, t], rd.at[i, t], partner)
 
     def home(i, t):
-        k, j = lax.rem(i // 4 + 1, 4), lax.rem(i, 4)
+        k, j = lax.rem(i // 4 + 2, 4), lax.rem(i, 4)
         slot = lax.rem(a + k, 4) * 4 + j
         dst = (dq, do)[t].at[slot]
         return remote(dst, dst, sd.at[i, t], rd.at[i, t], partner)
@@ -815,18 +853,30 @@
     for h in range(NH):
         gproj[:, h * HD : (h + 1) * HD] = grad_q[h * rows : (h + 1) * rows].astype(bf)
 
-    def hop_one(k, t):
+    def pair_of(k, h):
+        return pl.ds(line(k) * 4 + 2 * h, 2)
+
+    def sum_far(h, t):
+        src, dst = ((sq, fq), (so, fo))[t]
+        return remote(
+            src.at[pair_of(2, h)], dst.at[pl.ds(2 * h, 2)],
+            sfa.at[h, t], rfa.at[h, t], first_peer(3 if h else 1),
+        )
+
+    def sum_near(k, h, t):
         src, dst = ((sq, iq1), (so, io1))[t]
+        side = 0 if k == 1 else 1
         return remote(
-            src.at[pl.ds(line(k) * 4, 4)], dst.at[3 - k], s1.at[k, t], r1.at[4 - k, t], first_peer(k)
+            src.at[pair_of(k, h)], dst.at[side, pl.ds(2 * h, 2)],
+            s1.at[side, h, t], r1.at[side, h, t], first_peer(k),
         )
 
     def fold_cores(t):
-        for k in (1, 2, 3, 0):
+        for k in (2, 3, 1, 0):
             def add(j, carry, k=k):
                 slot = line(k) * 4 + j
                 f = block(line(k), j)
-                home((k + 3) % 4 * 4 + j, t).wait_recv()
+                home((k + 2) % 4 * 4 + j, t).wait_recv()
                 if t == 0:
                     sq[slot] = (
                         stage[f, :, q_cols(core)].astype(f32) + dq[slot].astype(f32)
@@ -838,8 +888,20 @@
                 return carry
 
             lax.fori_loop(0, 4, add, 0)
-            if k:
-                hop_one(k, t).start()
+            if k == 2:
+                sum_far(0, t).start()
+                sum_far(1, t).start()
+            elif k:
+                sum_near(k, 0 if k == 3 else 1, t).start()
+
+    def fold_far(t):
+        acc, far = ((sq, fq), (so, fo))[t]
+        for h, k in ((0, 1), (1, 3)):
+            sum_far(h, t).wait_recv()
+            acc[pair_of(k, h)] = (
+                acc[pair_of(k, h)].astype(f32) + far[2 * h : 2 * h + 2].astype(f32)
+            ).astype(bf)
+            sum_near(k, h, t).start()
 
     pass_far((1, 3))
 
@@ -900,6 +962,8 @@
 
     fold_cores(1)
     fold_cores(0)
+    fold_far(1)
+    fold_far(0)
 
     def hop_two(k, t):
         src, dst = ((tq, iq2), (to, io2))[t]
@@ -953,12 +1017,13 @@
 
     for t in (1, 0):
         own, got, dst = ((sq, iq1, tq), (so, io1, to))[t]
-        for k in (1, 3, 2):
-            hop_one(4 - k, t).wait_recv()
+        for k in (1, 3):
+            for h in (0, 1):
+                sum_near(k, h, t).wait_recv()
         for k in (2, 1, 3, 0):
             j = lax.rem(b + k, 4)
             total = own[a * 4 + j].astype(f32)
-            for m in range(3):
+            for m in (0, 1):
                 total = total + got[m, j].astype(f32)
             dst[j] = total.astype(bf)
             if k:
@@ -1037,8 +1102,11 @@
     for h in (0, 1):
         ff_cross(2, h).wait_send()
     for t in (0, 1):
+        for h in (0, 1):
+            sum_far(h, t).wait_send()
+            sum_near(1, h, t).wait_send()
+            sum_near(3, h, t).wait_send()
         for k in (1, 2, 3):
-            hop_one(k, t).wait_send()
             hop_two(k, t).wait_send()
         for k in range(1, chips):
             hop_chip(k, t).wait_send()
@@ -1092,7 +1160,7 @@
             pltpu.VMEM((8, width), f32),
             pltpu.VMEM((16, q_rows, width), bf),
             pltpu.VMEM((16, o_rows, o_width), bf),
-            *two(16), *two(16), *two(3, 4), *two(4), *two(3), *two(chips),
+            *two(16), *two(16), *two(4), *two(2, 4), *two(4), *two(3), *two(chips),
             dma((10,)),
             dma((4,)), dma((4,)),
             dma((2, 4)), dma((2, 4)),
@@ -1100,7 +1168,8 @@
             dma((12,)), dma((12,)),
             dma((reach,)), dma((reach,)),
             dma((16, 2)), dma((16, 2)),
-            dma((4, 2)), dma((4, 2)),
+            dma((2, 2)), dma((2, 2)),
+            dma((2, 2, 2)), dma((2, 2, 2)),
             dma((4, 2)), dma((4, 2)),
             dma((4, 2)), dma((4, 2)),
             dma((2,)), dma((2,)),
@@ -1115,11 +1184,17 @@
 
 
 def finish_kernel(*refs):
-    count = (len(refs) - 3 - 1) // 2
-    all_ref, sources = refs[0], refs[1 : 1 + count]
-    weights, results = refs[1 + count : 4 + count], refs[4 + count :]
-    for src, dst in zip(sources, results):
+    count = (len(refs) - 7) // 2
+    all_ref, tail_ref, sources = refs[0], refs[1], refs[2 : 2 + count]
+    weights, gains, qk = refs[2 + count : 5 + count], refs[5 + count], refs[6 + count]
+    for src, dst in zip(sources, refs[7 + count :]):
         dst[...] = src[...]
+    owner = lax.axis_index("fsdp")
+    width = tail_ref.shape[1]
+    for first, dst in ((0, gains), (4, qk)):
+        lines, own = dst.shape
+        shift = lax.rem(width - owner * own, width)
+        dst[...] = pltpu.roll(tail_ref[...], shift, 1)[first : first + lines, :own]
     members = all_ref.shape[0]
     share = all_ref.shape[1] // 3
     lines = weights[0].shape[0] // members
@@ -1130,16 +1205,18 @@
             ].astype(jnp.float32)[:lines]
 
 
-def finish(all_ff, lines, *rest):
+def finish(all_ff, tail, lines, gain_lines, qk_lines, *rest):
     vm = pl.BlockSpec(memory_space=pltpu.VMEM)
-    weight = jax.ShapeDtypeStruct((lines, D), jnp.float32)
+    f32 = jnp.float32
+    results = ((lines, D),) * 3 + (gain_lines, qk_lines)
     return pl.pallas_call(
         finish_kernel,
-        out_shape=(weight,) * 3 + tuple(jax.ShapeDtypeStruct(r.shape, r.dtype) for r in rest),
-        in_specs=[vm] * (1 + len(rest)),
-        out_specs=(vm,) * (3 + len(rest)),
+        out_shape=tuple(jax.ShapeDtypeStruct(s, f32) for s in results)
+        + tuple(jax.ShapeDtypeStruct(r.shape, r.dtype) for r in rest),
+        in_specs=[vm] * (2 + len(rest)),
+        out_specs=(vm,) * (5 + len(rest)),
         compiler_params=pltpu.CompilerParams(vmem_limit_bytes=62 * 1024 * 1024),
-    )(all_ff, *rest)
+    )(all_ff, tail, *rest)
 
 
 def on_device(
@@ -1199,8 +1276,7 @@
         out_weight,
         ffn_shard,
         flat,
-        jnp.broadcast_to(segments, (8, local_len)),
-        segments.reshape(local_len, 1),
+        segments,
         table,
         keep,
     )
@@ -1216,11 +1292,12 @@
         (qkv_full, out_full),
         keep,
     )
-    total_gate, total_up, total_down, grad_tokens, total_qkv, total_out, output = finish(
-        all_ff, own_rows, grad_tokens, total_qkv, total_out, output
-    )
-    total_gains = lax.dynamic_slice(tail, (0, owner * gain_lines[1]), gain_lines)
-    total_qk = lax.dynamic_slice(tail, (4, owner * qk_lines[1]), qk_lines)
+    (
+        total_gate, total_up, total_down, total_gains, total_qk,
+        grad_tokens, total_qkv, total_out, output,
+    ) = finish(
+        all_ff, tail, own_rows, gain_lines, qk_lines, grad_tokens, total_qkv, total_out, output
+    )
     return (
         output.reshape(tokens.shape),
         grad_tokens.reshape(tokens.shape),

time: 263 us -> 249 us (0.947)
  Pallas kernels: 249 us -> 239 us
  local copies, waits for them, and re-layouts: 8.06 us -> 2.77 us
    pallas_call x1, Pallas kernels: 77 us -> 71.7 us  [front(): pl.pallas_call(front_kernel, out_shape=tuple((jax.ShapeDtypeStruct(*s) fo...]
    pallas_call x1, Pallas kernels: 92.6 us -> 88.5 us  [backward_rest(): pl.pallas_call(back_kernel, out_shape=(jax.ShapeDtypeStruct((rows, D), f3...]
    dynamic_slice x2 -> x0, local copies, waits for them, and re-layouts: 2.66 us -> none  [the longest x1 1.34 us: on_device(): lax.dynamic_slice(tail, (0, owner * gain_lines[1]), gain_lines)]
where the time goes in v8:
time: 249 us; the launch traced here: 245 us
  Pallas kernels  239 us (96%)
  local copies, waits for them, and re-layouts  2.77 us (1%)
  other arithmetic  2.54 us (1%)
    pallas_call x1, Pallas kernels, backward_rest(): pl.pallas_call(back_kernel, out_shape=(jax.ShapeDtypeStruct((rows, D), f3...  88.5 us
    pallas_call x1, Pallas kernels, ffn(): pl.pallas_call(ffn_kernel, out_shape=(jax.ShapeDtypeStruct((rows, D), bf)...  72.9 us
    pallas_call x1, Pallas kernels, front(): pl.pallas_call(front_kernel, out_shape=tuple((jax.ShapeDtypeStruct(*s) fo...  71.7 us
    pallas_call x1, Pallas kernels, finish(): pl.pallas_call(finish_kernel, out_shape=tuple((jax.ShapeDtypeStruct(s, f3...  5.78 us

profile of v8, /device:TPU:73, one launch (start us, length us, event | category | flops | bytes accessed | tf_op | source)
XLA Modules:
  0.0 244.9 jit_solution(4800343800779924952)
XLA Ops:
  0.6 0.0 copy-start
  0.7 0.8 pad_dynamic-slice_fusion.1
  1.5 0.1 pad.39.clone
  1.6 0.8 pad_dynamic-slice_fusion
  2.3 0.0 copy-done
  2.4 1.7 fusion.11.qkv_ref
  4.1 1.0 constant_dynamic-slice_fusion
  5.2 0.8 fusion.9.ffn_ref
  6.0 71.7 %shard_map.178 = (bf16[1152,1536]{1,0:T(8,128)(2,1)}, bf16[1024,1152]{1,0:T(8,128)(2,1)}, bf16[16,192,1152]{2,1,0:T(8,128)(2,1)}, f32[4,1152]{1,0:T(4,128)}, f32...) custom-call(bf16[80,1536]{1,0:T(8,128)(2,1)} %fusion.11.qkv_ref, ...), custom_call_target="tpu_custom_call" | custom-call | flops 1358954496 | bytes 7864320 | tf_op jit(solution)/shard_map/pallas_call | solution.py:657
  77.7 72.9 %shard_map.179 = (bf16[128,1152]{1,0:T(8,128)(2,1)}, f32[128,1152]{1,0:T(8,128)}, f32[1,1152]{1,0:T(1,128)}, bf16[16,192,1152]{2,1,0:T(8,128)(2,1)}) custom-call(bf16[128,1152]{1,0:T(8,128)(2,1)} %get-tuple-element.42.normed_ref, f32[128,1152]{1,0:T(8,128)} %get-tuple-element.43.mid_ref, bf16[128,1152]{1,0:T(8,128)(2,1)} %bitcast.6, ...), custom_call_target="tpu_custom_call" | custom-call | flops 21743271936 | bytes 16515072 | tf_op jit(solution)/shard_map/pallas_call | solution.py:248
  150.5 88.5 %shard_map.180 = (f32[128,1152]{1,0:T(8,128)}, f32[72,1536]{1,0:T(8,128)}, f32[8,1536]{1,0:T(8,128)}, f32[64,1152]{1,0:T(8,128)}, bf16[8,192,1152]{2,1,0:T(8,128)(2,1)}) custom-call(bf16[16,192,1152]{2,1,0:T(8,128)(2,1)} %get-tuple-element.46.gff, f32[128,1152]{1,0:T(8,128)} %get-tuple-element.47.gn_ref, f32[128,1152]{1,0:T(8,128)} %get-tuple-element.43.mid_ref, ...), custom_call_target="tpu_custom_call" | custom-call | flops 2717908992 | bytes 14155776 | tf_op jit(solution)/shard_map/pallas_call | solution.py:1139
  239.1 5.8 %shard_map.181 = (f32[432,1152]{1,0:T(8,128)}, f32[432,1152]{1,0:T(8,128)}, f32[432,1152]{1,0:T(8,128)}, f32[4,72]{1,0:T(4,128)}, f32[2,16]{1,0:T(2,128)}, /*ind...) custom-call(bf16[8,192,1152]{2,1,0:T(8,128)(2,1)} %get-tuple-element.60.refs_0_, ...), custom_call_target="tpu_custom_call" | custom-call | tf_op jit(solution)/shard_map/pallas_call | solution.py:1212
  (2 shorter events, 0.0 us)
Async XLA Ops:
  0.6 1.7 copy-start

commit v9 on v8

--- a/solution.py
+++ b/solution.py
@@ -33,16 +33,86 @@
     return lax.dot_general(left, right, dims, preferred_element_type=jnp.float32)
 
 
+def place():
+    fsdp = lax.axis_index("fsdp")
+    ctx = lax.axis_index("ctx")
+    y, z = fsdp // 4, lax.rem(fsdp, 4)
+    chip, core = ctx // 2, lax.rem(ctx, 2)
+    return y, z, chip, core
+
+
+def shape_of(y, z, core):
+    first = (1 - core) * y + core * z
+    second = (1 - core) * z + core * y
+
+    def block(i, j):
+        return (1 - core) * (4 * i + j) + core * (4 * j + i)
+
+    return first, second, block
+
+
+def remote(src, dst, s_sem, r_sem, peer):
+    return pltpu.make_async_remote_copy(
+        src_ref=src, dst_ref=dst, send_sem=s_sem, recv_sem=r_sem,
+        device_id=peer, device_id_type=MESH,
+    )
+
+
+def greet(peers):
+    barrier = pltpu.get_barrier_semaphore()
+    for peer in peers:
+        pl.semaphore_signal(barrier, inc=1, device_id=peer, device_id_type=MESH)
+    pl.semaphore_wait(barrier, len(peers))
+
+
+def ring_gather(buf, rows, partner, chips, s_sem, r_sem):
+    started, got = [], {}
+
+    def send(src, dst, i, back, peer):
+        copy = remote(src, dst, s_sem.at[i], r_sem.at[back], peer)
+        copy.start()
+        started.append(copy)
+        return copy
+
+    def mine(k):
+        return buf.at[pl.ds(k * 2 * rows, rows)]
+
+    def other(k):
+        return buf.at[pl.ds(k * 2 * rows + rows, rows)]
+
+    def half_of(k, h, offset=0):
+        return buf.at[pl.ds(k * 2 * rows + offset + h * (rows // 2), rows // 2)]
+
+    def spread():
+        for k in (1, 3):
+            got[4 - k] = send(mine(0), mine(4 - k), k, 4 - k, chips[k])
+        got[0] = send(mine(0), other(0), 0, 0, partner)
+
+    def relay(k):
+        got[k].wait_recv()
+        h = 0 if k == 3 else 1
+        got[2, h] = send(half_of(k, h), half_of(2, h), 2 + 2 * h, 2 + 2 * h, chips[4 - k])
+        got[k] = send(mine(k), other(k), 4 + k, 4 + k, partner)
+
+    def relay_far():
+        for h in (0, 1):
+            got[2, h].wait_recv()
+            got[2, h] = send(half_of(2, h), half_of(2, h, rows), 6 + 2 * h, 6 + 2 * h, partner)
+
+    return spread, relay, relay_far, got, started
+
+
 def ffn_kernel(
-    normed_ref, mid_ref, cot_ref, gain_ref, w_hbm,
+    seq, mid_ref, cot_ref, gain_ref, w_hbm,
     out_ref, gn_ref, ggain_ref, gff_hbm,
-    wg, wu, wd, seq, gseq, act_a, act_b, hid, dgate, dup, part, keep, base,
+    wg, wu, wd, gseq, act_a, act_b, hid, dgate, dup, part, keep, base,
     d2d_snd, d2d_in, ici_snd, ici_in, dw,
     w_sem, o_sem, ag_s, ag_r, rd_s, rd_r, ri_s, ri_r,
 ):
-    rows = normed_ref.shape[0]
+    rows = mid_ref.shape[0]
     units = wg.shape[0]
-    share = units // w_hbm.shape[0]
+    owners = w_hbm.shape[0]
+    share = units // owners
     tile = 256
     me = lax.axis_index("ctx")
     chip, core = me // 2, lax.rem(me, 2)
@@ -55,7 +125,7 @@
             w_hbm.at[f, pl.ds(i * share, share), :], dst.at[pl.ds(f * share, share), :], w_sem.at[i, f]
         )
         for i, dst in enumerate((wg, wu, wd))
-        for f in range(w_hbm.shape[0])
+        for f in range(owners)
     ]
     for load in loads:
         load.start()
@@ -76,45 +146,10 @@
         started.append(copy)
         return copy
 
-    def mine(k):
-        return pl.ds(k * 2 * rows, rows)
-
-    def other(k):
-        return pl.ds(k * 2 * rows + rows, rows)
+    spread, relay, relay_far, got, gathers = ring_gather(gseq, rows, partner, chips, ag_s, ag_r)
 
     def pair(k):
         return pl.ds(k * 2 * rows, 2 * rows)
-
-    def spread(buf, ph):
-        own = buf.at[mine(0)]
-        got = {}
-        for k in (1, 3):
-            back = 4 - k
-            got[back] = send(own, buf.at[mine(back)], ag_s.at[ph, k], ag_r.at[ph, back], chips[k])
-        got[0] = send(own, buf.at[other(0)], ag_s.at[ph, 0], ag_r.at[ph, 0], partner)
-        return got
-
-    def half_of(k, h, offset=0):
-        return pl.ds(k * 2 * rows + offset + h * (rows // 2), rows // 2)
-
-    def relay(buf, ph, got, k):
-        got[k].wait_recv()
-        h = 0 if k == 3 else 1
-        got[2, h] = send(
-            buf.at[half_of(k, h)], buf.at[half_of(2, h)],
-            ag_s.at[ph, 2 + 2 * h], ag_r.at[ph, 2 + 2 * h], chips[4 - k],
-        )
-        got[k] = send(
-            buf.at[mine(k)], buf.at[other(k)], ag_s.at[ph, 4 + k], ag_r.at[ph, 4 + k], partner
-        )
-
-    def relay_far(buf, ph, got):
-        for h in (0, 1):
-            got[2, h].wait_recv()
-            got[2, h] = send(
-                buf.at[half_of(2, h)], buf.at[half_of(2, h, rows)],
-                ag_s.at[ph, 6 + 2 * h], ag_r.at[ph, 6 + 2 * h], partner,
-            )
 
     def swap(ph, k):
         d2d_snd[ph, k] = part[pl.ds(rows, rows), :].astype(jnp.bfloat16)
@@ -134,23 +169,20 @@
             chips[k],
         )
 
-    def phase(buf, ph, work):
-        got = spread(buf, ph)
-        if ph == 0:
-            for load in loads:
-                load.wait()
+    def phase(ph, work):
         sums = {}
         copy = waiting = None
         for k in order:
-            if k == 1:
-                relay(buf, ph, got, 1)
-                relay(buf, ph, got, 3)
-            if k == 2:
-                relay_far(buf, ph, got)
-                got[2, 0].wait_recv()
-                got[2, 1].wait_recv()
-            else:
-                got[k].wait_recv()
+            if ph == 1:
+                if k == 1:
+                    relay(1)
+                    relay(3)
+                if k == 2:
+                    relay_far()
+                    got[2, 0].wait_recv()
+                    got[2, 1].wait_recv()
+                else:
+                    got[k].wait_recv()
             if waiting is not None and k == 2:
                 sums[waiting] = sum_out(ph, waiting, copy)
                 waiting = None
@@ -186,10 +218,14 @@
             return carry
 
         lax.fori_loop(0, units // tile, one, 0)
+        if k == 0:
+            for load in loads[2 * owners :]:
+                load.wait()
         part[...] = dot32(hid[pair(k), :], wd[...], NN)
 
-    seq[mine(0), :] = normed_ref[...]
-    sums = phase(seq, 0, forward)
+    for load in loads[: 2 * owners]:
+        load.wait()
+    sums = phase(0, forward)
     mlp = collect(0, sums)
     r = lax.rsqrt(jnp.mean(mlp * mlp, axis=-1, keepdims=True) + EPS)
     n = mlp * r
@@ -199,7 +235,8 @@
     ggain_ref[...] = jnp.sum(dy * n, axis=0, keepdims=True)
     dyg = dy * gain
     dv = r * (dyg - n * jnp.mean(dyg * n, axis=-1, keepdims=True))
-    gseq[mine(0), :] = dv.astype(jnp.bfloat16)
+    gseq[pl.ds(0, rows), :] = dv.astype(jnp.bfloat16)
+    spread()
 
     def backward(k):
         def one(t, carry):
@@ -212,7 +249,7 @@
         lax.fori_loop(0, units // tile, one, 0)
         part[...] = dot32(dgate[pair(k), :], wg[...], NN) + dot32(dup[pair(k), :], wu[...], NN)
 
-    sums = phase(gseq, 1, backward)
+    sums = phase(1, backward)
     stores = []
     for i, (left, right) in enumerate(((dgate, seq), (dup, seq), (hid, gseq))):
         def one(t, carry, i=i, left=left, right=right):
@@ -230,14 +267,14 @@
         )
         stores[-1].start()
     gn_ref[...] = collect(1, sums)
-    for copy in started:
+    for copy in started + gathers:
         copy.wait_send()
     for store in stores:
         store.wait()
 
 
-def ffn(normed_two, mid, cot, gain, weights):
-    rows = normed_two.shape[0]
+def ffn(normed_seq, mid, cot, gain, weights):
+    rows = mid.shape[0]
     owners, lines = weights.shape[:2]
     units = owners * lines // 3
     seq_rows = rows * 8
@@ -260,7 +297,6 @@
             pltpu.VMEM((units, D), bf),
             pltpu.VMEM((units, D), bf),
             pltpu.VMEM((seq_rows, D), bf),
-            pltpu.VMEM((seq_rows, D), bf),
             pltpu.VMEM((seq_rows, units), f32),
             pltpu.VMEM((seq_rows, units), f32),
             pltpu.VMEM((seq_rows, units), bf),
@@ -275,7 +311,7 @@
             pltpu.VMEM((2, 3, rows, D), bf),
             pltpu.VMEM(weights.shape, bf),
             dma((3, owners)), dma((3,)),
-            dma((2, 10)), dma((2, 10)),
+            dma((10,)), dma((10,)),
             dma((2, 4)), dma((2, 4)),
             dma((2, 4)), dma((2, 4)),
         ],
@@ -285,39 +321,7 @@
         cost_estimate=pl.CostEstimate(
             flops=18 * seq_rows * units * D, bytes_accessed=14 * units * D, transcendentals=0
         ),
-    )(normed_two, mid, cot, gain, weights)
-
-
-def place():
-    fsdp = lax.axis_index("fsdp")
-    ctx = lax.axis_index("ctx")
-    y, z = fsdp // 4, lax.rem(fsdp, 4)
-    chip, core = ctx // 2, lax.rem(ctx, 2)
-    return y, z, chip, core
-
-
-def shape_of(y, z, core):
-    first = (1 - core) * y + core * z
-    second = (1 - core) * z + core * y
-
-    def block(i, j):
-        return (1 - core) * (4 * i + j) + core * (4 * j + i)
-
-    return first, second, block
-
-
-def remote(src, dst, s_sem, r_sem, peer):
-    return pltpu.make_async_remote_copy(
-        src_ref=src, dst_ref=dst, send_sem=s_sem, recv_sem=r_sem,
-        device_id=peer, device_id_type=MESH,
-    )
-
-
-def greet(peers):
-    barrier = pltpu.get_barrier_semaphore()
-    for peer in peers:
-        pl.semaphore_signal(barrier, inc=1, device_id=peer, device_id_type=MESH)
-    pl.semaphore_wait(barrier, len(peers))
+    )(normed_seq, mid, cot, gain, weights)
 
 
 def rms_back(values, grad, gain):
@@ -344,9 +348,9 @@
 def front_kernel(
     qkv_ref, wo_ref, ffn_ref, tok_ref, seg_line, table_ref,
     qkv_hbm, wo_hbm, ffn_all, gains_ref, qk_ref, normed_ref, proj_ref, q_ref, pair_ref, att_ref,
-    attn_ref, mid_ref, low_ref, bias_ref, turn_ref,
+    attn_ref, mid_ref, seq, bias_ref, turn_ref,
     qkv_all, qkv_out, wo_all, seg_ref, seg_in,
-    l_sem, s1, r1, s2, r2, sd, rd, s1f, r1f, s2f, r2f, skv, rkv, ssg, rsg,
+    l_sem, s1, r1, s2, r2, sd, rd, s1f, r1f, s2f, r2f, skv, rkv, ssg, rsg, ag_s, ag_r,
 ):
     f32, bf = jnp.float32, jnp.bfloat16
     y, z, chip, core = place()
@@ -598,7 +602,7 @@
         [bias_ref[...]] * NH, axis=0
     )
     expo = jnp.exp(scores - jnp.max(scores, axis=-1, keepdims=True))
-    probs = expo / jnp.sum(expo, axis=-1, keepdims=True)
+    probs = expo * (1.0 / jnp.sum(expo, axis=-1, keepdims=True))
     heads = dot32(probs.astype(bf), pair_ref[:, HD:], NN).astype(bf)
     for h in range(NH):
         att_ref[:, h * HD : (h + 1) * HD] = heads[h * rows : (h + 1) * rows]
@@ -608,14 +612,24 @@
     attn_ref[...] = attn
     mid = stream + rms_norm(attn, gains[1:2])
     mid_ref[...] = mid
-    low_ref[...] = rms_norm(mid, gains[2:3]).astype(bf)
+    seq[pl.ds(0, rows), :] = rms_norm(mid, gains[2:3]).astype(bf)
+    ring = {k: {"ctx": lax.rem(chip + k, members // 2) * 2 + core} for k in (1, 2, 3)}
+    spread, relay, relay_far, got, gathers = ring_gather(seq, rows, partner, ring, ag_s, ag_r)
+    spread()
 
     ffn_onward(2)
+    relay(1)
+    relay(3)
     for copy in saves + locals_[2:3]:
         copy.wait()
     for j in range(4):
         ffn_got(j, 1 if j < 2 else 3).wait_recv()
         ffn_got(j, 2).wait_recv()
+    relay_far()
+    for copy in got.values():
+        copy.wait_recv()
+    for copy in gathers:
+        copy.wait_send()
     for j in range(4):
         ffn_pass(j).wait_send()
         for k in (1, 3):
@@ -650,7 +664,7 @@
         ((rows, NH * HD), bf),
         ((rows, D), f32),
         ((rows, D), f32),
-        ((rows, D), bf),
+        ((rows * lax.axis_size("ctx"), D), bf),
         ((rows, pairs), f32),
         ((rows, HD), f32),
     )
@@ -673,6 +687,7 @@
             dma((4, 4)), dma((4, 4)),
             dma((reach,)), dma((reach,)),
             dma((reach,)), dma((reach,)),
+            dma((10,)), dma((10,)),
         ],
         compiler_params=pltpu.CompilerParams(
             collective_id=2, has_side_effects=True, vmem_limit_bytes=62 * 1024 * 1024
@@ -824,7 +839,7 @@
     grad_heads = stack_heads(grad_attended)
     scores = dot32(queries, keys, NT) * scale + jnp.concatenate([bias_ref[...]] * NH, axis=0)
     expo = jnp.exp(scores - jnp.max(scores, axis=-1, keepdims=True))
-    probs = expo / jnp.sum(expo, axis=-1, keepdims=True)
+    probs = expo * (1.0 / jnp.sum(expo, axis=-1, keepdims=True))
     grad_probs = dot32(grad_heads, vals, NT)
     row_total = jnp.sum(probs * grad_probs, axis=-1, keepdims=True)
     grad_scores = (probs * (grad_probs - row_total)).astype(bf)
@@ -888,11 +903,12 @@
                 return carry
 
             lax.fori_loop(0, 4, add, 0)
-            if k == 2:
-                sum_far(0, t).start()
-                sum_far(1, t).start()
-            elif k:
-                sum_near(k, 0 if k == 3 else 1, t).start()
+
+    def send_cores(t):
+        sum_far(0, t).start()
+        sum_far(1, t).start()
+        sum_near(3, 0, t).start()
+        sum_near(1, 1, t).start()
 
     def fold_far(t):
         acc, far = ((sq, fq), (so, fo))[t]
@@ -903,6 +919,8 @@
             ).astype(bf)
             sum_near(k, h, t).start()
 
+    fold_cores(1)
+    send_cores(1)
     pass_far((1, 3))
 
     total = gpair[pl.ds(reach * rows, rows), :]
@@ -939,6 +957,7 @@
 
     lax.fori_loop(0, width // 256, qkv_tile, 0)
     start_away(0)
+    fold_cores(0)
 
     for copy in own_loads[:4]:
         copy.wait()
@@ -960,8 +979,7 @@
         if k:
             ff_two(k).start()
 
-    fold_cores(1)
-    fold_cores(0)
+    send_cores(0)
     fold_far(1)
     fold_far(0)
 
@@ -1184,37 +1202,57 @@
 
 
 def finish_kernel(*refs):
+    refs, (buf, wide, i_sem, o_sem) = refs[:-4], refs[-4:]
     count = (len(refs) - 7) // 2
-    all_ref, tail_ref, sources = refs[0], refs[1], refs[2 : 2 + count]
+    all_hbm, tail_ref, sources = refs[0], refs[1], refs[2 : 2 + count]
     weights, gains, qk = refs[2 + count : 5 + count], refs[5 + count], refs[6 + count]
+    members = buf.shape[0]
+    share = buf.shape[1] // 3
+    lines = wide.shape[1] // members
+    loads, stores = [], []
+    for i in range(3):
+        third = pl.ds(i * share, share)
+        loads.append(
+            pltpu.make_async_copy(all_hbm.at[:, third, :], buf.at[:, third, :], i_sem.at[i])
+        )
+        loads[i].start()
     for src, dst in zip(sources, refs[7 + count :]):
         dst[...] = src[...]
     owner = lax.axis_index("fsdp")
     width = tail_ref.shape[1]
     for first, dst in ((0, gains), (4, qk)):
-        lines, own = dst.shape
+        count, own = dst.shape
         shift = lax.rem(width - owner * own, width)
-        dst[...] = pltpu.roll(tail_ref[...], shift, 1)[first : first + lines, :own]
-    members = all_ref.shape[0]
-    share = all_ref.shape[1] // 3
-    lines = weights[0].shape[0] // members
+        dst[...] = pltpu.roll(tail_ref[...], shift, 1)[first : first + count, :own]
     for i, dst in enumerate(weights):
+        loads[i].wait()
         for m in range(members):
-            dst[m * lines : (m + 1) * lines, :] = all_ref[
+            wide[i, m * lines : (m + 1) * lines, :] = buf[
                 m, i * share : (i + 1) * share, :
             ].astype(jnp.float32)[:lines]
+        stores.append(pltpu.make_async_copy(wide.at[i], dst, o_sem.at[i]))
+        stores[i].start()
+    for copy in stores:
+        copy.wait()
 
 
 def finish(all_ff, tail, lines, gain_lines, qk_lines, *rest):
     vm = pl.BlockSpec(memory_space=pltpu.VMEM)
+    hbm = pl.BlockSpec(memory_space=pl.ANY)
     f32 = jnp.float32
     results = ((lines, D),) * 3 + (gain_lines, qk_lines)
     return pl.pallas_call(
         finish_kernel,
         out_shape=tuple(jax.ShapeDtypeStruct(s, f32) for s in results)
         + tuple(jax.ShapeDtypeStruct(r.shape, r.dtype) for r in rest),
-        in_specs=[vm] * (2 + len(rest)),
-        out_specs=(vm,) * (5 + len(rest)),
+        in_specs=[hbm] + [vm] * (1 + len(rest)),
+        out_specs=(hbm,) * 3 + (vm,) * (2 + len(rest)),
+        scratch_shapes=[
+            pltpu.VMEM(all_ff.shape, all_ff.dtype),
+            pltpu.VMEM((3, lines, D), f32),
+            pltpu.SemaphoreType.DMA((3,)),
+            pltpu.SemaphoreType.DMA((3,)),
+        ],
         compiler_params=pltpu.CompilerParams(vmem_limit_bytes=62 * 1024 * 1024),
     )(all_ff, tail, *rest)
 
@@ -1270,7 +1308,7 @@
     cot = cotangent.reshape(local_len, D)
     (
         qkv_full, out_full, ffn_full, gains_all, qk_all, normed, projected, queries, pair_all,
-        attended, attn, mid, normed_two, bias, turn_table,
+        attended, attn, mid, normed_seq, bias, turn_table,
     ) = front(
         jnp.concatenate([qkv_weight, gain_rows], axis=0),
         out_weight,
@@ -1281,7 +1319,7 @@
         keep,
     )
     output, grad_normed_two, grad_gain_three, ffn_grads = ffn(
-        normed_two, mid, cot, gains_all, ffn_full
+        normed_seq, mid, cot, gains_all, ffn_full
     )
     grad_tokens, total_qkv, tail, total_out, all_ff = backward_rest(
         ffn_grads,

time: 249 us -> 251 us (level)
  Pallas kernels: 239 us -> 243 us
    pallas_call x1, Pallas kernels: 72.9 us -> 67.3 us  [ffn(): pl.pallas_call(ffn_kernel, out_shape=(jax.ShapeDtypeStruct((rows, D), bf)...]
    pallas_call x1, Pallas kernels: 88.5 us -> 93.2 us  [backward_rest(): pl.pallas_call(back_kernel, out_shape=(jax.ShapeDtypeStruct((rows, D), f3...]
    pallas_call x1, Pallas kernels: 71.7 us -> 75.9 us  [front(): pl.pallas_call(front_kernel, out_shape=tuple((jax.ShapeDtypeStruct(*s) fo...]
where the time goes in v9:
time: 251 us; the launch traced here: 249 us
  Pallas kernels  243 us (97%)
  local copies, waits for them, and re-layouts  2.77 us (1%)
  other arithmetic  2.54 us (1%)
    pallas_call x1, Pallas kernels, backward_rest(): pl.pallas_call(back_kernel, out_shape=(jax.ShapeDtypeStruct((rows, D), f3...  93.2 us
    pallas_call x1, Pallas kernels, front(): pl.pallas_call(front_kernel, out_shape=tuple((jax.ShapeDtypeStruct(*s) fo...  75.9 us
    pallas_call x1, Pallas kernels, ffn(): pl.pallas_call(ffn_kernel, out_shape=(jax.ShapeDtypeStruct((rows, D), bf)...  67.3 us
    pallas_call x1, Pallas kernels, finish(): pl.pallas_call(finish_kernel, out_shape=tuple((jax.ShapeDtypeStruct(s, f3...  6.63 us

profile of v9, /device:TPU:73, one launch (start us, length us, event | category | flops | bytes accessed | tf_op | source)
XLA Modules:
  0.0 249.1 jit_solution(16166248179228691885)
XLA Ops:
  0.6 0.0 copy-start
  0.7 0.8 pad_dynamic-slice_fusion.1
  1.5 0.1 pad.39.clone
  1.6 0.8 pad_dynamic-slice_fusion
  2.3 0.0 copy-done
  2.4 1.7 fusion.11.qkv_ref
  4.1 1.0 constant_dynamic-slice_fusion
  5.2 0.8 fusion.9.ffn_ref
  6.0 75.9 %shard_map.178 = (bf16[1152,1536]{1,0:T(8,128)(2,1)}, bf16[1024,1152]{1,0:T(8,128)(2,1)}, bf16[16,192,1152]{2,1,0:T(8,128)(2,1)}, f32[4,1152]{1,0:T(4,128)}, f32...) custom-call(bf16[80,1536]{1,0:T(8,128)(2,1)} %fusion.11.qkv_ref, ...), custom_call_target="tpu_custom_call" | custom-call | flops 1358954496 | bytes 7864320 | tf_op jit(solution)/shard_map/pallas_call | solution.py:671
  81.9 67.3 %shard_map.179 = (bf16[128,1152]{1,0:T(8,128)(2,1)}, f32[128,1152]{1,0:T(8,128)}, f32[1,1152]{1,0:T(1,128)}, bf16[16,192,1152]{2,1,0:T(8,128)(2,1)}) custom-call(bf16[1024,1152]{1,0:T(8,128)(2,1)} %get-tuple-element.42.seq, f32[128,1152]{1,0:T(8,128)} %get-tuple-element.43.mid_ref, bf16[128,1152]{1,0:T(8,128)(2,1)} %bitcast.6, ...), custom_call_target="tpu_custom_call" | custom-call | flops 21743271936 | bytes 16515072 | tf_op jit(solution)/shard_map/pallas_call | solution.py:285
  149.1 93.2 %shard_map.180 = (f32[128,1152]{1,0:T(8,128)}, f32[72,1536]{1,0:T(8,128)}, f32[8,1536]{1,0:T(8,128)}, f32[64,1152]{1,0:T(8,128)}, bf16[8,192,1152]{2,1,0:T(8,128)(2,1)}) custom-call(bf16[16,192,1152]{2,1,0:T(8,128)(2,1)} %get-tuple-element.46.gff, f32[128,1152]{1,0:T(8,128)} %get-tuple-element.47.gn_ref, f32[128,1152]{1,0:T(8,128)} %get-tuple-element.43.mid_ref, ...), custom_call_target="tpu_custom_call" | custom-call | flops 2717908992 | bytes 14155776 | tf_op jit(solution)/shard_map/pallas_call | solution.py:1157
  242.3 6.6 %shard_map.181 = (f32[432,1152]{1,0:T(8,128)}, f32[432,1152]{1,0:T(8,128)}, f32[432,1152]{1,0:T(8,128)}, f32[4,72]{1,0:T(4,128)}, f32[2,16]{1,0:T(2,128)}, /*ind...) custom-call(bf16[8,192,1152]{2,1,0:T(8,128)(2,1)} %get-tuple-element.60.refs_0_, ...), custom_call_target="tpu_custom_call" | custom-call | tf_op jit(solution)/shard_map/pallas_call | solution.py:1244
  (2 shorter events, 0.0 us)
Async XLA Ops:
  0.6 1.7 copy-start

commit v10 on v9

--- a/solution.py
+++ b/solution.py
@@ -102,20 +102,80 @@
     return spread, relay, relay_far, got, started
 
 
+def plane_gather(src, dst, a, b, block, partner, s1, r1, s2, r2):
+    here = block(a, b)
+
+    def first_peer(k):
+        return {"fsdp": block(lax.rem(a + k, 4), b)}
+
+    def second_peer(k):
+        return {"fsdp": block(a, lax.rem(b + k, 4))}
+
+    def part(j, m):
+        return dst(block(lax.rem(a + j, 4), lax.rem(b + m, 4)))
+
+    def one(k):
+        return remote(src, dst(here), s1.at[k], r1.at[4 - k], first_peer(k))
+
+    def two(j, k):
+        return remote(
+            part(j, 0) if j else src, part(j, 0), s2.at[j, k], r2.at[j, 4 - k], second_peer(k)
+        )
+
+    def far(j):
+        m, k = (3, 1) if j < 2 else (1, 3)
+        return remote(part(j, m), part(j, m), s2.at[j, 2], r2.at[j, 2], second_peer(k))
+
+    def got(j, m):
+        sems = (s1.at[j], r1.at[j]) if m == 0 else (s2.at[j, m], r2.at[j, m])
+        return remote(part(j, m), part(j, m), *sems, partner)
+
+    def start():
+        for k in (1, 3, 2):
+            one(k).start()
+        for k in (1, 3):
+            two(0, k).start()
+
+    def turn_axis():
+        for j in (1, 3, 2):
+            got(j, 0).wait_recv()
+            for k in (1, 3):
+                two(j, k).start()
+
+    def onward(j):
+        got(j, 3 if j < 2 else 1).wait_recv()
+        far(j).start()
+
+    def end():
+        for j in range(4):
+            got(j, 1 if j < 2 else 3).wait_recv()
+            got(j, 2).wait_recv()
+
+    def sent():
+        for j in range(4):
+            far(j).wait_send()
+            for k in (1, 3):
+                two(j, k).wait_send()
+        for k in (1, 2, 3):
+            one(k).wait_send()
+
+    return start, turn_axis, onward, end, sent
+
+
 def ffn_kernel(
-    seq, mid_ref, cot_ref, gain_ref, w_hbm,
+    seq, mid_ref, cot_ref, gain_ref, down_ref, w_hbm,
     out_ref, gn_ref, ggain_ref, gff_hbm,
     wg, wu, wd, gseq, act_a, act_b, hid, dgate, dup, part, keep, base,
     d2d_snd, d2d_in, ici_snd, ici_in, dw,
-    w_sem, o_sem, ag_s, ag_r, rd_s, rd_r, ri_s, ri_r,
+    w_sem, o_sem, l_sem, s1f, r1f, s2f, r2f, ag_s, ag_r, rd_s, rd_r, ri_s, ri_r,
 ):
     rows = mid_ref.shape[0]
     units = wg.shape[0]
     owners = w_hbm.shape[0]
-    share = units // owners
+    share = down_ref.shape[0]
     tile = 256
-    me = lax.axis_index("ctx")
-    chip, core = me // 2, lax.rem(me, 2)
+    y, z, chip, core = place()
+    a, b, block = shape_of(y, z, core)
     partner = {"ctx": chip * 2 + 1 - core}
     chips = {k: {"ctx": lax.rem(chip + k, 4) * 2 + core} for k in (1, 2, 3)}
     order = (0, 1, 3, 2)
@@ -124,16 +184,25 @@
         pltpu.make_async_copy(
             w_hbm.at[f, pl.ds(i * share, share), :], dst.at[pl.ds(f * share, share), :], w_sem.at[i, f]
         )
-        for i, dst in enumerate((wg, wu, wd))
+        for i, dst in enumerate((wg, wu))
         for f in range(owners)
     ]
+    def down_lines(f):
+        return wd.at[pl.ds(pl.multiple_of(f * share, 16), share), :]
+
+    own_down = pltpu.make_async_copy(down_ref, down_lines(block(a, b)), l_sem)
+    own_down.start()
     for load in loads:
         load.start()
-
-    barrier = pltpu.get_barrier_semaphore()
-    for peer in (partner, chips[1], chips[2], chips[3]):
-        pl.semaphore_signal(barrier, inc=1, device_id=peer, device_id_type=MESH)
-    pl.semaphore_wait(barrier, 4)
+    down_start, down_turn, down_onward, down_end, down_sent = plane_gather(
+        down_ref, down_lines, a, b, block, partner, s1f, r1f, s2f, r2f
+    )
+    greet(
+        [partner, chips[1], chips[2], chips[3]]
+        + [{"fsdp": block(lax.rem(a + k, 4), b)} for k in (1, 2, 3)]
+        + [{"fsdp": block(a, lax.rem(b + k, 4))} for k in (1, 2, 3)]
+    )
+    down_start()
 
     started = []
 
@@ -153,12 +222,12 @@
 
     def swap(ph, k):
         d2d_snd[ph, k] = part[pl.ds(rows, rows), :].astype(jnp.bfloat16)
-        keep[order.index(k) % 2] = part[pl.ds(0, rows), :]
+        keep[k // 2] = part[pl.ds(0, rows), :]
         return send(d2d_snd.at[ph, k], d2d_in.at[ph, k], rd_s.at[ph, k], rd_r.at[ph, k], partner)
 
     def sum_out(ph, k, copy):
         copy.wait_recv()
-        total = keep[order.index(k) % 2] + d2d_in[ph, k].astype(jnp.float32)
+        total = keep[k // 2] + d2d_in[ph, k].astype(jnp.float32)
         if k == 0:
             base[...] = total
             return None
@@ -169,21 +238,12 @@
             chips[k],
         )
 
-    def phase(ph, work):
+    def phase(ph, work, ready, order):
         sums = {}
         copy = waiting = None
         for k in order:
-            if ph == 1:
-                if k == 1:
-                    relay(1)
-                    relay(3)
-                if k == 2:
-                    relay_far()
-                    got[2, 0].wait_recv()
-                    got[2, 1].wait_recv()
-                else:
-                    got[k].wait_recv()
-            if waiting is not None and k == 2:
+            ready(k)
+            if waiting is not None and k == order[-1]:
                 sums[waiting] = sum_out(ph, waiting, copy)
                 waiting = None
             work(k)
@@ -192,6 +252,17 @@
             copy, waiting = swap(ph, k), k
         sums[waiting] = sum_out(ph, waiting, copy)
         return sums
+
+    def gathered(k):
+        if k == 1:
+            relay(1)
+            relay(3)
+        if k == 2:
+            relay_far()
+            got[2, 0].wait_recv()
+            got[2, 1].wait_recv()
+        else:
+            got[k].wait_recv()
 
     def collect(ph, sums):
         total = base[...]
@@ -218,14 +289,24 @@
             return carry
 
         lax.fori_loop(0, units // tile, one, 0)
-        if k == 0:
-            for load in loads[2 * owners :]:
-                load.wait()
+
+    def project(k):
         part[...] = dot32(hid[pair(k), :], wd[...], NN)
 
-    for load in loads[: 2 * owners]:
+    for load in loads:
         load.wait()
-    sums = phase(0, forward)
+    forward(0)
+    down_turn()
+    forward(1)
+    down_onward(0)
+    down_onward(1)
+    forward(3)
+    down_onward(3)
+    down_onward(2)
+    forward(2)
+    down_end()
+    own_down.wait()
+    sums = phase(0, project, lambda k: None, (2, 1, 3, 0))
     mlp = collect(0, sums)
     r = lax.rsqrt(jnp.mean(mlp * mlp, axis=-1, keepdims=True) + EPS)
     n = mlp * r
@@ -249,7 +330,7 @@
         lax.fori_loop(0, units // tile, one, 0)
         part[...] = dot32(dgate[pair(k), :], wg[...], NN) + dot32(dup[pair(k), :], wu[...], NN)
 
-    sums = phase(1, backward)
+    sums = phase(1, backward, gathered, order)
     stores = []
     for i, (left, right) in enumerate(((dgate, seq), (dup, seq), (hid, gseq))):
         def one(t, carry, i=i, left=left, right=right):
@@ -269,14 +350,15 @@
     gn_ref[...] = collect(1, sums)
     for copy in started + gathers:
         copy.wait_send()
+    down_sent()
     for store in stores:
         store.wait()
 
 
-def ffn(normed_seq, mid, cot, gain, weights):
+def ffn(normed_seq, mid, cot, gain, down, weights):
     rows = mid.shape[0]
-    owners, lines = weights.shape[:2]
-    units = owners * lines // 3
+    owners, share = weights.shape[0], down.shape[0]
+    units = owners * share
     seq_rows = rows * 8
     bf, f32 = jnp.bfloat16, jnp.float32
     vm = pl.BlockSpec(memory_space=pltpu.VMEM)
@@ -288,9 +370,9 @@
             jax.ShapeDtypeStruct((rows, D), bf),
             jax.ShapeDtypeStruct((rows, D), f32),
             jax.ShapeDtypeStruct((1, D), f32),
-            jax.ShapeDtypeStruct(weights.shape, bf),
+            jax.ShapeDtypeStruct((owners, 3 * share, D), bf),
         ),
-        in_specs=[vm] * 4 + [hbm],
+        in_specs=[vm] * 5 + [hbm],
         out_specs=(vm, vm, vm, hbm),
         scratch_shapes=[
             pltpu.VMEM((units, D), bf),
@@ -309,8 +391,9 @@
             pltpu.VMEM((2, 4, rows, D), bf),
             pltpu.VMEM((2, 3, rows, D), bf),
             pltpu.VMEM((2, 3, rows, D), bf),
-            pltpu.VMEM(weights.shape, bf),
-            dma((3, owners)), dma((3,)),
+            pltpu.VMEM((owners, 3 * share, D), bf),
+            dma((2, owners)), dma((3,)), dma,
+            dma((4,)), dma((4,)), dma((4, 4)), dma((4, 4)),
             dma((10,)), dma((10,)),
             dma((2, 4)), dma((2, 4)),
             dma((2, 4)), dma((2, 4)),
@@ -321,7 +404,7 @@
         cost_estimate=pl.CostEstimate(
             flops=18 * seq_rows * units * D, bytes_accessed=14 * units * D, transcendentals=0
         ),
-    )(normed_seq, mid, cot, gain, weights)
+    )(normed_seq, mid, cot, gain, down, weights)
 
 
 def rms_back(values, grad, gain):
@@ -414,25 +497,9 @@
             seg_ref, seg_in.at[reach - d], ssg.at[d - 1], rsg.at[d - 1], member(d)
         )
 
-    def ffn_one(k):
-        return remote(ffn_ref, ffn_all.at[here], s1f.at[k], r1f.at[4 - k], first_peer(k))
-
-    def ffn_block(j, m):
-        return ffn_all.at[block(lax.rem(a + j, 4), lax.rem(b + m, 4))]
-
-    def ffn_two(j, k):
-        dst = ffn_block(j, 0)
-        src = dst if j else ffn_ref
-        return remote(src, dst, s2f.at[j, k], r2f.at[j, 4 - k], second_peer(k))
-
-    def ffn_pass(j):
-        dst, k = (ffn_block(j, 3), 1) if j < 2 else (ffn_block(j, 1), 3)
-        return remote(dst, dst, s2f.at[j, 2], r2f.at[j, 2], second_peer(k))
-
-    def ffn_got(j, m):
-        dst = ffn_block(j, m)
-        sems = (s1f.at[j], r1f.at[j]) if m == 0 else (s2f.at[j, m], r2f.at[j, m])
-        return remote(dst, dst, *sems, partner)
+    ffn_start, ffn_turn, ffn_onward, ffn_end, ffn_sent = plane_gather(
+        ffn_ref, lambda f: ffn_all.at[f], a, b, block, partner, s1f, r1f, s2f, r2f
+    )
 
     def hop_one(k, t):
         return remote(mine[t], views(here, core)[t], s1.at[k, t], r1.at[4 - k, t], first_peer(k))
@@ -480,10 +547,7 @@
 
     for d in range(1, reach + 1):
         seg_send(d).start()
-    for k in (1, 3, 2):
-        ffn_one(k).start()
-    for k in (1, 3):
-        ffn_two(0, k).start()
+    ffn_start()
 
     for j in (0, 1, 3, 2):
         for m in (3, 1) if j < 2 else (1, 3):
@@ -562,10 +626,7 @@
 
     for d in range(1, reach + 1):
         kv_send(d).start()
-    for j in (1, 3, 2):
-        ffn_got(j, 0).wait_recv()
-        for k in (1, 3):
-            ffn_two(j, k).start()
+    ffn_turn()
     queries = turn(
         stack_heads(proj_ref[:, : NH * HD]),
         extra[4:5, :HD],
@@ -591,10 +652,6 @@
         (spacing >= 0) & (spacing < WINDOW) & begun & (query_seg == key_seg.astype(f32))
     )
     bias_ref[...] = jnp.where(allowed, 0.0, NEG_FILL)
-    def ffn_onward(j):
-        ffn_got(j, 3 if j < 2 else 1).wait_recv()
-        ffn_pass(j).start()
-
     ffn_onward(0)
     for d in range(1, reach + 1):
         kv_send(d).wait_recv()
@@ -622,20 +679,13 @@
     relay(3)
     for copy in saves + locals_[2:3]:
         copy.wait()
-    for j in range(4):
-        ffn_got(j, 1 if j < 2 else 3).wait_recv()
-        ffn_got(j, 2).wait_recv()
+    ffn_end()
     relay_far()
     for copy in got.values():
         copy.wait_recv()
     for copy in gathers:
         copy.wait_send()
-    for j in range(4):
-        ffn_pass(j).wait_send()
-        for k in (1, 3):
-            ffn_two(j, k).wait_send()
-    for k in (1, 2, 3):
-        ffn_one(k).wait_send()
+    ffn_sent()
     for d in range(1, reach + 1):
         seg_send(d).wait_send()
         kv_send(d).wait_send()
@@ -903,12 +953,11 @@
                 return carry
 
             lax.fori_loop(0, 4, add, 0)
-
-    def send_cores(t):
-        sum_far(0, t).start()
-        sum_far(1, t).start()
-        sum_near(3, 0, t).start()
-        sum_near(1, 1, t).start()
+            if k == 2:
+                sum_far(0, t).start()
+                sum_far(1, t).start()
+            elif k:
+                sum_near(k, 0 if k == 3 else 1, t).start()
 
     def fold_far(t):
         acc, far = ((sq, fq), (so, fo))[t]
@@ -919,8 +968,6 @@
             ).astype(bf)
             sum_near(k, h, t).start()
 
-    fold_cores(1)
-    send_cores(1)
     pass_far((1, 3))
 
     total = gpair[pl.ds(reach * rows, rows), :]
@@ -957,7 +1004,6 @@
 
     lax.fori_loop(0, width // 256, qkv_tile, 0)
     start_away(0)
-    fold_cores(0)
 
     for copy in own_loads[:4]:
         copy.wait()
@@ -979,7 +1025,8 @@
         if k:
             ff_two(k).start()
 
-    send_cores(0)
+    fold_cores(1)
+    fold_cores(0)
     fold_far(1)
     fold_far(0)
 
@@ -1202,57 +1249,37 @@
 
 
 def finish_kernel(*refs):
-    refs, (buf, wide, i_sem, o_sem) = refs[:-4], refs[-4:]
     count = (len(refs) - 7) // 2
-    all_hbm, tail_ref, sources = refs[0], refs[1], refs[2 : 2 + count]
+    all_ref, tail_ref, sources = refs[0], refs[1], refs[2 : 2 + count]
     weights, gains, qk = refs[2 + count : 5 + count], refs[5 + count], refs[6 + count]
-    members = buf.shape[0]
-    share = buf.shape[1] // 3
-    lines = wide.shape[1] // members
-    loads, stores = [], []
-    for i in range(3):
-        third = pl.ds(i * share, share)
-        loads.append(
-            pltpu.make_async_copy(all_hbm.at[:, third, :], buf.at[:, third, :], i_sem.at[i])
-        )
-        loads[i].start()
     for src, dst in zip(sources, refs[7 + count :]):
         dst[...] = src[...]
     owner = lax.axis_index("fsdp")
     width = tail_ref.shape[1]
     for first, dst in ((0, gains), (4, qk)):
-        count, own = dst.shape
+        lines, own = dst.shape
         shift = lax.rem(width - owner * own, width)
-        dst[...] = pltpu.roll(tail_ref[...], shift, 1)[first : first + count, :own]
+        dst[...] = pltpu.roll(tail_ref[...], shift, 1)[first : first + lines, :own]
+    members = all_ref.shape[0]
+    share = all_ref.shape[1] // 3
+    lines = weights[0].shape[0] // members
     for i, dst in enumerate(weights):
-        loads[i].wait()
         for m in range(members):
-            wide[i, m * lines : (m + 1) * lines, :] = buf[
+            dst[m * lines : (m + 1) * lines, :] = all_ref[
                 m, i * share : (i + 1) * share, :
             ].astype(jnp.float32)[:lines]
-        stores.append(pltpu.make_async_copy(wide.at[i], dst, o_sem.at[i]))
-        stores[i].start()
-    for copy in stores:
-        copy.wait()
 
 
 def finish(all_ff, tail, lines, gain_lines, qk_lines, *rest):
     vm = pl.BlockSpec(memory_space=pltpu.VMEM)
-    hbm = pl.BlockSpec(memory_space=pl.ANY)
     f32 = jnp.float32
     results = ((lines, D),) * 3 + (gain_lines, qk_lines)
     return pl.pallas_call(
         finish_kernel,
         out_shape=tuple(jax.ShapeDtypeStruct(s, f32) for s in results)
         + tuple(jax.ShapeDtypeStruct(r.shape, r.dtype) for r in rest),
-        in_specs=[hbm] + [vm] * (1 + len(rest)),
-        out_specs=(hbm,) * 3 + (vm,) * (2 + len(rest)),
-        scratch_shapes=[
-            pltpu.VMEM(all_ff.shape, all_ff.dtype),
-            pltpu.VMEM((3, lines, D), f32),
-            pltpu.SemaphoreType.DMA((3,)),
-            pltpu.SemaphoreType.DMA((3,)),
-        ],
+        in_specs=[vm] * (2 + len(rest)),
+        out_specs=(vm,) * (5 + len(rest)),
         compiler_params=pltpu.CompilerParams(vmem_limit_bytes=62 * 1024 * 1024),
     )(all_ff, tail, *rest)
 
@@ -1294,7 +1321,7 @@
         return jnp.pad(part, ((0, padded - slice_rows), (0, 0)))
 
     ffn_shard = jnp.concatenate(
-        [my_slice(gate_weight), my_slice(up_weight), my_slice(down_weight)], axis=0
+        [my_slice(gate_weight), my_slice(up_weight)], axis=0
     )
     places = np.arange(ctx_size * local_len, dtype=np.float32)
     rates = (ROPE_BASE ** (-(2.0 * np.arange(HD // 2)) / HD)).astype(np.float32)
@@ -1319,7 +1346,7 @@
         keep,
     )
     output, grad_normed_two, grad_gain_three, ffn_grads = ffn(
-        normed_seq, mid, cot, gains_all, ffn_full
+        normed_seq, mid, cot, gains_all, my_slice(down_weight), ffn_full
     )
     grad_tokens, total_qkv, tail, total_out, all_ff = backward_rest(
         ffn_grads,

time: 251 us -> 254 us (1.012)
  Pallas kernels: 243 us -> 247 us
    pallas_call x1, Pallas kernels: 67.3 us -> 77.9 us  [ffn(): pl.pallas_call(ffn_kernel, out_shape=(jax.ShapeDtypeStruct((rows, D), bf)...]
    pallas_call x1, Pallas kernels: 75.9 us -> 71.5 us  [front(): pl.pallas_call(front_kernel, out_shape=tuple((jax.ShapeDtypeStruct(*s) fo...]
where the time goes in v10:
time: 254 us
  Pallas kernels  247 us (97%)
  local copies, waits for them, and re-layouts  3.45 us (1%)
    pallas_call x1, Pallas kernels, backward_rest(): pl.pallas_call(back_kernel, out_shape=(jax.ShapeDtypeStruct((rows, D), f3...  92 us
    pallas_call x1, Pallas kernels, ffn(): pl.pallas_call(ffn_kernel, out_shape=(jax.ShapeDtypeStruct((rows, D), bf)...  77.9 us
    pallas_call x1, Pallas kernels, front(): pl.pallas_call(front_kernel, out_shape=tuple((jax.ShapeDtypeStruct(*s) fo...  71.5 us
    pallas_call x1, Pallas kernels, finish(): pl.pallas_call(finish_kernel, out_shape=tuple((jax.ShapeDtypeStruct(s, f3...  5.78 us

profile of v10, /device:TPU:73, one launch (start us, length us, event | category | flops | bytes accessed | tf_op | source)
XLA Modules:
  0.0 253.9 jit_solution(1301948038758968948)
XLA Ops:
  0.6 0.0 copy-start
  0.7 0.8 pad_dynamic-slice_fusion.1
  1.5 0.1 pad.38.clone
  1.6 0.8 pad_dynamic-slice_fusion
  2.3 0.0 copy-done
  2.4 1.7 fusion.8.qkv_ref
  4.1 1.0 constant_dynamic-slice_fusion
  5.2 0.7 pad.32.down_ref
  5.9 0.7 fusion.6.ffn_ref
  6.6 71.5 %shard_map.178 = (bf16[1152,1536]{1,0:T(8,128)(2,1)}, bf16[1024,1152]{1,0:T(8,128)(2,1)}, bf16[16,128,1152]{2,1,0:T(8,128)(2,1)}, f32[4,1152]{1,0:T(4,128)}, f32...) custom-call(bf16[80,1536]{1,0:T(8,128)(2,1)} %fusion.8.qkv_ref, ...), custom_call_target="tpu_custom_call" | custom-call | flops 1358954496 | bytes 7864320 | tf_op jit(solution)/shard_map/pallas_call | solution.py:721
  78.1 77.9 %shard_map.179 = (bf16[128,1152]{1,0:T(8,128)(2,1)}, f32[128,1152]{1,0:T(8,128)}, f32[1,1152]{1,0:T(1,128)}, bf16[16,192,1152]{2,1,0:T(8,128)(2,1)}) custom-call(bf16[1024,1152]{1,0:T(8,128)(2,1)} %get-tuple-element.42.seq, f32[128,1152]{1,0:T(8,128)} %get-tuple-element.43.mid_ref, bf16[128,1152]{1,0:T(8,128)(2,1)} %bitcast.6, ...), custom_call_target="tpu_custom_call" | custom-call | flops 21743271936 | bytes 16515072 | tf_op jit(solution)/shard_map/pallas_call | solution.py:367
  156.1 92.0 %shard_map.180 = (f32[128,1152]{1,0:T(8,128)}, f32[72,1536]{1,0:T(8,128)}, f32[8,1536]{1,0:T(8,128)}, f32[64,1152]{1,0:T(8,128)}, bf16[8,192,1152]{2,1,0:T(8,128)(2,1)}) custom-call(bf16[16,192,1152]{2,1,0:T(8,128)(2,1)} %get-tuple-element.46.gff, f32[128,1152]{1,0:T(8,128)} %get-tuple-element.47.gn_ref, f32[128,1152]{1,0:T(8,128)} %get-tuple-element.43.mid_ref, ...), custom_call_target="tpu_custom_call" | custom-call | flops 2717908992 | bytes 14155776 | tf_op jit(solution)/shard_map/pallas_call | solution.py:1204
  248.1 5.8 %shard_map.181 = (f32[432,1152]{1,0:T(8,128)}, f32[432,1152]{1,0:T(8,128)}, f32[432,1152]{1,0:T(8,128)}, f32[4,72]{1,0:T(4,128)}, f32[2,16]{1,0:T(2,128)}, /*ind...) custom-call(bf16[8,192,1152]{2,1,0:T(8,128)(2,1)} %get-tuple-element.60.refs_0_, ...), custom_call_target="tpu_custom_call" | custom-call | tf_op jit(solution)/shard_map/pallas_call | solution.py:1277
  (2 shorter events, 0.0 us)
Async XLA Ops:
  0.6 1.7 copy-start

commit v11 on v8

--- a/solution.py
+++ b/solution.py
@@ -1,3 +1,5 @@
+import functools
+
 import jax
 import numpy as np
 import jax.numpy as jnp
@@ -313,10 +315,12 @@
     )
 
 
-def greet(peers):
+def greet(peers, meanwhile=None):
     barrier = pltpu.get_barrier_semaphore()
     for peer in peers:
         pl.semaphore_signal(barrier, inc=1, device_id=peer, device_id_type=MESH)
+    if meanwhile is not None:
+        meanwhile()
     pl.semaphore_wait(barrier, len(peers))
 
 
@@ -342,10 +346,10 @@
 
 
 def front_kernel(
-    qkv_ref, wo_ref, ffn_ref, tok_ref, seg_line, table_ref,
+    qkv_own, gain_own, qk_own, wo_ref, ffn_ref, tok_ref, seg_line, table_ref,
     qkv_hbm, wo_hbm, ffn_all, gains_ref, qk_ref, normed_ref, proj_ref, q_ref, pair_ref, att_ref,
     attn_ref, mid_ref, low_ref, bias_ref, turn_ref,
-    qkv_all, qkv_out, wo_all, seg_ref, seg_in,
+    qkv_ref, placing, qkv_all, qkv_out, wo_all, seg_ref, seg_in,
     l_sem, s1, r1, s2, r2, sd, rd, s1f, r1f, s2f, r2f, skv, rkv, ssg, rsg,
 ):
     f32, bf = jnp.float32, jnp.bfloat16
@@ -380,6 +384,18 @@
         wo_ref.at[pl.ds(pl.multiple_of(core * o_half, 16), o_half), :],
     )
     here = block(a, b)
+    def stage_shard():
+        owner = lax.axis_index("fsdp")
+        placing[...] = jnp.zeros_like(placing)
+        lines, own = gain_own.shape
+        placing[:lines, :own] = gain_own[...].astype(f32)
+        placed = pltpu.roll(placing[...], owner * own, 1)
+        placing[...] = jnp.zeros_like(placing)
+        more, own = qk_own.shape
+        placing[lines : lines + more, :own] = qk_own[...].astype(f32)
+        placed = placed + pltpu.roll(placing[...], owner * own, 1)
+        qkv_ref[...] = jnp.concatenate([qkv_own[...].astype(f32), placed], axis=0).astype(bf)
+
     locals_ = [
         pltpu.make_async_copy(
             qkv_ref, qkv_all.at[pl.ds(pl.multiple_of(here * q_rows, 16), q_rows), :], l_sem.at[0]
@@ -390,7 +406,7 @@
         pltpu.make_async_copy(ffn_ref, ffn_all.at[here], l_sem.at[2]),
         pltpu.make_async_copy(table_ref.at[me], turn_ref, l_sem.at[3]),
     ]
-    for copy in locals_:
+    for copy in locals_[1:]:
         copy.start()
 
     def first_peer(k):
@@ -402,8 +418,10 @@
     greet(
         [first_peer(k) for k in (1, 2, 3)]
         + [second_peer(k) for k in (1, 2, 3)]
-        + [member(k) for k in range(1, members)]
-    )
+        + [member(k) for k in range(1, members)],
+        stage_shard,
+    )
+    locals_[0].start()
 
     def seg_send(d):
         return remote(
@@ -598,7 +616,7 @@
         [bias_ref[...]] * NH, axis=0
     )
     expo = jnp.exp(scores - jnp.max(scores, axis=-1, keepdims=True))
-    probs = expo / jnp.sum(expo, axis=-1, keepdims=True)
+    probs = expo * (1.0 / jnp.sum(expo, axis=-1, keepdims=True))
     heads = dot32(probs.astype(bf), pair_ref[:, HD:], NN).astype(bf)
     for h in range(NH):
         att_ref[:, h * HD : (h + 1) * HD] = heads[h * rows : (h + 1) * rows]
@@ -627,12 +645,13 @@
         kv_send(d).wait_send()
 
 
-def front(qkv_shard, wo_shard, ffn_shard, tokens, seg_line, table, keep):
+def front(qkv_own, gain_own, qk_own, wo_shard, ffn_shard, tokens, seg_line, table):
     f32, bf = jnp.float32, jnp.bfloat16
     vm = pl.BlockSpec(memory_space=pltpu.VMEM)
     hbm = pl.BlockSpec(memory_space=pl.ANY)
     dma = pltpu.SemaphoreType.DMA
-    q_rows, width = qkv_shard.shape
+    keep, width = qkv_own.shape
+    q_rows = keep + 8
     o_rows, o_width = wo_shard.shape
     rows = tokens.shape[0]
     reach = min(-(-(WINDOW - 1) // rows), lax.axis_size("ctx") - 1)
@@ -657,9 +676,11 @@
     return pl.pallas_call(
         front_kernel,
         out_shape=tuple(jax.ShapeDtypeStruct(*s) for s in shapes),
-        in_specs=[vm, vm, hbm, vm, vm, hbm],
+        in_specs=[vm, vm, vm, vm, hbm, vm, vm, hbm],
         out_specs=(hbm,) * 3 + (vm,) * (len(shapes) - 3),
         scratch_shapes=[
+            pltpu.VMEM((q_rows, width), bf),
+            pltpu.VMEM((8, width), f32),
             pltpu.VMEM((16 * q_rows, width), bf),
             pltpu.VMEM((16 * keep, width), bf),
             pltpu.VMEM((16 * o_rows, o_width), bf),
@@ -680,11 +701,23 @@
         cost_estimate=pl.CostEstimate(
             flops=6 * rows * width * D, bytes_accessed=64 * q_rows * width, transcendentals=0
         ),
-    )(qkv_shard, wo_shard, ffn_shard, tokens, seg_line, table)
+    )(qkv_own, gain_own, qk_own, wo_shard, ffn_shard, tokens, seg_line, table)
+
+
+def back_entry(count, gff, *refs):
+    sources, refs = refs[:count], refs[count:]
+    hbm_and_out, refs = refs[:7], refs[7:]
+    held, v_sem, rest = refs[:count], refs[count], refs[count + 1 :]
+    loads = [
+        pltpu.make_async_copy(src, dst, v_sem.at[i]) for i, (src, dst) in enumerate(zip(sources, held))
+    ]
+    for load in loads:
+        load.start()
+    back_kernel(loads, gff, *held, *hbm_and_out, *rest)
 
 
 def back_kernel(
-    gff, gn_ref, mid_ref, attn_ref, cot_ref, tok_ref, gains_ref, qk_ref, proj_ref, q_ref,
+    loads, gff, gn_ref, mid_ref, attn_ref, cot_ref, tok_ref, gains_ref, qk_ref, proj_ref, q_ref,
     pair_ref, att_ref, normed_ref, turn_ref, bias_ref, g3_ref, qkv_hbm, wo_hbm,
     gt_ref, oq_out, tail_out, oo_ref, all_ff,
     qkv_ref, wo_ref, oq_ref, own_ff, far_own, far_in, in1_ff, t_ff, in2_ff, kv_snd, kv_in, gmid, gpair, gproj, tail,
@@ -773,7 +806,7 @@
             far_own[j] = (far_own[j].astype(f32) + far_in[j].astype(f32)).astype(bf)
             ff_near(1 if j < 2 else 3, j).start()
 
-    for copy in weight_loads[:1]:
+    for copy in loads + weight_loads[:1]:
         copy.wait()
 
     grad_final = cot_ref[...].astype(f32)
@@ -824,7 +857,7 @@
     grad_heads = stack_heads(grad_attended)
     scores = dot32(queries, keys, NT) * scale + jnp.concatenate([bias_ref[...]] * NH, axis=0)
     expo = jnp.exp(scores - jnp.max(scores, axis=-1, keepdims=True))
-    probs = expo / jnp.sum(expo, axis=-1, keepdims=True)
+    probs = expo * (1.0 / jnp.sum(expo, axis=-1, keepdims=True))
     grad_probs = dot32(grad_heads, vals, NT)
     row_total = jnp.sum(probs * grad_probs, axis=-1, keepdims=True)
     grad_scores = (probs * (grad_probs - row_total)).astype(bf)
@@ -1137,7 +1170,7 @@
         return pltpu.VMEM(lead + (ff_rows, D), bf)
 
     return pl.pallas_call(
-        back_kernel,
+        functools.partial(back_entry, len(values)),
         out_shape=(
             jax.ShapeDtypeStruct((rows, D), f32),
             jax.ShapeDtypeStruct((keep, width), f32),
@@ -1145,9 +1178,11 @@
             jax.ShapeDtypeStruct((o_rows, o_width), f32),
             jax.ShapeDtypeStruct((2 * chips, ff_rows, D), bf),
         ),
-        in_specs=[hbm] + [vm] * len(values) + [hbm] * 2,
+        in_specs=[hbm] * (3 + len(values)),
         out_specs=(vm,) * 5,
         scratch_shapes=[
+            *(pltpu.VMEM(v.shape, v.dtype) for v in values),
+            dma((len(values),)),
             pltpu.VMEM((16 * keep, width), bf),
             pltpu.VMEM((16 * o_rows, o_width), bf),
             pltpu.VMEM((q_rows, width), f32),
@@ -1233,24 +1268,12 @@
 ):
     local_len = tokens.shape[1]
     ctx_index = lax.axis_index("ctx")
-    owner = lax.axis_index("fsdp")
     ctx_size = lax.axis_size("ctx")
     own_rows = gate_weight.shape[0]
     slice_rows = own_rows // ctx_size
     padded = -(-slice_rows // 16) * 16
-    keep, width = qkv_weight.shape
+    keep = qkv_weight.shape[0]
     gain_lines, qk_lines = norm_gains.shape, qk_gains.shape
-    def placed(lines):
-        count, own = lines.shape
-        room = (lax.axis_size("fsdp") - 1) * own
-        padded_lines = jnp.pad(lines, ((0, 0), (room, room)))
-        spread = lax.dynamic_slice(padded_lines, (0, room - owner * own), (count, room + own))
-        return jnp.pad(spread, ((0, 0), (0, width - room - own)))
-
-    gain_rows = jnp.concatenate(
-        [placed(norm_gains), placed(qk_gains), jnp.zeros((2, width), jnp.bfloat16)], axis=0
-    )
-
     def my_slice(weight):
         part = lax.dynamic_slice(weight, (ctx_index * slice_rows, 0), (slice_rows, D))
         return jnp.pad(part, ((0, padded - slice_rows), (0, 0)))
@@ -1272,13 +1295,14 @@
         qkv_full, out_full, ffn_full, gains_all, qk_all, normed, projected, queries, pair_all,
         attended, attn, mid, normed_two, bias, turn_table,
     ) = front(
-        jnp.concatenate([qkv_weight, gain_rows], axis=0),
+        qkv_weight,
+        norm_gains,
+        qk_gains,
         out_weight,
         ffn_shard,
         flat,
         segments,
         table,
-        keep,
     )
     output, grad_normed_two, grad_gain_three, ffn_grads = ffn(
         normed_two, mid, cot, gains_all, ffn_full

time: 249 us -> 246 us (0.988)
  no operation moved by 1% of the time
where the time goes in v11:
time: 246 us; the launch traced here: 242 us
  Pallas kernels  238 us (97%)
    pallas_call x1, Pallas kernels, backward_rest(): pl.pallas_call(functools.partial(back_entry, len(values)), out_shape=(jax...  87.3 us
    pallas_call x1, Pallas kernels, ffn(): pl.pallas_call(ffn_kernel, out_shape=(jax.ShapeDtypeStruct((rows, D), bf)...  72.9 us
    pallas_call x1, Pallas kernels, front(): pl.pallas_call(front_kernel, out_shape=tuple((jax.ShapeDtypeStruct(*s) fo...  71.7 us
    pallas_call x1, Pallas kernels, finish(): pl.pallas_call(finish_kernel, out_shape=tuple((jax.ShapeDtypeStruct(s, f3...  5.78 us

profile of v11, /device:TPU:73, one launch (start us, length us, event | category | flops | bytes accessed | tf_op | source)
XLA Modules:
  0.0 241.5 jit_solution(14491379572951119578)
XLA Ops:
  0.6 0.0 copy-start
  0.7 1.2 copy-done
  1.9 1.1 constant_dynamic-slice_fusion
  3.0 0.8 fusion.5.ffn_ref
  3.8 71.7 %shard_map.178 = (bf16[1152,1536]{1,0:T(8,128)(2,1)}, bf16[1024,1152]{1,0:T(8,128)(2,1)}, bf16[16,192,1152]{2,1,0:T(8,128)(2,1)}, f32[4,1152]{1,0:T(4,128)}, f32...) custom-call(bf16[72,1536]{1,0:T(8,128)(2,1)} %qkv_own.1, ...), custom_call_target="tpu_custom_call" | custom-call | flops 1358954496 | bytes 7864320 | tf_op jit(solution)/shard_map/pallas_call | solution.py:676
  75.5 72.9 %shard_map.179 = (bf16[128,1152]{1,0:T(8,128)(2,1)}, f32[128,1152]{1,0:T(8,128)}, f32[1,1152]{1,0:T(1,128)}, bf16[16,192,1152]{2,1,0:T(8,128)(2,1)}) custom-call(bf16[128,1152]{1,0:T(8,128)(2,1)} %get-tuple-element.42.normed_ref, f32[128,1152]{1,0:T(8,128)} %get-tuple-element.43.mid_ref.refs_1_, bf16[128,1152]{1,0:T(8,128)(2,1)} %bitcast.6, ...), custom_call_target="tpu_custom_call" | custom-call | flops 21743271936 | bytes 16515072 | tf_op jit(solution)/shard_map/pallas_call | solution.py:250
  148.4 87.3 %shard_map.180 = (f32[128,1152]{1,0:T(8,128)}, f32[72,1536]{1,0:T(8,128)}, f32[8,1536]{1,0:T(8,128)}, f32[64,1152]{1,0:T(8,128)}, bf16[8,192,1152]{2,1,0:T(8,128)(2,1)}) custom-call(bf16[16,192,1152]{2,1,0:T(8,128)(2,1)} %get-tuple-element.46.gff, f32[128,1152]{1,0:T(8,128)} %get-tuple-element.47.refs_0_, f32[128,1152]{1,0:T(8,128)} %get-tuple-element.43.mid_ref.refs_1_, ...), custom_call_target="tpu_custom_call" | custom-call | flops 2717908992 | bytes 14155776 | tf_op jit(solution)/shard_map/pallas_call | solution.py:1172
  235.7 5.8 %shard_map.181 = (f32[432,1152]{1,0:T(8,128)}, f32[432,1152]{1,0:T(8,128)}, f32[432,1152]{1,0:T(8,128)}, f32[4,72]{1,0:T(4,128)}, f32[2,16]{1,0:T(2,128)}, /*ind...) custom-call(bf16[8,192,1152]{2,1,0:T(8,128)(2,1)} %get-tuple-element.60.refs_0_, ...), custom_call_target="tpu_custom_call" | custom-call | tf_op jit(solution)/shard_map/pallas_call | solution.py:1247
  (1 shorter events, 0.0 us)
Async XLA Ops:
  0.6 1.2 copy-start

commit v12 on v11

--- a/solution.py
+++ b/solution.py
@@ -346,10 +346,10 @@
 
 
 def front_kernel(
-    qkv_own, gain_own, qk_own, wo_ref, ffn_ref, tok_ref, seg_line, table_ref,
+    qkv_own, gain_own, qk_own, wo_ref, gate_hbm, up_hbm, down_hbm, tok_ref, seg_line, table_ref,
     qkv_hbm, wo_hbm, ffn_all, gains_ref, qk_ref, normed_ref, proj_ref, q_ref, pair_ref, att_ref,
     attn_ref, mid_ref, low_ref, bias_ref, turn_ref,
-    qkv_ref, placing, qkv_all, qkv_out, wo_all, seg_ref, seg_in,
+    ffn_ref, window, win_sem, qkv_ref, placing, qkv_all, qkv_out, wo_all, seg_ref, seg_in,
     l_sem, s1, r1, s2, r2, sd, rd, s1f, r1f, s2f, r2f, skv, rkv, ssg, rsg,
 ):
     f32, bf = jnp.float32, jnp.bfloat16
@@ -384,6 +384,26 @@
         wo_ref.at[pl.ds(pl.multiple_of(core * o_half, 16), o_half), :],
     )
     here = block(a, b)
+    lines, tall = gate_hbm.shape[0] // members, window.shape[1]
+    begin = lines * me // 16 * 16 - me // (members - 1) * 16
+    skip = lines * me - begin
+    windows = [
+        pltpu.make_async_copy(
+            src.at[pl.ds(pl.multiple_of(begin, 16), tall), :], window.at[i], win_sem.at[i]
+        )
+        for i, src in enumerate((gate_hbm, up_hbm, down_hbm))
+    ]
+    for copy in windows:
+        copy.start()
+
+    def stage_ffn():
+        share = ffn_ref.shape[0] // 3
+        inside = lax.broadcasted_iota(jnp.int32, (share, 1), 0) < lines
+        for i, copy in enumerate(windows):
+            copy.wait()
+            moved = pltpu.roll(window[i].astype(f32), lax.rem(tall - skip, tall), 0)[:share]
+            ffn_ref[i * share : (i + 1) * share, :] = jnp.where(inside, moved, 0.0).astype(bf)
+
     def stage_shard():
         owner = lax.axis_index("fsdp")
         placing[...] = jnp.zeros_like(placing)
@@ -406,7 +426,7 @@
         pltpu.make_async_copy(ffn_ref, ffn_all.at[here], l_sem.at[2]),
         pltpu.make_async_copy(table_ref.at[me], turn_ref, l_sem.at[3]),
     ]
-    for copy in locals_[1:]:
+    for copy in (locals_[1], locals_[3]):
         copy.start()
 
     def first_peer(k):
@@ -485,6 +505,8 @@
     for k in (1, 3):
         for t in both:
             hop_two(0, k, t).start()
+    stage_ffn()
+    locals_[2].start()
     for j in (1, 3, 2):
         for t in both:
             arrive_one(j, t).wait_recv()
@@ -645,7 +667,7 @@
         kv_send(d).wait_send()
 
 
-def front(qkv_own, gain_own, qk_own, wo_shard, ffn_shard, tokens, seg_line, table):
+def front(qkv_own, gain_own, qk_own, wo_shard, ffn_own, padded, tokens, seg_line, table):
     f32, bf = jnp.float32, jnp.bfloat16
     vm = pl.BlockSpec(memory_space=pltpu.VMEM)
     hbm = pl.BlockSpec(memory_space=pl.ANY)
@@ -659,7 +681,7 @@
     shapes = (
         ((16 * keep, width), bf),
         ((16 * o_rows, o_width), bf),
-        ((16, *ffn_shard.shape), bf),
+        ((16, 3 * padded, D), bf),
         ((4, D), f32),
         ((2, HD), f32),
         ((rows, D), bf),
@@ -676,9 +698,12 @@
     return pl.pallas_call(
         front_kernel,
         out_shape=tuple(jax.ShapeDtypeStruct(*s) for s in shapes),
-        in_specs=[vm, vm, vm, vm, hbm, vm, vm, hbm],
+        in_specs=[vm, vm, vm, vm, hbm, hbm, hbm, vm, vm, hbm],
         out_specs=(hbm,) * 3 + (vm,) * (len(shapes) - 3),
         scratch_shapes=[
+            pltpu.VMEM((3 * padded, D), bf),
+            pltpu.VMEM((3, padded + 16, D), bf),
+            dma((3,)),
             pltpu.VMEM((q_rows, width), bf),
             pltpu.VMEM((8, width), f32),
             pltpu.VMEM((16 * q_rows, width), bf),
@@ -701,7 +726,7 @@
         cost_estimate=pl.CostEstimate(
             flops=6 * rows * width * D, bytes_accessed=64 * q_rows * width, transcendentals=0
         ),
-    )(qkv_own, gain_own, qk_own, wo_shard, ffn_shard, tokens, seg_line, table)
+    )(qkv_own, gain_own, qk_own, wo_shard, *ffn_own, tokens, seg_line, table)
 
 
 def back_entry(count, gff, *refs):
@@ -1267,20 +1292,12 @@
     cotangent,
 ):
     local_len = tokens.shape[1]
-    ctx_index = lax.axis_index("ctx")
     ctx_size = lax.axis_size("ctx")
     own_rows = gate_weight.shape[0]
     slice_rows = own_rows // ctx_size
     padded = -(-slice_rows // 16) * 16
     keep = qkv_weight.shape[0]
     gain_lines, qk_lines = norm_gains.shape, qk_gains.shape
-    def my_slice(weight):
-        part = lax.dynamic_slice(weight, (ctx_index * slice_rows, 0), (slice_rows, D))
-        return jnp.pad(part, ((0, padded - slice_rows), (0, 0)))
-
-    ffn_shard = jnp.concatenate(
-        [my_slice(gate_weight), my_slice(up_weight), my_slice(down_weight)], axis=0
-    )
     places = np.arange(ctx_size * local_len, dtype=np.float32)
     rates = (ROPE_BASE ** (-(2.0 * np.arange(HD // 2)) / HD)).astype(np.float32)
     angles = (places[:, None] * rates).astype(np.float64)
@@ -1299,7 +1316,8 @@
         norm_gains,
         qk_gains,
         out_weight,
-        ffn_shard,
+        (gate_weight, up_weight, down_weight),
+        padded,
         flat,
         segments,
         table,

time: 246 us -> 242 us (0.984)
  no operation moved by 1% of the time
where the time goes in v12:
time: 242 us; the launch traced here: 238 us
  Pallas kernels  238 us (98%)
    pallas_call x1, Pallas kernels, backward_rest(): pl.pallas_call(functools.partial(back_entry, len(values)), out_shape=(jax...  87.1 us
    pallas_call x1, Pallas kernels, ffn(): pl.pallas_call(ffn_kernel, out_shape=(jax.ShapeDtypeStruct((rows, D), bf)...  72.8 us
    pallas_call x1, Pallas kernels, front(): pl.pallas_call(front_kernel, out_shape=tuple((jax.ShapeDtypeStruct(*s) fo...  71.9 us
    pallas_call x1, Pallas kernels, finish(): pl.pallas_call(finish_kernel, out_shape=tuple((jax.ShapeDtypeStruct(s, f3...  5.78 us

profile of v12, /device:TPU:73, one launch (start us, length us, event | category | flops | bytes accessed | tf_op | source)
XLA Modules:
  0.0 238.2 jit_solution(10527479029508132469)
XLA Ops:
  0.6 71.9 %shard_map.178 = (bf16[1152,1536]{1,0:T(8,128)(2,1)}, bf16[1024,1152]{1,0:T(8,128)(2,1)}, bf16[16,192,1152]{2,1,0:T(8,128)(2,1)}, f32[4,1152]{1,0:T(4,128)}, f32...) custom-call(bf16[72,1536]{1,0:T(8,128)(2,1)} %qkv_own.1, ...), custom_call_target="tpu_custom_call" | custom-call | flops 1358954496 | bytes 7864320 | tf_op jit(solution)/shard_map/pallas_call | solution.py:698
  72.5 72.8 %shard_map.179 = (bf16[128,1152]{1,0:T(8,128)(2,1)}, f32[128,1152]{1,0:T(8,128)}, f32[1,1152]{1,0:T(1,128)}, bf16[16,192,1152]{2,1,0:T(8,128)(2,1)}) custom-call(bf16[128,1152]{1,0:T(8,128)(2,1)} %get-tuple-element.42.normed_ref, f32[128,1152]{1,0:T(8,128)} %get-tuple-element.43.mid_ref.refs_1_, bf16[128,1152]{1,0:T(8,128)(2,1)} %bitcast.6, ...), custom_call_target="tpu_custom_call" | custom-call | flops 21743271936 | bytes 16515072 | tf_op jit(solution)/shard_map/pallas_call | solution.py:250
  145.3 87.1 %shard_map.180 = (f32[128,1152]{1,0:T(8,128)}, f32[72,1536]{1,0:T(8,128)}, f32[8,1536]{1,0:T(8,128)}, f32[64,1152]{1,0:T(8,128)}, bf16[8,192,1152]{2,1,0:T(8,128)(2,1)}) custom-call(bf16[16,192,1152]{2,1,0:T(8,128)(2,1)} %get-tuple-element.46.gff, f32[128,1152]{1,0:T(8,128)} %get-tuple-element.47.refs_0_, f32[128,1152]{1,0:T(8,128)} %get-tuple-element.43.mid_ref.refs_1_, ...), custom_call_target="tpu_custom_call" | custom-call | flops 2717908992 | bytes 14155776 | tf_op jit(solution)/shard_map/pallas_call | solution.py:1197
  232.4 5.8 %shard_map.181 = (f32[432,1152]{1,0:T(8,128)}, f32[432,1152]{1,0:T(8,128)}, f32[432,1152]{1,0:T(8,128)}, f32[4,72]{1,0:T(4,128)}, f32[2,16]{1,0:T(2,128)}, /*ind...) custom-call(bf16[8,192,1152]{2,1,0:T(8,128)(2,1)} %get-tuple-element.60.refs_0_, ...), custom_call_target="tpu_custom_call" | custom-call | tf_op jit(solution)/shard_map/pallas_call | solution.py:1272
